TPU v7x, 512 devices: a whole 4x4x16 slice. The times are simulated.
512 devices in a mesh: gx: 128 (over z, x, y_hi), gy: 4 (over y_lo, core).
Axes of the slice: x: 4, y: 4 (y_hi: 2, y_lo: 2; y = y_hi * 2 + y_lo), z: 16, core: 2. Of those that a mesh axis runs over, the one named last changes fastest.
Arguments:
- populations: float32 [19, 256, 64, 256], P(None, 'gx', 'gy'), may hold values from 0.01 to 0.15
- target_density: float32 [256, 64, 256], P('gx', 'gy'), may hold values from 1.1 to 1.9
- weight_in: float32 [19, 32], replicated, may hold values from -1.25 to 1.25
- bias_in: float32 [32], replicated, may hold values from -3 to 3
- weight_out: float32 [32, 19], replicated, may hold values from -1 to 1
- bias_out: float32 [19], replicated, may hold values from -4 to 4
Outputs:
- moments: float32 [4, 256, 64, 256], P(None, 'gx', 'gy')
- grad_weight_in: float32 [19, 32], replicated
- grad_bias_in: float32 [32], replicated
- grad_weight_out: float32 [32, 19], replicated
- grad_bias_out: float32 [19], replicated
All inputs are finite; a program needn't handle non-finite values.
Results may differ from a plain program's by a relative error of at most 0.0003.
Values sent between devices are 32-bit elements; how exact they have to be, the bound alone decides.
No kernel may reach another device: no remote copies, remote signals or barrier semaphores. Data moves between devices by JAX's collectives and lax.ppermute only.
A program may use at most 64 MiB of HBM per device.

v0:
```python
import math

import jax
import jax.numpy as jnp
from jax import lax
from jax.sharding import PartitionSpec as P

velocity_table = (
    (0, 0, 0),
    (1, 0, 0),
    (-1, 0, 0),
    (0, 1, 0),
    (0, -1, 0),
    (0, 0, 1),
    (0, 0, -1),
    (1, 1, 0),
    (-1, -1, 0),
    (1, -1, 0),
    (-1, 1, 0),
    (1, 0, 1),
    (-1, 0, -1),
    (1, 0, -1),
    (-1, 0, 1),
    (0, 1, 1),
    (0, -1, -1),
    (0, 1, -1),
    (0, -1, 1),
)
lattice_weights = (1.0 / 3.0,) + (1.0 / 18.0,) * 6 + (1.0 / 36.0,) * 12
input_scale = 8.0
output_scale = 0.05
relax_time = 0.8


def padded_2(x, sides, width):
    for axis, dim in sides:
        peers, length = (lax.axis_size(axis), x.shape[dim])
        up = [(i, (i + 1) % peers) for i in range(peers)]
        down = [(j, i) for i, j in up]
        last = lax.slice_in_dim(x, length - width, length, axis=dim)
        first = lax.slice_in_dim(x, 0, width, axis=dim)
        before = lax.ppermute(last, axis, up)
        after = lax.ppermute(first, axis, down)
        x = jnp.concatenate([before, x, after], axis=dim)
    return x


def collide(lattice, weight_in, bias_in, weight_out, bias_out):
    highest = lax.Precision.HIGHEST
    vel_table = jnp.array(velocity_table, jnp.float32)
    lattice_w = jnp.array(lattice_weights, jnp.float32)
    bcast_shape = (19,) + (1,) * (lattice.ndim - 1)
    density = jnp.sum(lattice, axis=0)
    momentum = jnp.einsum("qd,q...->d...", vel_table, lattice, precision=highest)
    projected = jnp.einsum("qd,d...->q...", vel_table, momentum, precision=highest)
    speed_sq = jnp.sum(momentum * momentum, axis=0)
    equilibrium = lattice_w.reshape(bcast_shape) * (
        density + 3.0 * projected + 4.5 * projected * projected - 1.5 * speed_sq
    )
    excess = lattice - equilibrium
    hidden = jnp.tanh(
        jnp.einsum("qh,q...->h...", weight_in, input_scale * excess, precision=highest)
        + bias_in.reshape((-1,) + (1,) * (lattice.ndim - 1))
    )
    correction = output_scale * (
        jnp.einsum("hq,h...->q...", weight_out, hidden, precision=highest)
        + bias_out.reshape(bcast_shape)
    )
    return lattice - excess / relax_time + correction


def local_stream(padded, heading):
    first_len = padded.shape[1] - 2
    second_len = padded.shape[2] - 2
    planes = []
    for q in range(19):
        step_x = heading * velocity_table[q][0]
        step_y = heading * velocity_table[q][1]
        step_z = heading * velocity_table[q][2]
        window = padded[
            q, 1 - step_x : 1 - step_x + first_len, 1 - step_y : 1 - step_y + second_len, :
        ]
        planes.append(jnp.roll(window, step_z, axis=-1))
    return jnp.stack(planes)


def stream(lattice, heading):
    padded = padded_2(lattice, (("gx", 1), ("gy", 2)), 1)
    return local_stream(padded, heading)


def body(populations, target_density, weight_in, bias_in, weight_out, bias_out):
    params = (weight_in, bias_in, weight_out, bias_out)
    vel_table = jnp.array(velocity_table, jnp.float32)
    cells_all = populations[0].size * lax.axis_size("gx") * lax.axis_size("gy")
    residual_scale = 1.0 / math.sqrt(cells_all)
    after1 = stream(collide(populations, *params), 1)
    after2 = stream(collide(after1, *params), 1)
    density = jnp.sum(after2, axis=0)
    momentum = jnp.einsum("qd,q...->d...", vel_table, after2, precision=lax.Precision.HIGHEST)
    moments = jnp.concatenate([density[None], momentum], axis=0)
    grad_density = (density - target_density) * residual_scale
    cotangent = jnp.broadcast_to(grad_density[None], after2.shape)
    back1 = stream(cotangent, -1)
    _, pullback_late = jax.vjp(collide, after1, *params)
    late_terms = pullback_late(back1)
    back0 = stream(late_terms[0], -1)
    _, pullback_early = jax.vjp(collide, populations, *params)
    early_terms = pullback_early(back0)
    late_sum = lax.psum(tuple(late_terms[1:]), ("gx", "gy"))
    early_sum = lax.psum(tuple(early_terms[1:]), ("gx", "gy"))
    totals = tuple((a + b for a, b in zip(early_sum, late_sum)))
    return (moments, totals[0], totals[1], totals[2], totals[3])


def solution(mesh):
    placed = (P(None, "gx", "gy", None), P("gx", "gy", None), P(), P(), P(), P())
    return jax.shard_map(
        body,
        mesh=mesh,
        in_specs=placed,
        out_specs=(P(None, "gx", "gy", None), P(), P(), P(), P()),
        check_vma=False,
    )
```

profile of v0, /device:TPU:1, one launch (start us, length us, event | category | flops | bytes accessed | tf_op | source)
XLA Modules:
  0.0 264.7 jit_solution(3001566090079589804)
XLA Ops:
  0.7 1.2 reduce_sum.286
  1.9 0.9 multiply_reduce_fusion.1
  2.8 0.9 fusion.88
  4.4 1.4 fusion.5
  5.9 0.8 fusion.72
  7.5 5.7 %collective-permute-start = (f32[19,1,16,256]{3,2,1,0:T(8,128)S(1)}, f32[19,1,16,256]{3,2,1,0:T(8,128)S(1)}, u32[]{:S(2)}, u32[]{:S(2)}) collective-permute-start(f32[19,1,16,256]{3,2,1,0:T(8,128)S(1)} %get-tuple-element.113), channel_id=1, source_target_pairs={{0,4},{4,8},{8,12},{12,16},{16,20},{20,24},{24,28},{28,32},{32,36}... | collective-permute-start | bytes 933896 | tf_op jit(solution)/shard_map/ppermute | solution.py:42
  13.1 13.0 %collective-permute-start.1 = (f32[19,1,16,256]{3,2,1,0:T(8,128)S(1)}, f32[19,1,16,256]{3,2,1,0:T(8,128)S(1)}, u32[]{:S(2)}, u32[]{:S(2)}) collective-permute-start(f32[19,1,16,256]{3,2,1,0:T(8,128)S(1)} %get-tuple-element.114), channel_id=1, source_target_pairs={{4,0},{8,4},{12,8},{16,12},{20,16},{24,20},{28,24},{32,28},{36,32}... | collective-permute-start | bytes 933896 | tf_op jit(solution)/shard_map/ppermute | solution.py:43
  26.2 5.1 %collective-permute-done = f32[19,1,16,256]{3,2,1,0:T(8,128)S(1)} collective-permute-done((f32[19,1,16,256]{3,2,1,0:T(8,128)S(1)}, f32[19,1,16,256]{3,2,1,0:T(8,128)S(1)}, u32[]{:S(2)}, u32[]{:S(2)}) %collective-permute-start) | collective-permute-done | bytes 311328 | tf_op jit(solution)/shard_map/ppermute | solution.py:42
  31.3 0.9 collective-permute-done.1
  32.3 3.7 %collective-permute-start.2 = (f32[19,4,1,256]{3,2,1,0:T(1,128)S(1)}, f32[19,4,1,256]{3,2,1,0:T(1,128)S(1)}, u32[]{:S(2)}, u32[]{:S(2)}) collective-permute-start(f32[19,4,1,256]{3,2,1,0:T(1,128)S(1)} %get-tuple-element.72), channel_id=1, source_target_pairs={{0,1},{1,2},{2,3},{3,0},{4,5},{5,6},{6,7},{7,4},{8,9},{9,10},{10,1... | collective-permute-start | bytes 233480 | tf_op jit(solution)/shard_map/ppermute | solution.py:42
  36.1 1.9 collective-permute-start.3
  38.5 3.3 %collective-permute-done.3 = f32[19,4,1,256]{3,2,1,0:T(1,128)S(1)} collective-permute-done((f32[19,4,1,256]{3,2,1,0:T(1,128)S(1)}, f32[19,4,1,256]{3,2,1,0:T(1,128)S(1)}, u32[]{:S(2)}, u32[]{:S(2)}) %collective-permute-start.3) | collective-permute-done | bytes 77856 | tf_op jit(solution)/shard_map/ppermute | solution.py:43
  43.1 0.9 multiply_reduce_fusion
  44.0 0.9 fusion.89
  45.2 1.4 fusion.3
  46.6 0.8 fusion.70
  48.1 1.9 collective-permute-start.4
  50.1 11.0 %collective-permute-start.5 = (f32[19,1,16,256]{3,2,1,0:T(8,128)S(1)}, f32[19,1,16,256]{3,2,1,0:T(8,128)S(1)}, u32[]{:S(2)}, u32[]{:S(2)}) collective-permute-start(f32[19,1,16,256]{3,2,1,0:T(8,128)S(1)} %get-tuple-element.105), channel_id=1, source_target_pairs={{4,0},{8,4},{12,8},{16,12},{20,16},{24,20},{28,24},{32,28},{36,32}... | collective-permute-start | bytes 933896 | tf_op jit(solution)/shard_map/ppermute | solution.py:43
  61.0 5.0 %collective-permute-done.4 = f32[19,1,16,256]{3,2,1,0:T(8,128)S(1)} collective-permute-done((f32[19,1,16,256]{3,2,1,0:T(8,128)S(1)}, f32[19,1,16,256]{3,2,1,0:T(8,128)S(1)}, u32[]{:S(2)}, u32[]{:S(2)}) %collective-permute-start.4) | collective-permute-done | bytes 311328 | tf_op jit(solution)/shard_map/ppermute | solution.py:42
  66.0 3.3 %collective-permute-done.5 = f32[19,1,16,256]{3,2,1,0:T(8,128)S(1)} collective-permute-done((f32[19,1,16,256]{3,2,1,0:T(8,128)S(1)}, f32[19,1,16,256]{3,2,1,0:T(8,128)S(1)}, u32[]{:S(2)}, u32[]{:S(2)}) %collective-permute-start.5) | collective-permute-done | bytes 311328 | tf_op jit(solution)/shard_map/ppermute | solution.py:43
  69.5 2.3 collective-permute-start.6
  71.8 2.2 collective-permute-start.7
  74.5 3.0 %collective-permute-done.7 = f32[19,4,1,256]{3,2,1,0:T(1,128)S(1)} collective-permute-done((f32[19,4,1,256]{3,2,1,0:T(1,128)S(1)}, f32[19,4,1,256]{3,2,1,0:T(1,128)S(1)}, u32[]{:S(2)}, u32[]{:S(2)}) %collective-permute-start.7) | collective-permute-done | bytes 77856 | tf_op jit(solution)/shard_map/ppermute | solution.py:43
  79.6 0.9 fusion.17
  80.7 9.5 %collective-permute-start.8 = (f32[19,1,16,256]{3,2,1,0:T(8,128)S(1)}, f32[19,1,16,256]{3,2,1,0:T(8,128)S(1)}, u32[]{:S(2)}, u32[]{:S(2)}) collective-permute-start(f32[19,1,16,256]{3,2,1,0:T(8,128)S(1)} %broadcast_in_dim.11), channel_id=1, source_target_pairs={{4,0},{8,4},{12,8},{16,12},{20,16},{24,20},{28,24},{32,28},{36,32}... | collective-permute-start | bytes 933896 | tf_op jit(solution)/shard_map/ppermute | solution.py:43
  90.2 1.9 collective-permute-start.9
  92.9 3.5 %collective-permute-done.8 = f32[19,1,16,256]{3,2,1,0:T(8,128)S(1)} collective-permute-done((f32[19,1,16,256]{3,2,1,0:T(8,128)S(1)}, f32[19,1,16,256]{3,2,1,0:T(8,128)S(1)}, u32[]{:S(2)}, u32[]{:S(2)}) %collective-permute-start.8) | collective-permute-done | bytes 311328 | tf_op jit(solution)/shard_map/ppermute | solution.py:43
  96.5 9.9 %collective-permute-done.9 = f32[19,1,16,256]{3,2,1,0:T(8,128)S(1)} collective-permute-done((f32[19,1,16,256]{3,2,1,0:T(8,128)S(1)}, f32[19,1,16,256]{3,2,1,0:T(8,128)S(1)}, u32[]{:S(2)}, u32[]{:S(2)}) %collective-permute-start.9) | collective-permute-done | bytes 311328 | tf_op jit(solution)/shard_map/ppermute | solution.py:42
  106.5 2.6 collective-permute-start.11
  109.2 1.9 collective-permute-start.10
  111.1 3.8 %collective-permute-done.10 = f32[19,4,1,256]{3,2,1,0:T(1,128)S(1)} collective-permute-done((f32[19,4,1,256]{3,2,1,0:T(1,128)S(1)}, f32[19,4,1,256]{3,2,1,0:T(1,128)S(1)}, u32[]{:S(2)}, u32[]{:S(2)}) %collective-permute-start.10) | collective-permute-done | bytes 77856 | tf_op jit(solution)/shard_map/ppermute | solution.py:43
  116.5 1.2 convolution_bitcast_fusion.2
  117.7 1.6 fusion.87
  119.3 0.8 fusion.74
  120.8 0.8 convolution_add_fusion.2
  121.7 0.9 fusion.90
  123.1 1.9 collective-permute-start.13
  125.0 9.1 %collective-permute-start.12 = (f32[19,1,16,256]{3,2,1,0:T(8,128)S(1)}, f32[19,1,16,256]{3,2,1,0:T(8,128)S(1)}, u32[]{:S(2)}, u32[]{:S(2)}) collective-permute-start(f32[19,1,16,256]{3,2,1,0:T(8,128)S(1)} %get-tuple-element.96), channel_id=1, source_target_pairs={{4,0},{8,4},{12,8},{16,12},{20,16},{24,20},{28,24},{32,28},{36,32}... | collective-permute-start | bytes 933896 | tf_op jit(solution)/shard_map/ppermute | solution.py:43
  134.1 1.2 convolution_bitcast_fusion.4
  135.3 4.5 %collective-permute-done.13 = f32[19,1,16,256]{3,2,1,0:T(8,128)S(1)} collective-permute-done((f32[19,1,16,256]{3,2,1,0:T(8,128)S(1)}, f32[19,1,16,256]{3,2,1,0:T(8,128)S(1)}, u32[]{:S(2)}, u32[]{:S(2)}) %collective-permute-start.13) | collective-permute-done | bytes 311328 | tf_op jit(solution)/shard_map/ppermute | solution.py:42
  139.8 4.4 %collective-permute-done.12 = f32[19,1,16,256]{3,2,1,0:T(8,128)S(1)} collective-permute-done((f32[19,1,16,256]{3,2,1,0:T(8,128)S(1)}, f32[19,1,16,256]{3,2,1,0:T(8,128)S(1)}, u32[]{:S(2)}, u32[]{:S(2)}) %collective-permute-start.12) | collective-permute-done | bytes 311328 | tf_op jit(solution)/shard_map/ppermute | solution.py:43
  144.3 2.6 %collective-permute-start.15 = (f32[19,4,1,256]{3,2,1,0:T(1,128)S(1)}, f32[19,4,1,256]{3,2,1,0:T(1,128)S(1)}, u32[]{:S(2)}, u32[]{:S(2)}) collective-permute-start(f32[19,4,1,256]{3,2,1,0:T(1,128)S(1)} %get-tuple-element.62), channel_id=1, source_target_pairs={{0,1},{1,2},{2,3},{3,0},{4,5},{5,6},{6,7},{7,4},{8,9},{9,10},{10,1... | collective-permute-start | bytes 233480 | tf_op jit(solution)/shard_map/ppermute | solution.py:42
  146.9 2.1 collective-permute-start.14
  149.1 3.5 %collective-permute-done.14 = f32[19,4,1,256]{3,2,1,0:T(1,128)S(1)} collective-permute-done((f32[19,4,1,256]{3,2,1,0:T(1,128)S(1)}, f32[19,4,1,256]{3,2,1,0:T(1,128)S(1)}, u32[]{:S(2)}, u32[]{:S(2)}) %collective-permute-start.14) | collective-permute-done | bytes 77856 | tf_op jit(solution)/shard_map/ppermute | solution.py:43
  154.6 1.6 fusion.86
  156.2 1.2 fusion.7
  157.5 1.2 fusion.6
  158.7 106.0 %all-reduce = (f32[19,32]{1,0:T(8,128)}, f32[32]{0:T(128)}, f32[32,19]{0,1:T(8,128)}, f32[19]{0:T(128)}) all-reduce(f32[19,32]{1,0:T(8,128)S(1)} %fusion.6, f32[32]{0:T(128)S(1)} %add.152, f32[32,19]{0,1:T(8,128)S(1)} %fusion.7, f32[19]{0:T(128)S(1)} %add.154), channel_id=1, replica_groups=mesh['gx'=128,'gy'=4] {'gx','gy'}, use_global_device_ids=true, to_apply=%region_6.7 | all-reduce | flops 1267 | bytes 10136 | tf_op jit(solution)/shard_map/psum | solution.py:111
  (186 shorter events, 12.7 us)
Async XLA Ops:
  0.6 5.3 %copy-start = (f32[32,19]{0,1:T(8,128)S(1)}, f32[32,19]{0,1:T(8,128)}, u32[]{:S(2)}) copy-start(f32[32,19]{0,1:T(8,128)} %param.19) | copy-start | bytes 7300
  0.6 1.2 copy-start.3
  0.7 1.3 copy-start.1
  2.8 0.9 copy-start.5
  3.7 0.7 copy-start.2
  3.7 0.7 copy-start.6
  5.9 0.9 copy-start.7
  7.5 23.8 %collective-permute-start = (f32[19,1,16,256]{3,2,1,0:T(8,128)S(1)}, f32[19,1,16,256]{3,2,1,0:T(8,128)S(1)}, u32[]{:S(2)}, u32[]{:S(2)}) collective-permute-start(f32[19,1,16,256]{3,2,1,0:T(8,128)S(1)} %get-tuple-element.113), channel_id=1, source_target_pairs={{0,4},{4,8},{8,12},{12,16},{16,20},{20,24},{24,28},{28,32},{32,36}... | collective-permute-start | bytes 933896 | tf_op jit(solution)/shard_map/ppermute | solution.py:42
  13.1 19.1 %collective-permute-start.1 = (f32[19,1,16,256]{3,2,1,0:T(8,128)S(1)}, f32[19,1,16,256]{3,2,1,0:T(8,128)S(1)}, u32[]{:S(2)}, u32[]{:S(2)}) collective-permute-start(f32[19,1,16,256]{3,2,1,0:T(8,128)S(1)} %get-tuple-element.114), channel_id=1, source_target_pairs={{4,0},{8,4},{12,8},{16,12},{20,16},{24,20},{28,24},{32,28},{36,32}... | collective-permute-start | bytes 933896 | tf_op jit(solution)/shard_map/ppermute | solution.py:43
  32.3 6.2 %collective-permute-start.2 = (f32[19,4,1,256]{3,2,1,0:T(1,128)S(1)}, f32[19,4,1,256]{3,2,1,0:T(1,128)S(1)}, u32[]{:S(2)}, u32[]{:S(2)}) collective-permute-start(f32[19,4,1,256]{3,2,1,0:T(1,128)S(1)} %get-tuple-element.72), channel_id=1, source_target_pairs={{0,1},{1,2},{2,3},{3,0},{4,5},{5,6},{6,7},{7,4},{8,9},{9,10},{10,1... | collective-permute-start | bytes 233480 | tf_op jit(solution)/shard_map/ppermute | solution.py:42
  36.1 5.7 %collective-permute-start.3 = (f32[19,4,1,256]{3,2,1,0:T(1,128)S(1)}, f32[19,4,1,256]{3,2,1,0:T(1,128)S(1)}, u32[]{:S(2)}, u32[]{:S(2)}) collective-permute-start(f32[19,4,1,256]{3,2,1,0:T(1,128)S(1)} %get-tuple-element.73), channel_id=1, source_target_pairs={{1,0},{2,1},{3,2},{0,3},{5,4},{6,5},{7,6},{4,7},{9,8},{10,9},{11,1... | collective-permute-start | bytes 233480 | tf_op jit(solution)/shard_map/ppermute | solution.py:43
  48.1 17.9 %collective-permute-start.4 = (f32[19,1,16,256]{3,2,1,0:T(8,128)S(1)}, f32[19,1,16,256]{3,2,1,0:T(8,128)S(1)}, u32[]{:S(2)}, u32[]{:S(2)}) collective-permute-start(f32[19,1,16,256]{3,2,1,0:T(8,128)S(1)} %get-tuple-element.104), channel_id=1, source_target_pairs={{0,4},{4,8},{8,12},{12,16},{16,20},{20,24},{24,28},{28,32},{32,36}... | collective-permute-start | bytes 933896 | tf_op jit(solution)/shard_map/ppermute | solution.py:42
  50.1 19.3 %collective-permute-start.5 = (f32[19,1,16,256]{3,2,1,0:T(8,128)S(1)}, f32[19,1,16,256]{3,2,1,0:T(8,128)S(1)}, u32[]{:S(2)}, u32[]{:S(2)}) collective-permute-start(f32[19,1,16,256]{3,2,1,0:T(8,128)S(1)} %get-tuple-element.105), channel_id=1, source_target_pairs={{4,0},{8,4},{12,8},{16,12},{20,16},{24,20},{28,24},{32,28},{36,32}... | collective-permute-start | bytes 933896 | tf_op jit(solution)/shard_map/ppermute | solution.py:43
  69.5 5.0 %collective-permute-start.6 = (f32[19,4,1,256]{3,2,1,0:T(1,128)S(1)}, f32[19,4,1,256]{3,2,1,0:T(1,128)S(1)}, u32[]{:S(2)}, u32[]{:S(2)}) collective-permute-start(f32[19,4,1,256]{3,2,1,0:T(1,128)S(1)} %get-tuple-element.68), channel_id=1, source_target_pairs={{0,1},{1,2},{2,3},{3,0},{4,5},{5,6},{6,7},{7,4},{8,9},{9,10},{10,1... | collective-permute-start | bytes 233480 | tf_op jit(solution)/shard_map/ppermute | solution.py:42
  71.8 5.7 %collective-permute-start.7 = (f32[19,4,1,256]{3,2,1,0:T(1,128)S(1)}, f32[19,4,1,256]{3,2,1,0:T(1,128)S(1)}, u32[]{:S(2)}, u32[]{:S(2)}) collective-permute-start(f32[19,4,1,256]{3,2,1,0:T(1,128)S(1)} %get-tuple-element.69), channel_id=1, source_target_pairs={{1,0},{2,1},{3,2},{0,3},{5,4},{6,5},{7,6},{4,7},{9,8},{10,9},{11,1... | collective-permute-start | bytes 233480 | tf_op jit(solution)/shard_map/ppermute | solution.py:43
  77.7 0.8 copy-start.4
  80.7 15.8 %collective-permute-start.8 = (f32[19,1,16,256]{3,2,1,0:T(8,128)S(1)}, f32[19,1,16,256]{3,2,1,0:T(8,128)S(1)}, u32[]{:S(2)}, u32[]{:S(2)}) collective-permute-start(f32[19,1,16,256]{3,2,1,0:T(8,128)S(1)} %broadcast_in_dim.11), channel_id=1, source_target_pairs={{4,0},{8,4},{12,8},{16,12},{20,16},{24,20},{28,24},{32,28},{36,32}... | collective-permute-start | bytes 933896 | tf_op jit(solution)/shard_map/ppermute | solution.py:43
  90.2 16.1 %collective-permute-start.9 = (f32[19,1,16,256]{3,2,1,0:T(8,128)S(1)}, f32[19,1,16,256]{3,2,1,0:T(8,128)S(1)}, u32[]{:S(2)}, u32[]{:S(2)}) collective-permute-start(f32[19,1,16,256]{3,2,1,0:T(8,128)S(1)} %broadcast_in_dim.12), channel_id=1, source_target_pairs={{0,4},{4,8},{8,12},{12,16},{16,20},{20,24},{24,28},{28,32},{32,36}... | collective-permute-start | bytes 933896 | tf_op jit(solution)/shard_map/ppermute | solution.py:42
  106.5 8.4 %collective-permute-start.11 = (f32[19,4,1,256]{3,2,1,0:T(1,128)S(1)}, f32[19,4,1,256]{3,2,1,0:T(1,128)S(1)}, u32[]{:S(2)}, u32[]{:S(2)}) collective-permute-start(f32[19,4,1,256]{3,2,1,0:T(1,128)S(1)} %get-tuple-element.64), channel_id=1, source_target_pairs={{0,1},{1,2},{2,3},{3,0},{4,5},{5,6},{6,7},{7,4},{8,9},{9,10},{10,1... | collective-permute-start | bytes 233480 | tf_op jit(solution)/shard_map/ppermute | solution.py:42
  109.2 5.7 %collective-permute-start.10 = (f32[19,4,1,256]{3,2,1,0:T(1,128)S(1)}, f32[19,4,1,256]{3,2,1,0:T(1,128)S(1)}, u32[]{:S(2)}, u32[]{:S(2)}) collective-permute-start(f32[19,4,1,256]{3,2,1,0:T(1,128)S(1)} %get-tuple-element.65), channel_id=1, source_target_pairs={{1,0},{2,1},{3,2},{0,3},{5,4},{6,5},{7,6},{4,7},{9,8},{10,9},{11,1... | collective-permute-start | bytes 233480 | tf_op jit(solution)/shard_map/ppermute | solution.py:43
  123.1 16.7 %collective-permute-start.13 = (f32[19,1,16,256]{3,2,1,0:T(8,128)S(1)}, f32[19,1,16,256]{3,2,1,0:T(8,128)S(1)}, u32[]{:S(2)}, u32[]{:S(2)}) collective-permute-start(f32[19,1,16,256]{3,2,1,0:T(8,128)S(1)} %get-tuple-element.95), channel_id=1, source_target_pairs={{0,4},{4,8},{8,12},{12,16},{16,20},{20,24},{24,28},{28,32},{32,36}... | collective-permute-start | bytes 933896 | tf_op jit(solution)/shard_map/ppermute | solution.py:42
  125.0 19.2 %collective-permute-start.12 = (f32[19,1,16,256]{3,2,1,0:T(8,128)S(1)}, f32[19,1,16,256]{3,2,1,0:T(8,128)S(1)}, u32[]{:S(2)}, u32[]{:S(2)}) collective-permute-start(f32[19,1,16,256]{3,2,1,0:T(8,128)S(1)} %get-tuple-element.96), channel_id=1, source_target_pairs={{4,0},{8,4},{12,8},{16,12},{20,16},{24,20},{28,24},{32,28},{36,32}... | collective-permute-start | bytes 933896 | tf_op jit(solution)/shard_map/ppermute | solution.py:43
  144.3 8.4 %collective-permute-start.15 = (f32[19,4,1,256]{3,2,1,0:T(1,128)S(1)}, f32[19,4,1,256]{3,2,1,0:T(1,128)S(1)}, u32[]{:S(2)}, u32[]{:S(2)}) collective-permute-start(f32[19,4,1,256]{3,2,1,0:T(1,128)S(1)} %get-tuple-element.62), channel_id=1, source_target_pairs={{0,1},{1,2},{2,3},{3,0},{4,5},{5,6},{6,7},{7,4},{8,9},{9,10},{10,1... | collective-permute-start | bytes 233480 | tf_op jit(solution)/shard_map/ppermute | solution.py:42
  146.9 5.7 %collective-permute-start.14 = (f32[19,4,1,256]{3,2,1,0:T(1,128)S(1)}, f32[19,4,1,256]{3,2,1,0:T(1,128)S(1)}, u32[]{:S(2)}, u32[]{:S(2)}) collective-permute-start(f32[19,4,1,256]{3,2,1,0:T(1,128)S(1)} %get-tuple-element.63), channel_id=1, source_target_pairs={{1,0},{2,1},{3,2},{0,3},{5,4},{6,5},{7,6},{4,7},{9,8},{10,9},{11,1... | collective-permute-start | bytes 233480 | tf_op jit(solution)/shard_map/ppermute | solution.py:43
where the time goes:
time: 266 us; the launch traced here: 265 us
  blocking collectives  106 us (40%)
  starting transfers between devices  73.5 us (28%)
  waiting for transfers between devices  50.3 us (19%)
  matrix products  19.5 us (7%)
  other arithmetic  8.72 us (3%)
  local copies, waits for them, and re-layouts  5.14 us (2%)
    psum x1, blocking collectives, body(): early_sum = lax.psum(tuple(early_terms[1:]), ('gx', 'gy'))  106 us
    ppermute x8, starting transfers between devices, padded_2(): after = lax.ppermute(first, axis, down)  50.7 us
    ppermute x8, waiting for transfers between devices, padded_2(): after = lax.ppermute(first, axis, down)  25.7 us
    ppermute x8, waiting for transfers between devices, padded_2(): before = lax.ppermute(last, axis, up)  24.5 us
    ppermute x8, starting transfers between devices, padded_2(): before = lax.ppermute(last, axis, up)  22.8 us
    dot_general x6, matrix products, collide(): jnp.einsum('hq,h...->q...', weight_out, hidden, precision=highest)  7.36 us
    dot_general x5, matrix products, collide(): jnp.einsum('qh,q...->h...', weight_in, input_scale * excess, precision=hi...  6.14 us
  transfers between devices with their start and end apart: 16, of which 12 were waited for; matrix products, arithmetic and copies ran while one was open for 1% of the time, Pallas kernels for 0%

commit v1 on v0

v1 whole, which is shorter than its diff:
```python
import math

import jax
import jax.numpy as jnp
from jax import lax
from jax.experimental import pallas as pl
from jax.experimental.pallas import tpu as pltpu
from jax.sharding import Mesh, PartitionSpec as P

velocity_table = (
    (0, 0, 0),
    (1, 0, 0),
    (-1, 0, 0),
    (0, 1, 0),
    (0, -1, 0),
    (0, 0, 1),
    (0, 0, -1),
    (1, 1, 0),
    (-1, -1, 0),
    (1, -1, 0),
    (-1, 1, 0),
    (1, 0, 1),
    (-1, 0, -1),
    (1, 0, -1),
    (-1, 0, 1),
    (0, 1, 1),
    (0, -1, -1),
    (0, 1, -1),
    (0, -1, 1),
)
lattice_weights = (1.0 / 3.0,) + (1.0 / 18.0,) * 6 + (1.0 / 36.0,) * 12
input_scale = 8.0
output_scale = 0.05
relax_time = 0.8

Q = 19
H = 32
NZ = 256
YW = 20
ROWS = 6 * YW
G1 = ROWS // 8
B2 = 16
G2 = 11
MARGIN = 24
SP = 8
QS = 20 * SP
HS = H * SP
F32 = jnp.float32
BF16 = jnp.bfloat16


def row_shift(q):
    return YW * velocity_table[q][0] + velocity_table[q][1]


def split(x):
    hi = x.astype(BF16)
    lo = (x - hi.astype(F32)).astype(BF16)
    return hi, lo


def mm(a, b):
    return lax.dot_general(a, b, (((1,), (0,)), ((), ())), preferred_element_type=F32)


def mm_nt(a, b):
    return lax.dot_general(a, b, (((1,), (1,)), ((), ())), preferred_element_type=F32)


def prep_kernel(win_ref, bin_ref, wout_ref, lin_ref, lint_ref, lout_ref, loutt_ref):
    hp = lax.Precision.HIGHEST
    nt = (((1,), (1,)), ((), ()))
    eq = (
        lax.broadcasted_iota(jnp.int32, (QS, Q), 0) // SP
        == lax.broadcasted_iota(jnp.int32, (QS, Q), 1)
    ).astype(F32)
    eh = (
        lax.broadcasted_iota(jnp.int32, (HS, H), 0) // SP
        == lax.broadcasted_iota(jnp.int32, (HS, H), 1)
    ).astype(F32)
    rq = lax.broadcasted_iota(jnp.int32, (QS, HS), 0)
    rh = lax.broadcasted_iota(jnp.int32, (QS, HS), 1)
    mask_qh = (rq % SP) == (rh % SP)
    ch = lax.broadcasted_iota(jnp.int32, (HS, QS), 0)
    cq = lax.broadcasted_iota(jnp.int32, (HS, QS), 1)
    mask_hq = (ch % SP) == (cq % SP)

    t_in = lax.dot_general(eq, win_ref[...] * input_scale, (((1,), (0,)), ((), ())), precision=hp, preferred_element_type=F32)
    t_out = lax.dot_general(eq, wout_ref[...] * output_scale, nt, precision=hp, preferred_element_type=F32)
    is_bias = lax.broadcasted_iota(jnp.int32, (QS, H), 0) >= Q * SP
    t_inb = jnp.where(is_bias, jnp.broadcast_to(bin_ref[...], (QS, H)), t_in)

    def put(ref, a, b, mask):
        full = lax.dot_general(a, b, nt, precision=hp, preferred_element_type=F32)
        hi, lo = split(jnp.where(mask, full, 0.0))
        n = full.shape[1]
        ref[:, 0:n] = hi
        ref[:, n : 2 * n] = hi
        ref[:, 2 * n : 3 * n] = lo

    put(lin_ref, eh, t_inb, mask_hq)
    put(lint_ref, t_in, eh, mask_qh)
    put(lout_ref, t_out, eh, mask_qh)
    put(loutt_ref, eh, t_out, mask_hq)


def equilibrium_parts(f):
    density = f[0]
    for q in range(1, Q):
        density = density + f[q]
    momentum = []
    for a in range(3):
        plus = None
        minus = None
        for q in range(Q):
            c = velocity_table[q][a]
            if c == 1:
                plus = f[q] if plus is None else plus + f[q]
            elif c == -1:
                minus = f[q] if minus is None else minus + f[q]
        momentum.append(plus - minus)
    return density, momentum


def project(q, m):
    out = None
    for a in range(3):
        c = velocity_table[q][a]
        if c == 0:
            continue
        if out is None:
            out = m[a] if c == 1 else -m[a]
        else:
            out = out + m[a] if c == 1 else out - m[a]
    return out


def excess_of(f):
    density, m = equilibrium_parts(f)
    base = density - 1.5 * (m[0] * m[0] + m[1] * m[1] + m[2] * m[2])
    excess = [f[0] - lattice_weights[0] * base]
    for q in range(1, Q, 2):
        w = lattice_weights[q]
        cm = project(q, m)
        even = w * (base + 4.5 * (cm * cm))
        odd = (3.0 * w) * cm
        excess.append(f[q] - (even + odd))
        excess.append(f[q + 1] - (even - odd))
    return excess, m


def rows8(x, q):
    return x[q * SP : (q + 1) * SP, :]


def collide(f, lin_ref, lout_ref, bout_ref, save_x, save_h):
    excess, m = excess_of(f)
    x = jnp.concatenate(excess + [jnp.ones((SP, NZ), F32)], axis=0)
    xhi, xlo = split(x)
    save_x(xhi, xlo)
    pre = mm(lin_ref[...], jnp.concatenate([xhi, xlo, xhi], axis=0))
    hid = jnp.tanh(pre)
    hhi, hlo = split(hid)
    save_h(hhi, hlo)
    corr = mm(lout_ref[...], jnp.concatenate([hhi, hlo, hhi], axis=0))
    out = []
    for q in range(Q):
        out.append(f[q] - excess[q] * (1.0 / relax_time) + (rows8(corr, q) + output_scale * bout_ref[q]))
    return out, m


def zroll(x, step):
    if step == 0:
        return x
    return pltpu.roll(x, step % NZ, 1)


def main_kernel(
    parity_ref,
    bout_ref,
    own_ref,
    a_ref,
    b_ref,
    target_ref,
    lin_ref,
    lint_ref,
    lout_ref,
    loutt_ref,
    moments_ref,
    grads_ref,
    fs,
    c1s,
    c2s,
    g1s,
    rs,
    x1s,
    h1s,
    x2s,
    h2s,
    m2s,
    acc_in,
    acc_out,
    acc_b,
    sems,
):
    parity = parity_ref[0]
    a_row = pl.multiple_of(80 * (1 - parity), 8)
    b_row = pl.multiple_of(80 * parity, 8)
    copies = [
        pltpu.make_async_copy(own_ref, fs.at[:, 40:80, :], sems.at[0]),
        pltpu.make_async_copy(a_ref, fs.at[:, pl.ds(a_row, 40), :], sems.at[1]),
        pltpu.make_async_copy(b_ref, fs.at[:, pl.ds(b_row, 40), :], sems.at[2]),
    ]
    for c in copies:
        c.start()
    acc_in[...] = jnp.zeros_like(acc_in)
    acc_out[...] = jnp.zeros_like(acc_out)
    acc_b[...] = jnp.zeros_like(acc_b)
    rs[...] = jnp.zeros_like(rs)
    zero_top = jnp.zeros((Q, MARGIN, NZ), F32)
    c1s[:, 0:MARGIN, :] = zero_top
    c1s[:, MARGIN + ROWS :, :] = zero_top
    g1s[:, 0 : MARGIN + B2, :] = jnp.zeros((Q, MARGIN + B2, NZ), F32)
    g1s[:, MARGIN + B2 + 8 * G2 :, :] = jnp.zeros((Q, MARGIN + ROWS - B2 - 8 * G2, NZ), F32)
    for c in copies:
        c.wait()

    def load(ref, q, row, off):
        base = (off // 8) * 8
        rem = off % 8
        start = pl.multiple_of(row + base, 8)
        if rem == 0:
            return ref[q, pl.ds(start, 8), :]
        both = ref[q, pl.ds(start, 16), :]
        return both[rem : rem + 8, :]

    def stage1(g, _):
        row = pl.multiple_of(g * 8, 8)
        f = [fs[q, pl.ds(row, 8), :] for q in range(Q)]

        def save_x(hi, lo):
            x1s[g, 0:QS, :] = hi
            x1s[g, QS : 2 * QS, :] = lo

        def save_h(hi, lo):
            h1s[g, 0:HS, :] = hi
            h1s[g, HS : 2 * HS, :] = lo

        out, _m = collide(f, lin_ref, lout_ref, bout_ref, save_x, save_h)
        for q in range(Q):
            c1s[q, pl.ds(row + MARGIN, 8), :] = zroll(out[q], velocity_table[q][2])
        return 0

    lax.fori_loop(0, G1, stage1, 0)

    def stage2(g, _):
        row = pl.multiple_of(g * 8 + B2, 8)
        f = [load(c1s, q, row, MARGIN - row_shift(q)) for q in range(Q)]

        def save_x(hi, lo):
            x2s[g, 0:QS, :] = hi
            x2s[g, QS : 2 * QS, :] = lo

        def save_h(hi, lo):
            h2s[g, 0:HS, :] = hi
            h2s[g, HS : 2 * HS, :] = lo

        out, m = collide(f, lin_ref, lout_ref, bout_ref, save_x, save_h)
        for a in range(3):
            m2s[g, a] = m[a]
        for q in range(Q):
            c2s[q, pl.ds(row, 8), :] = zroll(out[q], velocity_table[q][2])
        return 0

    lax.fori_loop(0, G2, stage2, 0)

    residual_scale = 1.0 / math.sqrt(256 * 64 * 256)
    for x in range(2):
        for half in range(2):
            first = YW * (x + 2) + 2 + 8 * half
            f = [c2s[q, first - row_shift(q) : first - row_shift(q) + 8, :] for q in range(Q)]
            density, m = equilibrium_parts(f)
            moments_ref[0, x, 8 * half : 8 * half + 8, :] = density
            for a in range(3):
                moments_ref[a + 1, x, 8 * half : 8 * half + 8, :] = m[a]
            r = (density - target_ref[x, 8 * half : 8 * half + 8, :]) * residual_scale
            rs[0, MARGIN + first : MARGIN + first + 8, :] = r
            rs[1, MARGIN + first : MARGIN + first + 8, :] = zroll(r, -1)
            rs[2, MARGIN + first : MARGIN + first + 8, :] = zroll(r, 1)

    def pull_params(gq, x_hl, h_hl, g):
        gs = jnp.concatenate(gq + [jnp.zeros((SP, NZ), F32)], axis=0)
        ghi, glo = split(gs)
        dh = mm(loutt_ref[...], jnp.concatenate([ghi, glo, ghi], axis=0))
        hhi = h_hl[g, 0:HS, :]
        hlo = h_hl[g, HS : 2 * HS, :]
        hid = hhi.astype(F32) + hlo.astype(F32)
        dpre = dh * (1.0 - hid * hid)
        dhi, dlo = split(dpre)
        xhi = x_hl[g, 0:QS, :]
        xlo = x_hl[g, QS : 2 * QS, :]
        acc_in[...] += mm_nt(
            jnp.concatenate([xhi, xlo, xhi], axis=1), jnp.concatenate([dhi, dhi, dlo], axis=1)
        )
        acc_out[...] += mm_nt(
            jnp.concatenate([ghi, glo, ghi], axis=1), jnp.concatenate([hhi, hhi, hlo], axis=1)
        )
        acc_b[...] += gs
        return dhi, dlo

    def stage4(g, _):
        row = pl.multiple_of(g * 8 + B2, 8)
        gq = []
        for q in range(Q):
            cz = velocity_table[q][2]
            gq.append(load(rs, {0: 0, 1: 1, -1: 2}[cz], row, MARGIN + row_shift(q)))
        dhi, dlo = pull_params(gq, x2s, h2s, g)
        back = mm(lint_ref[...], jnp.concatenate([dhi, dlo, dhi], axis=0))
        m = [m2s[g, a] for a in range(3)]
        de = [rows8(back, q) - gq[q] * (1.0 / relax_time) for q in range(Q)]
        t = [lattice_weights[q] * de[q] for q in range(Q)]
        drho = t[0]
        for q in range(1, Q):
            drho = drho + t[q]
        u = [None] * Q
        for q in range(1, Q, 2):
            cm = 9.0 * project(q, m)
            u[q] = t[q] * (3.0 + cm)
            u[q + 1] = t[q + 1] * (3.0 - cm)
        dm = []
        for a in range(3):
            plus = None
            minus = None
            for q in range(Q):
                c = velocity_table[q][a]
                if c == 1:
                    plus = u[q] if plus is None else plus + u[q]
                elif c == -1:
                    minus = u[q] if minus is None else minus + u[q]
            dm.append(plus - minus - 3.0 * m[a] * drho)
        for q in range(Q):
            df = gq[q] + de[q] - drho
            if q:
                df = df - project(q, dm)
            g1s[q, pl.ds(row + MARGIN, 8), :] = zroll(df, -velocity_table[q][2])
        return 0

    lax.fori_loop(0, G2, stage4, 0)

    def stage5(g, _):
        row = pl.multiple_of(g * 8, 8)
        gq = [load(g1s, q, row, MARGIN + row_shift(q)) for q in range(Q)]
        pull_params(gq, x1s, h1s, g)
        return 0

    lax.fori_loop(0, G1, stage5, 0)

    hp = lax.Precision.HIGHEST
    rq = lax.broadcasted_iota(jnp.int32, (QS, HS), 0)
    rh = lax.broadcasted_iota(jnp.int32, (QS, HS), 1)
    mask = (rq % SP) == (rh % SP)
    fold = (
        lax.broadcasted_iota(jnp.int32, (HS, H), 0) // SP
        == lax.broadcasted_iota(jnp.int32, (HS, H), 1)
    ).astype(F32)

    def trace(acc):
        kept = jnp.where(mask, acc[...], 0.0).reshape(20, SP, HS).sum(axis=1)
        return lax.dot_general(
            kept, fold, (((1,), (0,)), ((), ())), precision=hp, preferred_element_type=F32
        )

    q_index = lax.broadcasted_iota(jnp.int32, (20, H), 0)
    d_in = trace(acc_in) * jnp.where(q_index < Q, input_scale, 1.0)
    d_out = trace(acc_out) * output_scale
    d_b = acc_b[...].reshape(20, SP, NZ).sum(axis=1).sum(axis=1, keepdims=True) * output_scale
    grads_ref[...] = jnp.zeros_like(grads_ref)
    grads_ref[0:10, 0:H] = d_in[0:10]
    grads_ref[0:10, H : 2 * H] = d_in[10:20]
    grads_ref[0:10, 2 * H : 3 * H] = d_out[0:10]
    grads_ref[0:10, 3 * H : 4 * H] = d_out[10:20]
    for i in range(4):
        grads_ref[10:15, i : i + 1] = d_b[5 * i : 5 * i + 5]


def unpack(grads):
    d_in = jnp.concatenate([grads[0:10, 0:H], grads[0:10, H : 2 * H]], axis=0)
    d_out = jnp.concatenate([grads[0:10, 2 * H : 3 * H], grads[0:10, 3 * H :]], axis=0)
    d_b = grads[10:15, 0:4].T.reshape(20)
    return d_in[0:Q], d_in[Q], d_out[0:Q].T, d_b[0:Q]


def prep(weight_in, bias_in, weight_out):
    return pl.pallas_call(
        prep_kernel,
        out_shape=(
            jax.ShapeDtypeStruct((HS, 3 * QS), BF16),
            jax.ShapeDtypeStruct((QS, 3 * HS), BF16),
            jax.ShapeDtypeStruct((QS, 3 * HS), BF16),
            jax.ShapeDtypeStruct((HS, 3 * QS), BF16),
        ),
        compiler_params=pltpu.CompilerParams(vmem_limit_bytes=24 * 1024 * 1024),
        name="prep",
    )(weight_in, bias_in.reshape(1, H), weight_out)


def main(parity, bias_out, own, a, b, target, mats):
    vmem = pl.BlockSpec(memory_space=pltpu.VMEM)
    smem = pl.BlockSpec(memory_space=pltpu.SMEM)
    anym = pl.BlockSpec(memory_space=pl.ANY)
    span = 2 * MARGIN + ROWS
    return pl.pallas_call(
        main_kernel,
        out_shape=(
            jax.ShapeDtypeStruct((4, 2, 16, NZ), F32),
            jax.ShapeDtypeStruct((16, 128), F32),
        ),
        in_specs=[smem, smem, anym, anym, anym, vmem, vmem, vmem, vmem, vmem],
        out_specs=(vmem, vmem),
        scratch_shapes=[
            pltpu.VMEM((Q, ROWS, NZ), F32),
            pltpu.VMEM((Q, span, NZ), F32),
            pltpu.VMEM((Q, ROWS, NZ), F32),
            pltpu.VMEM((Q, span, NZ), F32),
            pltpu.VMEM((3, span, NZ), F32),
            pltpu.VMEM((G1, 2 * QS, NZ), BF16),
            pltpu.VMEM((G1, 2 * HS, NZ), BF16),
            pltpu.VMEM((G2, 2 * QS, NZ), BF16),
            pltpu.VMEM((G2, 2 * HS, NZ), BF16),
            pltpu.VMEM((G2, 3, SP, NZ), F32),
            pltpu.VMEM((QS, HS), F32),
            pltpu.VMEM((QS, HS), F32),
            pltpu.VMEM((QS, NZ), F32),
            pltpu.SemaphoreType.DMA((3,)),
        ],
        compiler_params=pltpu.CompilerParams(vmem_limit_bytes=48 * 1024 * 1024),
        name="lattice",
    )(parity, bias_out, own, a, b, target, *mats)


def body(populations, target_density, weight_in, bias_in, weight_out, bias_out):
    gx, gy = ("zh", "zl", "x", "yh"), ("yl", "c")
    nx, ny = lax.axis_size(gx), lax.axis_size(gy)
    mats = prep(weight_in, bias_in, weight_out)
    last = populations[:, :, 14:16, :].reshape(Q, 4, NZ)
    first = populations[:, :, 0:2, :].reshape(Q, 4, NZ)
    before = lax.ppermute(last, gy, [(j, (j + 1) % ny) for j in range(ny)])
    after = lax.ppermute(first, gy, [((j + 1) % ny, j) for j in range(ny)])
    own = jnp.concatenate(
        [
            before[:, 0:2],
            populations[:, 0],
            after[:, 0:2],
            before[:, 2:4],
            populations[:, 1],
            after[:, 2:4],
        ],
        axis=1,
    )
    pair = [(i, i ^ 1) for i in range(nx)]
    cross = [(i, (i + 1) % nx if i % 2 else (i - 1) % nx) for i in range(nx)]
    b = lax.ppermute(own, gx, cross)
    a = lax.ppermute(own, gx, pair)
    parity = (lax.axis_index("yh") % 2).astype(jnp.int32).reshape(1)
    moments, grads = main(parity, bias_out, own, a, b, target_density, mats)
    grads = lax.psum(grads, ("yl", "c"))
    grads = lax.psum(grads, "yh")
    grads = lax.psum(grads, "x")
    grads = lax.psum(grads, "zl")
    grads = lax.psum(grads, "zh")
    return (moments, *unpack(grads))


def solution(mesh):
    fine = Mesh(mesh.devices.reshape(4, 4, 4, 2, 2, 2), ("zh", "zl", "x", "yh", "yl", "c"))
    gx, gy = ("zh", "zl", "x", "yh"), ("yl", "c")
    placed = (P(None, gx, gy, None), P(gx, gy, None), P(), P(), P(), P())
    return jax.shard_map(
        body,
        mesh=fine,
        in_specs=placed,
        out_specs=(P(None, gx, gy, None), P(), P(), P(), P()),
        check_vma=False,
    )
```

time: 266 us -> 150 us (0.56)
  the two profiles are of different devices: /device:TPU:1 before, /device:TPU:16 now
where the time goes in v1:
time: 150 us; the launch traced here: 149 us
  blocking collectives  51.8 us (35%)
  Pallas kernels  38.1 us (25%)
  waiting for transfers between devices  28.9 us (19%)
  starting transfers between devices  24 us (16%)
  local copies, waits for them, and re-layouts  5.04 us (3%)
    pallas_call x1, Pallas kernels, main(): pl.pallas_call(main_kernel, out_shape=(jax.ShapeDtypeStruct((4, 2, 16, NZ...  36.9 us
    ppermute x1, waiting for transfers between devices, body(): a = lax.ppermute(own, gx, pair)  23.2 us
    psum x1, blocking collectives, body(): grads = lax.psum(grads, 'zh')  17.7 us
    ppermute x1, starting transfers between devices, body(): a = lax.ppermute(own, gx, pair)  15.3 us
    psum x1, blocking collectives, body(): grads = lax.psum(grads, 'zl')  12.9 us
    psum x1, blocking collectives, body(): grads = lax.psum(grads, 'x')  7.83 us
    psum x1, blocking collectives, body(): grads = lax.psum(grads, ('yl', 'c'))  6.81 us
    psum x1, blocking collectives, body(): grads = lax.psum(grads, 'yh')  6.53 us
  transfers between devices with their start and end apart: 4, of which 3 were waited for; matrix products, arithmetic and copies ran while one was open for 0% of the time, Pallas kernels for 1%

profile of v1, /device:TPU:16, one launch (start us, length us, event | category | flops | bytes accessed | tf_op | source)
XLA Modules:
  0.0 149.3 jit_solution(18093530216254278919)
XLA Ops:
  0.6 0.0 copy-start.4
  0.6 1.2 fusion.1
  1.8 0.1 reshape.26
  1.9 1.9 %collective-permute-start = (f32[19,4,256]{2,1,0:T(4,128)S(1)}, f32[19,4,256]{2,1,0:T(4,128)S(1)}, u32[]{:S(2)}, u32[]{:S(2)}) collective-permute-start(f32[19,4,256]{2,1,0:T(4,128)S(1)} %reshape.26), channel_id=1, source_target_pairs={{0,1},{1,2},{2,3},{3,0},{4,5},{5,6},{6,7},{7,4},{8,9},{9,10},{10,1... | collective-permute-start | bytes 233480 | tf_op jit(solution)/shard_map/ppermute | solution.py:447
  3.8 0.1 reshape.27
  3.9 3.6 %collective-permute-start.1 = (f32[19,4,256]{2,1,0:T(4,128)S(1)}, f32[19,4,256]{2,1,0:T(4,128)S(1)}, u32[]{:S(2)}, u32[]{:S(2)}) collective-permute-start(f32[19,4,256]{2,1,0:T(4,128)S(1)} %reshape.27), channel_id=1, source_target_pairs={{1,0},{2,1},{3,2},{0,3},{5,4},{6,5},{7,6},{4,7},{9,8},{10,9},{11,1... | collective-permute-start | bytes 233480 | tf_op jit(solution)/shard_map/ppermute | solution.py:448
  7.6 0.0 copy-done.4
  7.6 0.0 collective-permute-done
  7.7 1.9 %collective-permute-done.1 = f32[19,4,256]{2,1,0:T(4,128)S(1)} collective-permute-done((f32[19,4,256]{2,1,0:T(4,128)S(1)}, f32[19,4,256]{2,1,0:T(4,128)S(1)}, u32[]{:S(2)}, u32[]{:S(2)}) %collective-permute-start.1) | collective-permute-done | bytes 77856 | tf_op jit(solution)/shard_map/ppermute | solution.py:448
  9.6 0.9 concatenate.9.own_ref
  10.5 0.0 copy-start.5
  10.5 3.2 %collective-permute-start.3 = (f32[19,40,256]{2,1,0:T(8,128)S(1)}, f32[19,40,256]{2,1,0:T(8,128)S(1)}, u32[]{:S(2)}, u32[]{:S(2)}) collective-permute-start(f32[19,40,256]{2,1,0:T(8,128)S(1)} %concatenate.9.own_ref), channel_id=1, source_target_pairs={{0,508},{4,8},{8,4},{12,16},{16,12},{20,24},{24,20},{28,32},{32,28... | collective-permute-start | bytes 2334728 | tf_op jit(solution)/shard_map/ppermute | solution.py:462
  13.7 15.3 %collective-permute-start.2 = (f32[19,40,256]{2,1,0:T(8,128)S(1)}, f32[19,40,256]{2,1,0:T(8,128)S(1)}, u32[]{:S(2)}, u32[]{:S(2)}) collective-permute-start(f32[19,40,256]{2,1,0:T(8,128)S(1)} %concatenate.9.own_ref), channel_id=1, source_target_pairs={{0,4},{4,0},{8,12},{12,8},{16,20},{20,16},{24,28},{28,24},{32,36},... | collective-permute-start | bytes 2334728 | tf_op jit(solution)/shard_map/ppermute | solution.py:463
  29.0 0.0 copy-start.2
  29.0 0.0 copy-start.1
  29.0 0.0 copy-done.5
  29.0 0.0 copy-start
  29.1 0.1 copy.17.wout_ref
  29.1 0.5 copy-done.2
  29.7 0.1 copy-done.1
  29.7 1.2 prep.1
  30.9 3.8 %collective-permute-done.3.b_ref = f32[19,40,256]{2,1,0:T(8,128)S(1)} collective-permute-done((f32[19,40,256]{2,1,0:T(8,128)S(1)}, f32[19,40,256]{2,1,0:T(8,128)S(1)}, u32[]{:S(2)}, u32[]{:S(2)}) %collective-permute-start.3) | collective-permute-done | bytes 778272 | tf_op jit(solution)/shard_map/ppermute | solution.py:462
  34.7 23.2 %collective-permute-done.2.a_ref = f32[19,40,256]{2,1,0:T(8,128)S(1)} collective-permute-done((f32[19,40,256]{2,1,0:T(8,128)S(1)}, f32[19,40,256]{2,1,0:T(8,128)S(1)}, u32[]{:S(2)}, u32[]{:S(2)}) %collective-permute-start.2) | collective-permute-done | bytes 778272 | tf_op jit(solution)/shard_map/ppermute | solution.py:463
  58.0 0.0 copy-start.3
  58.0 0.0 copy-done
  58.0 0.7 copy-done.3
  58.6 36.9 %lattice.1 = (f32[4,2,16,256]{3,2,1,0:T(8,128)}, f32[16,128]{1,0:T(8,128)S(1)}) custom-call(s32[1]{0:T(128)} %bitcast.parity_ref, f32[19]{0:T(128)S(1)} %copy-done.3, f32[19,40,256]{2,1,0:T(8,128)S(1)} %concatenate.9.own_ref, f32[19,40,256]{2,1,0:T(8,128)S(1)} %collective-permute-done.2.a_ref, f32[19,40,256]{2,1,0:T(8,128)S(1)} %collective-permute-done.3.b_ref, ...), custom_call_target="tpu_custom_call" | custom-call | tf_op jit(solution)/shard_map/lattice/pallas_call | solution.py:412
  95.5 6.8 %psum.35 = f32[16,128]{1,0:T(8,128)S(1)} all-reduce(f32[16,128]{1,0:T(8,128)S(1)} %get-tuple-element.16), channel_id=1, replica_groups=mesh['zh'=4,'zl'=4,'x'=4,'yh'=2,'yl'=2,'c'=2] {'yl','c'}, use_global_device_ids=true, to_apply=%region_0.1 | all-reduce | flops 2048 | bytes 16384 | tf_op jit(solution)/shard_map/psum | solution.py:466
  102.4 6.5 %psum.36 = f32[16,128]{1,0:T(8,128)S(1)} all-reduce(f32[16,128]{1,0:T(8,128)S(1)} %psum.35), channel_id=1, replica_groups=mesh['zh'=4,'zl'=4,'x'=4,'yh'=2,'yl'=2,'c'=2] {'yh'}, use_global_device_ids=true, to_apply=%region_1.2 | all-reduce | flops 2048 | bytes 16384 | tf_op jit(solution)/shard_map/psum | solution.py:467
  108.9 7.8 %psum.37 = f32[16,128]{1,0:T(8,128)S(1)} all-reduce(f32[16,128]{1,0:T(8,128)S(1)} %psum.36), channel_id=1, replica_groups=mesh['zh'=4,'zl'=4,'x'=4,'yh'=2,'yl'=2,'c'=2] {'x'}, use_global_device_ids=true, to_apply=%region_2.3 | all-reduce | flops 2048 | bytes 16384 | tf_op jit(solution)/shard_map/psum | solution.py:468
  116.7 12.9 %psum.38 = f32[16,128]{1,0:T(8,128)S(1)} all-reduce(f32[16,128]{1,0:T(8,128)S(1)} %psum.37), channel_id=1, replica_groups=mesh['zh'=4,'zl'=4,'x'=4,'yh'=2,'yl'=2,'c'=2] {'zl'}, use_global_device_ids=true, to_apply=%region_3.4 | all-reduce | flops 2048 | bytes 16384 | tf_op jit(solution)/shard_map/psum | solution.py:469
  129.6 17.7 %psum.39 = f32[16,128]{1,0:T(8,128)S(1)} all-reduce(f32[16,128]{1,0:T(8,128)S(1)} %psum.38), channel_id=1, replica_groups=mesh['zh'=4,'zl'=4,'x'=4,'yh'=2,'yl'=2,'c'=2] {'zh'}, use_global_device_ids=true, to_apply=%region_4.5 | all-reduce | flops 2048 | bytes 16384 | tf_op jit(solution)/shard_map/psum | solution.py:470
  147.4 0.6 slice_bitcast_fusion.3
  147.9 0.1 fusion.4
  148.0 0.1 copy.18
  148.1 0.6 reshape.29
  148.7 0.6 fusion
  (4 shorter events, 0.1 us)
Async XLA Ops:
  0.6 6.9 %copy-start.4 = (f32[19,2,16,256]{3,2,1,0:T(8,128)S(1)}, f32[19,2,16,256]{3,2,1,0:T(8,128)}, u32[]{:S(2)}) copy-start(f32[19,2,16,256]{3,2,1,0:T(8,128)} %param.6) | copy-start | bytes 1867780
  1.9 5.7 %collective-permute-start = (f32[19,4,256]{2,1,0:T(4,128)S(1)}, f32[19,4,256]{2,1,0:T(4,128)S(1)}, u32[]{:S(2)}, u32[]{:S(2)}) collective-permute-start(f32[19,4,256]{2,1,0:T(4,128)S(1)} %reshape.26), channel_id=1, source_target_pairs={{0,1},{1,2},{2,3},{3,0},{4,5},{5,6},{6,7},{7,4},{8,9},{9,10},{10,1... | collective-permute-start | bytes 233480 | tf_op jit(solution)/shard_map/ppermute | solution.py:447
  3.9 5.6 %collective-permute-start.1 = (f32[19,4,256]{2,1,0:T(4,128)S(1)}, f32[19,4,256]{2,1,0:T(4,128)S(1)}, u32[]{:S(2)}, u32[]{:S(2)}) collective-permute-start(f32[19,4,256]{2,1,0:T(4,128)S(1)} %reshape.27), channel_id=1, source_target_pairs={{1,0},{2,1},{3,2},{0,3},{5,4},{6,5},{7,6},{4,7},{9,8},{10,9},{11,1... | collective-permute-start | bytes 233480 | tf_op jit(solution)/shard_map/ppermute | solution.py:448
  10.5 18.5 %copy-start.5 = (f32[32,19]{0,1:T(8,128)S(1)}, f32[32,19]{0,1:T(8,128)}, u32[]{:S(2)}) copy-start(f32[32,19]{0,1:T(8,128)} %param.10) | copy-start | bytes 7300
  10.5 24.2 %collective-permute-start.3 = (f32[19,40,256]{2,1,0:T(8,128)S(1)}, f32[19,40,256]{2,1,0:T(8,128)S(1)}, u32[]{:S(2)}, u32[]{:S(2)}) collective-permute-start(f32[19,40,256]{2,1,0:T(8,128)S(1)} %concatenate.9.own_ref), channel_id=1, source_target_pairs={{0,508},{4,8},{8,4},{12,16},{16,12},{20,24},{24,20},{28,32},{32,28... | collective-permute-start | bytes 2334728 | tf_op jit(solution)/shard_map/ppermute | solution.py:462
  13.7 44.3 %collective-permute-start.2 = (f32[19,40,256]{2,1,0:T(8,128)S(1)}, f32[19,40,256]{2,1,0:T(8,128)S(1)}, u32[]{:S(2)}, u32[]{:S(2)}) collective-permute-start(f32[19,40,256]{2,1,0:T(8,128)S(1)} %concatenate.9.own_ref), channel_id=1, source_target_pairs={{0,4},{4,0},{8,12},{12,8},{16,20},{20,16},{24,28},{28,24},{32,36},... | collective-permute-start | bytes 2334728 | tf_op jit(solution)/shard_map/ppermute | solution.py:463
  29.0 0.7 copy-start.2
  29.0 0.7 copy-start.1
  29.0 28.9 %copy-start = (f32[2,16,256]{2,1,0:T(8,128)S(1)}, f32[2,16,256]{2,1,0:T(8,128)}, u32[]{:S(2)}) copy-start(f32[2,16,256]{2,1,0:T(8,128)} %target_ref.1) | copy-start | bytes 98308
  58.0 0.7 copy-start.3

commit v2 on v1

--- a/solution.py
+++ b/solution.py
@@ -179,8 +179,8 @@
     parity_ref,
     bout_ref,
     own_ref,
+    b_ref,
     a_ref,
-    b_ref,
     target_ref,
     lin_ref,
     lint_ref,
@@ -251,7 +251,7 @@
             c1s[q, pl.ds(row + MARGIN, 8), :] = zroll(out[q], velocity_table[q][2])
         return 0
 
-    lax.fori_loop(0, G1, stage1, 0)
+    lax.fori_loop(0, G1, stage1, 0, unroll=True)
 
     def stage2(g, _):
         row = pl.multiple_of(g * 8 + B2, 8)
@@ -272,7 +272,7 @@
             c2s[q, pl.ds(row, 8), :] = zroll(out[q], velocity_table[q][2])
         return 0
 
-    lax.fori_loop(0, G2, stage2, 0)
+    lax.fori_loop(0, G2, stage2, 0, unroll=True)
 
     residual_scale = 1.0 / math.sqrt(256 * 64 * 256)
     for x in range(2):
@@ -345,7 +345,7 @@
             g1s[q, pl.ds(row + MARGIN, 8), :] = zroll(df, -velocity_table[q][2])
         return 0
 
-    lax.fori_loop(0, G2, stage4, 0)
+    lax.fori_loop(0, G2, stage4, 0, unroll=True)
 
     def stage5(g, _):
         row = pl.multiple_of(g * 8, 8)
@@ -353,7 +353,7 @@
         pull_params(gq, x1s, h1s, g)
         return 0
 
-    lax.fori_loop(0, G1, stage5, 0)
+    lax.fori_loop(0, G1, stage5, 0, unroll=True)
 
     hp = lax.Precision.HIGHEST
     rq = lax.broadcasted_iota(jnp.int32, (QS, HS), 0)
@@ -435,7 +435,13 @@
         ],
         compiler_params=pltpu.CompilerParams(vmem_limit_bytes=48 * 1024 * 1024),
         name="lattice",
-    )(parity, bias_out, own, a, b, target, *mats)
+    )(parity, bias_out, own, b, a, target, *mats)
+
+
+def gather_sum(x, axes):
+    peers = lax.axis_size(axes)
+    copies = jnp.broadcast_to(x[None], (peers,) + x.shape)
+    return jnp.sum(lax.all_to_all(copies, axes, 0, 0, tiled=True), axis=0)
 
 
 def body(populations, target_density, weight_in, bias_in, weight_out, bias_out):
@@ -459,14 +465,12 @@
     )
     pair = [(i, i ^ 1) for i in range(nx)]
     cross = [(i, (i + 1) % nx if i % 2 else (i - 1) % nx) for i in range(nx)]
+    a = lax.ppermute(own, gx, pair)
     b = lax.ppermute(own, gx, cross)
-    a = lax.ppermute(own, gx, pair)
     parity = (lax.axis_index("yh") % 2).astype(jnp.int32).reshape(1)
     moments, grads = main(parity, bias_out, own, a, b, target_density, mats)
-    grads = lax.psum(grads, ("yl", "c"))
-    grads = lax.psum(grads, "yh")
-    grads = lax.psum(grads, "x")
-    grads = lax.psum(grads, "zl")
+    grads = gather_sum(grads, ("yh", "yl", "c"))
+    grads = gather_sum(grads, ("zl", "x"))
     grads = lax.psum(grads, "zh")
     return (moments, *unpack(grads))
 

time: 150 us -> 121 us (0.81)
  the two profiles are of different devices: /device:TPU:16 before, /device:TPU:1 now
where the time goes in v2:
time: 121 us; the launch traced here: 119 us
  blocking collectives  43 us (36%)
  starting transfers between devices  27.3 us (23%)
  Pallas kernels  23.4 us (19%)
  waiting for transfers between devices  18.4 us (15%)
  local copies, waits for them, and re-layouts  5.05 us (4%)
    all_to_all x2, blocking collectives, gather_sum(): return jnp.sum(lax.all_to_all(copies, axes, 0, 0, tiled=True), axis=0)  26.4 us
    pallas_call x1, Pallas kernels, main(): pl.pallas_call(main_kernel, out_shape=(jax.ShapeDtypeStruct((4, 2, 16, NZ...  22.2 us
    ppermute x1, waiting for transfers between devices, body(): a = lax.ppermute(own, gx, pair)  17.6 us
    psum x1, blocking collectives, body(): grads = lax.psum(grads, 'zh')  16.7 us
    ppermute x1, starting transfers between devices, body(): b = lax.ppermute(own, gx, cross)  13.4 us
    ppermute x1, starting transfers between devices, body(): after = lax.ppermute(first, gy, [((j + 1) % ny, j) for j in range(ny)])  6.11 us
    ppermute x1, starting transfers between devices, body(): before = lax.ppermute(last, gy, [(j, (j + 1) % ny) for j in range(ny)])  4.59 us
    ppermute x1, starting transfers between devices, body(): a = lax.ppermute(own, gx, pair)  3.23 us
  transfers between devices with their start and end apart: 4, of which 2 were waited for; matrix products, arithmetic and copies ran while one was open for 0% of the time, Pallas kernels for 1%

profile of v2, /device:TPU:1, one launch (start us, length us, event | category | flops | bytes accessed | tf_op | source)
XLA Modules:
  0.0 118.6 jit_solution(18008090833660392665)
XLA Ops:
  0.6 0.0 copy-start.4
  0.6 1.2 %fusion.1 = (f32[19,2,2,256]{3,2,1,0:T(2,128)S(1)}, f32[19,2,2,256]{3,2,1,0:T(2,128)S(1)}) fusion(f32[19,2,16,256]{3,2,1,0:T(8,128)} %param.6), kind=kLoop, calls=%fused_computation.7 | loop fusion | bytes 311296 | tf_op jit(solution)/shard_map/slice | solution.py:452
  1.8 0.1 reshape.28
  1.9 4.6 %collective-permute-start = (f32[19,4,256]{2,1,0:T(4,128)S(1)}, f32[19,4,256]{2,1,0:T(4,128)S(1)}, u32[]{:S(2)}, u32[]{:S(2)}) collective-permute-start(f32[19,4,256]{2,1,0:T(4,128)S(1)} %reshape.28), channel_id=1, source_target_pairs={{0,1},{1,2},{2,3},{3,0},{4,5},{5,6},{6,7},{7,4},{8,9},{9,10},{10,1... | collective-permute-start | bytes 233480 | tf_op jit(solution)/shard_map/ppermute | solution.py:453
  6.5 0.1 reshape.29
  6.6 6.1 %collective-permute-start.1 = (f32[19,4,256]{2,1,0:T(4,128)S(1)}, f32[19,4,256]{2,1,0:T(4,128)S(1)}, u32[]{:S(2)}, u32[]{:S(2)}) collective-permute-start(f32[19,4,256]{2,1,0:T(4,128)S(1)} %reshape.29), channel_id=1, source_target_pairs={{1,0},{2,1},{3,2},{0,3},{5,4},{6,5},{7,6},{4,7},{9,8},{10,9},{11,1... | collective-permute-start | bytes 233480 | tf_op jit(solution)/shard_map/ppermute | solution.py:454
  12.7 0.0 copy-done.4
  12.8 0.0 collective-permute-done
  12.8 0.8 collective-permute-done.1
  13.6 0.9 concatenate.9.own_ref
  14.5 0.0 copy-start.5
  14.6 3.2 %collective-permute-start.3 = (f32[19,40,256]{2,1,0:T(8,128)S(1)}, f32[19,40,256]{2,1,0:T(8,128)S(1)}, u32[]{:S(2)}, u32[]{:S(2)}) collective-permute-start(f32[19,40,256]{2,1,0:T(8,128)S(1)} %concatenate.9.own_ref), channel_id=1, source_target_pairs={{0,4},{4,0},{8,12},{12,8},{16,20},{20,16},{24,28},{28,24},{32,36},... | collective-permute-start | bytes 2334728 | tf_op jit(solution)/shard_map/ppermute | solution.py:468
  17.8 13.4 %collective-permute-start.2 = (f32[19,40,256]{2,1,0:T(8,128)S(1)}, f32[19,40,256]{2,1,0:T(8,128)S(1)}, u32[]{:S(2)}, u32[]{:S(2)}) collective-permute-start(f32[19,40,256]{2,1,0:T(8,128)S(1)} %concatenate.9.own_ref), channel_id=1, source_target_pairs={{0,508},{4,8},{8,4},{12,16},{16,12},{20,24},{24,20},{28,32},{32,28... | collective-permute-start | bytes 2334728 | tf_op jit(solution)/shard_map/ppermute | solution.py:469
  31.2 0.0 copy-start.2
  31.2 0.0 copy-start.1
  31.2 0.0 copy-done.5
  31.2 0.0 copy-start
  31.2 0.1 copy.21.wout_ref
  31.3 0.5 copy-done.2
  31.9 0.1 copy-done.1
  31.9 1.2 prep.1
  33.1 17.6 %collective-permute-done.3.a_ref = f32[19,40,256]{2,1,0:T(8,128)S(1)} collective-permute-done((f32[19,40,256]{2,1,0:T(8,128)S(1)}, f32[19,40,256]{2,1,0:T(8,128)S(1)}, u32[]{:S(2)}, u32[]{:S(2)}) %collective-permute-start.3) | collective-permute-done | bytes 778272 | tf_op jit(solution)/shard_map/ppermute | solution.py:468
  50.7 0.0 collective-permute-done.2.b_ref
  50.7 0.0 copy-start.3
  50.7 0.0 copy-done
  50.7 0.6 copy-done.3
  51.3 22.2 %lattice.1 = (f32[4,2,16,256]{3,2,1,0:T(8,128)}, f32[16,128]{1,0:T(8,128)S(1)}) custom-call(s32[1]{0:T(128)} %bitcast.parity_ref, f32[19]{0:T(128)S(1)} %copy-done.3, f32[19,40,256]{2,1,0:T(8,128)S(1)} %concatenate.9.own_ref, f32[19,40,256]{2,1,0:T(8,128)S(1)} %collective-permute-done.2.b_ref, f32[19,40,256]{2,1,0:T(8,128)S(1)} %collective-permute-done.3.a_ref, ...), custom_call_target="tpu_custom_call" | custom-call | tf_op jit(solution)/shard_map/lattice/pallas_call | solution.py:412
  73.6 11.5 %all_to_all.10 = f32[8,16,128]{2,1,0:T(8,128)S(1)} all-to-all(f32[8,16,128]{2,1,0:T(8,128)S(1)} %broadcast_in_dim.4), channel_id=1, replica_groups=mesh['zh'=4,'zl'=4,'x'=4,'yh'=2,'yl'=2,'c'=2] {'yh','yl','c'}, dimensions={0} | all-to-all | bytes 131072 | tf_op jit(solution)/shard_map/all_to_all | solution.py:444
  85.2 14.8 %all_to_all.11 = f32[16,16,128]{2,1,0:T(8,128)S(1)} all-to-all(f32[16,16,128]{2,1,0:T(8,128)S(1)} %broadcast_in_dim.5), channel_id=1, replica_groups=mesh['zh'=4,'zl'=4,'x'=4,'yh'=2,'yl'=2,'c'=2] {'zl','x'}, dimensions={0} | all-to-all | bytes 262144 | tf_op jit(solution)/shard_map/all_to_all | solution.py:444
  100.0 16.7 %psum.7 = f32[16,128]{1,0:T(8,128)S(1)} all-reduce(f32[16,128]{1,0:T(8,128)S(1)} %reduce_sum.19), channel_id=1, replica_groups=mesh['zh'=4,'zl'=4,'x'=4,'yh'=2,'yl'=2,'c'=2] {'zh'}, use_global_device_ids=true, to_apply=%region_2.3 | all-reduce | flops 2048 | bytes 16384 | tf_op jit(solution)/shard_map/psum | solution.py:474
  116.7 0.6 slice_bitcast_fusion.3
  117.3 0.1 fusion.4
  117.3 0.1 copy.22
  117.4 0.6 reshape.31
  118.0 0.6 fusion
  (8 shorter events, 0.2 us)
Async XLA Ops:
  0.6 12.1 %copy-start.4 = (f32[19,2,16,256]{3,2,1,0:T(8,128)S(1)}, f32[19,2,16,256]{3,2,1,0:T(8,128)}, u32[]{:S(2)}) copy-start(f32[19,2,16,256]{3,2,1,0:T(8,128)} %param.6) | copy-start | bytes 1867780
  1.9 10.9 %collective-permute-start = (f32[19,4,256]{2,1,0:T(4,128)S(1)}, f32[19,4,256]{2,1,0:T(4,128)S(1)}, u32[]{:S(2)}, u32[]{:S(2)}) collective-permute-start(f32[19,4,256]{2,1,0:T(4,128)S(1)} %reshape.28), channel_id=1, source_target_pairs={{0,1},{1,2},{2,3},{3,0},{4,5},{5,6},{6,7},{7,4},{8,9},{9,10},{10,1... | collective-permute-start | bytes 233480 | tf_op jit(solution)/shard_map/ppermute | solution.py:453
  6.6 7.0 %collective-permute-start.1 = (f32[19,4,256]{2,1,0:T(4,128)S(1)}, f32[19,4,256]{2,1,0:T(4,128)S(1)}, u32[]{:S(2)}, u32[]{:S(2)}) collective-permute-start(f32[19,4,256]{2,1,0:T(4,128)S(1)} %reshape.29), channel_id=1, source_target_pairs={{1,0},{2,1},{3,2},{0,3},{5,4},{6,5},{7,6},{4,7},{9,8},{10,9},{11,1... | collective-permute-start | bytes 233480 | tf_op jit(solution)/shard_map/ppermute | solution.py:454
  14.5 16.7 %copy-start.5 = (f32[32,19]{0,1:T(8,128)S(1)}, f32[32,19]{0,1:T(8,128)}, u32[]{:S(2)}) copy-start(f32[32,19]{0,1:T(8,128)} %param.10) | copy-start | bytes 7300
  14.6 36.1 %collective-permute-start.3 = (f32[19,40,256]{2,1,0:T(8,128)S(1)}, f32[19,40,256]{2,1,0:T(8,128)S(1)}, u32[]{:S(2)}, u32[]{:S(2)}) collective-permute-start(f32[19,40,256]{2,1,0:T(8,128)S(1)} %concatenate.9.own_ref), channel_id=1, source_target_pairs={{0,4},{4,0},{8,12},{12,8},{16,20},{20,16},{24,28},{28,24},{32,36},... | collective-permute-start | bytes 2334728 | tf_op jit(solution)/shard_map/ppermute | solution.py:468
  17.8 32.9 %collective-permute-start.2 = (f32[19,40,256]{2,1,0:T(8,128)S(1)}, f32[19,40,256]{2,1,0:T(8,128)S(1)}, u32[]{:S(2)}, u32[]{:S(2)}) collective-permute-start(f32[19,40,256]{2,1,0:T(8,128)S(1)} %concatenate.9.own_ref), channel_id=1, source_target_pairs={{0,508},{4,8},{8,4},{12,16},{16,12},{20,24},{24,20},{28,32},{32,28... | collective-permute-start | bytes 2334728 | tf_op jit(solution)/shard_map/ppermute | solution.py:469
  31.2 0.7 copy-start.2
  31.2 0.7 copy-start.1
  31.2 19.4 %copy-start = (f32[2,16,256]{2,1,0:T(8,128)S(1)}, f32[2,16,256]{2,1,0:T(8,128)}, u32[]{:S(2)}) copy-start(f32[2,16,256]{2,1,0:T(8,128)} %target_ref.1) | copy-start | bytes 98308
  50.7 0.7 copy-start.3

commit v3 on v2

--- a/solution.py
+++ b/solution.py
@@ -36,21 +36,24 @@
 Q = 19
 H = 32
 NZ = 256
-YW = 20
-ROWS = 6 * YW
-G1 = ROWS // 8
-B2 = 16
-G2 = 11
-MARGIN = 24
+W1 = 20
+W2 = 18
+G1 = 2 * W1 // 8
+G2 = 4 * W2 // 8
+PG = (2, 7)
+MARGIN = 8
 SP = 8
 QS = 20 * SP
 HS = H * SP
+MSG = 344
 F32 = jnp.float32
 BF16 = jnp.bfloat16
-
-
-def row_shift(q):
-    return YW * velocity_table[q][0] + velocity_table[q][1]
+MIB = 1024 * 1024
+
+to_right = [(q, -1) for q in range(19) if velocity_table[q][0] >= 0]
+to_right += [(q, 0) for q in range(19) if velocity_table[q][0] == 1]
+to_left = [(q, 2) for q in range(19) if velocity_table[q][0] <= 0]
+to_left += [(q, 1) for q in range(19) if velocity_table[q][0] == -1]
 
 
 def split(x):
@@ -175,130 +178,168 @@
     return pltpu.roll(x, step % NZ, 1)
 
 
-def main_kernel(
+def first_kernel(
     parity_ref,
     bout_ref,
-    own_ref,
-    b_ref,
-    a_ref,
+    pop_ref,
+    before_ref,
+    after_ref,
+    lin_ref,
+    lout_ref,
+    msg_a_ref,
+    msg_b_ref,
+    c1_ref,
+    x1_ref,
+    h1_ref,
+    fs,
+):
+    for x in range(2):
+        fs[:, W1 * x : W1 * x + 2, :] = before_ref[:, 2 * x : 2 * x + 2, :]
+        fs[:, W1 * x + 2 : W1 * x + 18, :] = pop_ref[:, x]
+        fs[:, W1 * x + 18 : W1 * x + 20, :] = after_ref[:, 2 * x : 2 * x + 2, :]
+    for g in range(G1):
+        f = [fs[q, 8 * g : 8 * g + 8, :] for q in range(Q)]
+
+        def save_x(hi, lo):
+            x1_ref[g, 0:QS, :] = hi
+            x1_ref[g, QS : 2 * QS, :] = lo
+
+        def save_h(hi, lo):
+            h1_ref[g, 0:HS, :] = hi
+            h1_ref[g, HS : 2 * HS, :] = lo
+
+        out, _m = collide(f, lin_ref, lout_ref, bout_ref, save_x, save_h)
+        for q in range(Q):
+            c1_ref[q, 8 * g : 8 * g + 8, :] = zroll(out[q], velocity_table[q][2])
+    odd = parity_ref[0] == 1
+
+    def piece(q, plane):
+        start = W1 * (plane - velocity_table[q][0]) + 1 - velocity_table[q][1]
+        return c1_ref[q, start : start + W2, :]
+
+    for k in range(Q):
+        q, plane = to_right[k]
+        right = piece(q, plane + 2)
+        q, plane = to_left[k]
+        left = piece(q, plane - 2)
+        msg_a_ref[W2 * k : W2 * k + W2, :] = jnp.where(odd, left, right)
+        msg_b_ref[W2 * k : W2 * k + W2, :] = jnp.where(odd, right, left)
+    msg_a_ref[W2 * Q :, :] = jnp.zeros((MSG - W2 * Q, NZ), F32)
+    msg_b_ref[W2 * Q :, :] = jnp.zeros((MSG - W2 * Q, NZ), F32)
+
+
+def second_kernel(
+    parity_ref,
+    bout_ref,
+    c1_ref,
+    msg_a_ref,
+    msg_b_ref,
     target_ref,
     lin_ref,
-    lint_ref,
     lout_ref,
-    loutt_ref,
     moments_ref,
-    grads_ref,
-    fs,
-    c1s,
-    c2s,
-    g1s,
-    rs,
-    x1s,
-    h1s,
-    x2s,
-    h2s,
-    m2s,
-    acc_in,
-    acc_out,
-    acc_b,
-    sems,
+    r_ref,
+    x2_ref,
+    h2_ref,
+    m2_ref,
+    a1,
+    c2,
 ):
-    parity = parity_ref[0]
-    a_row = pl.multiple_of(80 * (1 - parity), 8)
-    b_row = pl.multiple_of(80 * parity, 8)
-    copies = [
-        pltpu.make_async_copy(own_ref, fs.at[:, 40:80, :], sems.at[0]),
-        pltpu.make_async_copy(a_ref, fs.at[:, pl.ds(a_row, 40), :], sems.at[1]),
-        pltpu.make_async_copy(b_ref, fs.at[:, pl.ds(b_row, 40), :], sems.at[2]),
-    ]
-    for c in copies:
-        c.start()
-    acc_in[...] = jnp.zeros_like(acc_in)
-    acc_out[...] = jnp.zeros_like(acc_out)
-    acc_b[...] = jnp.zeros_like(acc_b)
-    rs[...] = jnp.zeros_like(rs)
-    zero_top = jnp.zeros((Q, MARGIN, NZ), F32)
-    c1s[:, 0:MARGIN, :] = zero_top
-    c1s[:, MARGIN + ROWS :, :] = zero_top
-    g1s[:, 0 : MARGIN + B2, :] = jnp.zeros((Q, MARGIN + B2, NZ), F32)
-    g1s[:, MARGIN + B2 + 8 * G2 :, :] = jnp.zeros((Q, MARGIN + ROWS - B2 - 8 * G2, NZ), F32)
-    for c in copies:
-        c.wait()
-
-    def load(ref, q, row, off):
-        base = (off // 8) * 8
-        rem = off % 8
-        start = pl.multiple_of(row + base, 8)
-        if rem == 0:
-            return ref[q, pl.ds(start, 8), :]
-        both = ref[q, pl.ds(start, 16), :]
-        return both[rem : rem + 8, :]
-
-    def stage1(g, _):
-        row = pl.multiple_of(g * 8, 8)
-        f = [fs[q, pl.ds(row, 8), :] for q in range(Q)]
+    odd = parity_ref[0] == 1
+    for k in range(Q):
+        rows = slice(W2 * k, W2 * k + W2)
+        msg_a = msg_a_ref[rows, :]
+        msg_b = msg_b_ref[rows, :]
+        q, plane = to_right[k]
+        a1[q, W2 * (plane + 1) : W2 * (plane + 2), :] = jnp.where(odd, msg_a, msg_b)
+        q, plane = to_left[k]
+        a1[q, W2 * (plane + 1) : W2 * (plane + 2), :] = jnp.where(odd, msg_b, msg_a)
+    for q in range(Q):
+        for plane in range(-1, 3):
+            source = plane - velocity_table[q][0]
+            if source in (0, 1):
+                start = W1 * source + 1 - velocity_table[q][1]
+                a1[q, W2 * (plane + 1) : W2 * (plane + 2), :] = c1_ref[q, start : start + W2, :]
+    for g in range(G2):
+        f = [a1[q, 8 * g : 8 * g + 8, :] for q in range(Q)]
 
         def save_x(hi, lo):
-            x1s[g, 0:QS, :] = hi
-            x1s[g, QS : 2 * QS, :] = lo
+            if PG[0] <= g < PG[1]:
+                x2_ref[g - PG[0], 0:QS, :] = hi
+                x2_ref[g - PG[0], QS : 2 * QS, :] = lo
 
         def save_h(hi, lo):
-            h1s[g, 0:HS, :] = hi
-            h1s[g, HS : 2 * HS, :] = lo
-
-        out, _m = collide(f, lin_ref, lout_ref, bout_ref, save_x, save_h)
-        for q in range(Q):
-            c1s[q, pl.ds(row + MARGIN, 8), :] = zroll(out[q], velocity_table[q][2])
-        return 0
-
-    lax.fori_loop(0, G1, stage1, 0, unroll=True)
-
-    def stage2(g, _):
-        row = pl.multiple_of(g * 8 + B2, 8)
-        f = [load(c1s, q, row, MARGIN - row_shift(q)) for q in range(Q)]
-
-        def save_x(hi, lo):
-            x2s[g, 0:QS, :] = hi
-            x2s[g, QS : 2 * QS, :] = lo
-
-        def save_h(hi, lo):
-            h2s[g, 0:HS, :] = hi
-            h2s[g, HS : 2 * HS, :] = lo
+            h2_ref[g, 0:HS, :] = hi
+            h2_ref[g, HS : 2 * HS, :] = lo
 
         out, m = collide(f, lin_ref, lout_ref, bout_ref, save_x, save_h)
         for a in range(3):
-            m2s[g, a] = m[a]
+            m2_ref[g, a] = m[a]
         for q in range(Q):
-            c2s[q, pl.ds(row, 8), :] = zroll(out[q], velocity_table[q][2])
-        return 0
-
-    lax.fori_loop(0, G2, stage2, 0, unroll=True)
-
+            c2[q, 8 * g : 8 * g + 8, :] = zroll(out[q], velocity_table[q][2])
     residual_scale = 1.0 / math.sqrt(256 * 64 * 256)
     for x in range(2):
         for half in range(2):
-            first = YW * (x + 2) + 2 + 8 * half
-            f = [c2s[q, first - row_shift(q) : first - row_shift(q) + 8, :] for q in range(Q)]
+            first = W2 * (x + 1) + 1 + 8 * half
+            f = []
+            for q in range(Q):
+                start = first - W2 * velocity_table[q][0] - velocity_table[q][1]
+                f.append(c2[q, start : start + 8, :])
             density, m = equilibrium_parts(f)
             moments_ref[0, x, 8 * half : 8 * half + 8, :] = density
             for a in range(3):
                 moments_ref[a + 1, x, 8 * half : 8 * half + 8, :] = m[a]
             r = (density - target_ref[x, 8 * half : 8 * half + 8, :]) * residual_scale
-            rs[0, MARGIN + first : MARGIN + first + 8, :] = r
-            rs[1, MARGIN + first : MARGIN + first + 8, :] = zroll(r, -1)
-            rs[2, MARGIN + first : MARGIN + first + 8, :] = zroll(r, 1)
-
-    def pull_params(gq, x_hl, h_hl, g):
+            r_ref[16 * x + 8 * half : 16 * x + 8 * half + 8, :] = r
+
+
+def third_kernel(
+    parity_ref,
+    r_ref,
+    r_b_ref,
+    r_a_ref,
+    x1_ref,
+    h1_ref,
+    x2_ref,
+    h2_ref,
+    m2_ref,
+    lint_ref,
+    loutt_ref,
+    grads_ref,
+    rs,
+    g1s,
+    acc_in,
+    acc_out,
+    acc_b,
+):
+    odd = parity_ref[0] == 1
+    rs[...] = jnp.zeros_like(rs)
+    g1s[...] = jnp.zeros_like(g1s)
+    acc_in[...] = jnp.zeros_like(acc_in)
+    acc_out[...] = jnp.zeros_like(acc_out)
+    acc_b[...] = jnp.zeros_like(acc_b)
+    r_a, r_b = r_a_ref[...], r_b_ref[...]
+    parts = (jnp.where(odd, r_a, r_b), r_ref[...], jnp.where(odd, r_b, r_a))
+    for i in range(6):
+        first = MARGIN + W2 * i + 1
+        for half in range(2):
+            at = 16 * (i % 2) + 8 * half
+            r = parts[i // 2][at : at + 8, :]
+            rows = slice(first + 8 * half, first + 8 * half + 8)
+            rs[0, rows, :] = r
+            rs[1, rows, :] = zroll(r, -1)
+            rs[2, rows, :] = zroll(r, 1)
+
+    def hidden_pull(gq, hhi, hlo):
         gs = jnp.concatenate(gq + [jnp.zeros((SP, NZ), F32)], axis=0)
         ghi, glo = split(gs)
         dh = mm(loutt_ref[...], jnp.concatenate([ghi, glo, ghi], axis=0))
-        hhi = h_hl[g, 0:HS, :]
-        hlo = h_hl[g, HS : 2 * HS, :]
         hid = hhi.astype(F32) + hlo.astype(F32)
-        dpre = dh * (1.0 - hid * hid)
+        return gs, dh * (1.0 - hid * hid)
+
+    def add_params(gs, dpre, xhi, xlo, hhi, hlo):
+        ghi, glo = split(gs)
         dhi, dlo = split(dpre)
-        xhi = x_hl[g, 0:QS, :]
-        xlo = x_hl[g, QS : 2 * QS, :]
         acc_in[...] += mm_nt(
             jnp.concatenate([xhi, xlo, xhi], axis=1), jnp.concatenate([dhi, dhi, dlo], axis=1)
         )
@@ -306,17 +347,36 @@
             jnp.concatenate([ghi, glo, ghi], axis=1), jnp.concatenate([hhi, hhi, hlo], axis=1)
         )
         acc_b[...] += gs
-        return dhi, dlo
-
-    def stage4(g, _):
-        row = pl.multiple_of(g * 8 + B2, 8)
+
+    def keep(x, lo, hi):
+        if lo == 0 and hi == SP:
+            return x
+        row = lax.broadcasted_iota(jnp.int32, x.shape, 0) % SP
+        return jnp.where((row >= lo) & (row < hi), x, 0.0)
+
+    for g in range(G2):
         gq = []
         for q in range(Q):
-            cz = velocity_table[q][2]
-            gq.append(load(rs, {0: 0, 1: 1, -1: 2}[cz], row, MARGIN + row_shift(q)))
-        dhi, dlo = pull_params(gq, x2s, h2s, g)
+            cx, cy, cz = velocity_table[q]
+            start = MARGIN + W2 + 8 * g + W2 * cx + cy
+            gq.append(rs[{0: 0, 1: 1, -1: 2}[cz], start : start + 8, :])
+        hhi = h2_ref[g, 0:HS, :]
+        hlo = h2_ref[g, HS : 2 * HS, :]
+        gs, dpre = hidden_pull(gq, hhi, hlo)
+        if PG[0] <= g < PG[1]:
+            lo = max(W2 - 8 * g, 0)
+            hi = min(3 * W2 - 8 * g, SP)
+            add_params(
+                keep(gs, lo, hi),
+                keep(dpre, lo, hi),
+                x2_ref[g - PG[0], 0:QS, :],
+                x2_ref[g - PG[0], QS : 2 * QS, :],
+                hhi,
+                hlo,
+            )
+        dhi, dlo = split(dpre)
         back = mm(lint_ref[...], jnp.concatenate([dhi, dlo, dhi], axis=0))
-        m = [m2s[g, a] for a in range(3)]
+        m = [m2_ref[g, a] for a in range(3)]
         de = [rows8(back, q) - gq[q] * (1.0 / relax_time) for q in range(Q)]
         t = [lattice_weights[q] * de[q] for q in range(Q)]
         drho = t[0]
@@ -342,18 +402,24 @@
             df = gq[q] + de[q] - drho
             if q:
                 df = df - project(q, dm)
-            g1s[q, pl.ds(row + MARGIN, 8), :] = zroll(df, -velocity_table[q][2])
-        return 0
-
-    lax.fori_loop(0, G2, stage4, 0, unroll=True)
-
-    def stage5(g, _):
-        row = pl.multiple_of(g * 8, 8)
-        gq = [load(g1s, q, row, MARGIN + row_shift(q)) for q in range(Q)]
-        pull_params(gq, x1s, h1s, g)
-        return 0
-
-    lax.fori_loop(0, G1, stage5, 0, unroll=True)
+            df = zroll(df, -velocity_table[q][2])
+            for plane in range(4):
+                lo = max(W2 * plane, 8 * g)
+                hi = min(W2 * plane + W2, 8 * g + 8)
+                if lo < hi:
+                    at = MARGIN + 1 + 2 * plane
+                    g1s[q, at + lo : at + hi, :] = df[lo - 8 * g : hi - 8 * g, :]
+
+    for g in range(G1):
+        gq = []
+        for q in range(Q):
+            cx, cy, _cz = velocity_table[q]
+            start = MARGIN + W1 + 8 * g + W1 * cx + cy
+            gq.append(g1s[q, start : start + 8, :])
+        hhi = h1_ref[g, 0:HS, :]
+        hlo = h1_ref[g, HS : 2 * HS, :]
+        gs, dpre = hidden_pull(gq, hhi, hlo)
+        add_params(gs, dpre, x1_ref[g, 0:QS, :], x1_ref[g, QS : 2 * QS, :], hhi, hlo)
 
     hp = lax.Precision.HIGHEST
     rq = lax.broadcasted_iota(jnp.int32, (QS, HS), 0)
@@ -404,38 +470,66 @@
     )(weight_in, bias_in.reshape(1, H), weight_out)
 
 
-def main(parity, bias_out, own, a, b, target, mats):
-    vmem = pl.BlockSpec(memory_space=pltpu.VMEM)
-    smem = pl.BlockSpec(memory_space=pltpu.SMEM)
-    anym = pl.BlockSpec(memory_space=pl.ANY)
-    span = 2 * MARGIN + ROWS
+VMEM = pl.BlockSpec(memory_space=pltpu.VMEM)
+SMEM = pl.BlockSpec(memory_space=pltpu.SMEM)
+
+
+def shape(*dims, kind=F32):
+    return jax.ShapeDtypeStruct(dims, kind)
+
+
+def first(parity, bias_out, populations, before, after, lin, lout):
     return pl.pallas_call(
-        main_kernel,
+        first_kernel,
         out_shape=(
-            jax.ShapeDtypeStruct((4, 2, 16, NZ), F32),
-            jax.ShapeDtypeStruct((16, 128), F32),
+            shape(MSG, NZ),
+            shape(MSG, NZ),
+            shape(Q, 2 * W1, NZ),
+            shape(G1, 2 * QS, NZ, kind=BF16),
+            shape(G1, 2 * HS, NZ, kind=BF16),
         ),
-        in_specs=[smem, smem, anym, anym, anym, vmem, vmem, vmem, vmem, vmem],
-        out_specs=(vmem, vmem),
+        in_specs=[SMEM, SMEM] + [VMEM] * 5,
+        out_specs=(VMEM,) * 5,
+        scratch_shapes=[pltpu.VMEM((Q, 2 * W1, NZ), F32)],
+        compiler_params=pltpu.CompilerParams(vmem_limit_bytes=24 * MIB),
+        name="first",
+    )(parity, bias_out, populations, before, after, lin, lout)
+
+
+def second(parity, bias_out, c1, msg_a, msg_b, target, lin, lout):
+    return pl.pallas_call(
+        second_kernel,
+        out_shape=(
+            shape(4, 2, 16, NZ),
+            shape(32, NZ),
+            shape(PG[1] - PG[0], 2 * QS, NZ, kind=BF16),
+            shape(G2, 2 * HS, NZ, kind=BF16),
+            shape(G2, 3, SP, NZ),
+        ),
+        in_specs=[SMEM, SMEM] + [VMEM] * 6,
+        out_specs=(VMEM,) * 5,
+        scratch_shapes=[pltpu.VMEM((Q, 4 * W2, NZ), F32)] * 2,
+        compiler_params=pltpu.CompilerParams(vmem_limit_bytes=24 * MIB),
+        name="second",
+    )(parity, bias_out, c1, msg_a, msg_b, target, lin, lout)
+
+
+def third(parity, r, r_b, r_a, x1, h1, x2, h2, m2, lint, loutt):
+    return pl.pallas_call(
+        third_kernel,
+        out_shape=shape(16, 128),
+        in_specs=[SMEM] + [VMEM] * 10,
+        out_specs=VMEM,
         scratch_shapes=[
-            pltpu.VMEM((Q, ROWS, NZ), F32),
-            pltpu.VMEM((Q, span, NZ), F32),
-            pltpu.VMEM((Q, ROWS, NZ), F32),
-            pltpu.VMEM((Q, span, NZ), F32),
-            pltpu.VMEM((3, span, NZ), F32),
-            pltpu.VMEM((G1, 2 * QS, NZ), BF16),
-            pltpu.VMEM((G1, 2 * HS, NZ), BF16),
-            pltpu.VMEM((G2, 2 * QS, NZ), BF16),
-            pltpu.VMEM((G2, 2 * HS, NZ), BF16),
-            pltpu.VMEM((G2, 3, SP, NZ), F32),
+            pltpu.VMEM((3, 2 * MARGIN + 6 * W2 + 4, NZ), F32),
+            pltpu.VMEM((Q, 2 * MARGIN + 4 * W1, NZ), F32),
             pltpu.VMEM((QS, HS), F32),
             pltpu.VMEM((QS, HS), F32),
             pltpu.VMEM((QS, NZ), F32),
-            pltpu.SemaphoreType.DMA((3,)),
         ],
-        compiler_params=pltpu.CompilerParams(vmem_limit_bytes=48 * 1024 * 1024),
-        name="lattice",
-    )(parity, bias_out, own, b, a, target, *mats)
+        compiler_params=pltpu.CompilerParams(vmem_limit_bytes=24 * MIB),
+        name="third",
+    )(parity, r, r_b, r_a, x1, h1, x2, h2, m2, lint, loutt)
 
 
 def gather_sum(x, axes):
@@ -447,28 +541,23 @@
 def body(populations, target_density, weight_in, bias_in, weight_out, bias_out):
     gx, gy = ("zh", "zl", "x", "yh"), ("yl", "c")
     nx, ny = lax.axis_size(gx), lax.axis_size(gy)
-    mats = prep(weight_in, bias_in, weight_out)
+    lin, lint, lout, loutt = prep(weight_in, bias_in, weight_out)
     last = populations[:, :, 14:16, :].reshape(Q, 4, NZ)
-    first = populations[:, :, 0:2, :].reshape(Q, 4, NZ)
+    start = populations[:, :, 0:2, :].reshape(Q, 4, NZ)
     before = lax.ppermute(last, gy, [(j, (j + 1) % ny) for j in range(ny)])
-    after = lax.ppermute(first, gy, [((j + 1) % ny, j) for j in range(ny)])
-    own = jnp.concatenate(
-        [
-            before[:, 0:2],
-            populations[:, 0],
-            after[:, 0:2],
-            before[:, 2:4],
-            populations[:, 1],
-            after[:, 2:4],
-        ],
-        axis=1,
-    )
+    after = lax.ppermute(start, gy, [((j + 1) % ny, j) for j in range(ny)])
     pair = [(i, i ^ 1) for i in range(nx)]
     cross = [(i, (i + 1) % nx if i % 2 else (i - 1) % nx) for i in range(nx)]
-    a = lax.ppermute(own, gx, pair)
-    b = lax.ppermute(own, gx, cross)
     parity = (lax.axis_index("yh") % 2).astype(jnp.int32).reshape(1)
-    moments, grads = main(parity, bias_out, own, a, b, target_density, mats)
+    msg_a, msg_b, c1, x1, h1 = first(parity, bias_out, populations, before, after, lin, lout)
+    got_a = lax.ppermute(msg_a, gx, pair)
+    got_b = lax.ppermute(msg_b, gx, cross)
+    moments, r, x2, h2, m2 = second(
+        parity, bias_out, c1, got_a, got_b, target_density, lin, lout
+    )
+    r_a = lax.ppermute(r, gx, pair)
+    r_b = lax.ppermute(r, gx, cross)
+    grads = third(parity, r, r_b, r_a, x1, h1, x2, h2, m2, lint, loutt)
     grads = gather_sum(grads, ("yh", "yl", "c"))
     grads = gather_sum(grads, ("zl", "x"))
     grads = lax.psum(grads, "zh")

time: 121 us -> 110 us (0.909)
  the two profiles are of different devices: /device:TPU:1 before, /device:TPU:2 now
where the time goes in v3:
time: 110 us
  blocking collectives  43.7 us (40%)
  starting transfers between devices  31.1 us (28%)
  Pallas kernels  15.4 us (14%)
  waiting for transfers between devices  10.7 us (10%)
  local copies, waits for them, and re-layouts  7.26 us (7%)
    all_to_all x2, blocking collectives, gather_sum(): return jnp.sum(lax.all_to_all(copies, axes, 0, 0, tiled=True), axis=0)  25 us
    psum x1, blocking collectives, body(): grads = lax.psum(grads, 'zh')  18.7 us
    ppermute x1, waiting for transfers between devices, body(): got_a = lax.ppermute(msg_a, gx, pair)  8.77 us
    ppermute x1, starting transfers between devices, body(): r_b = lax.ppermute(r, gx, cross)  8.01 us
    ppermute x1, starting transfers between devices, body(): got_b = lax.ppermute(msg_b, gx, cross)  7.59 us
    pallas_call x1, Pallas kernels, third(): pl.pallas_call(third_kernel, out_shape=shape(16, 128), in_specs=[SMEM] +...  6.22 us
    pallas_call x1, Pallas kernels, second(): pl.pallas_call(second_kernel, out_shape=(shape(4, 2, 16, NZ), shape(32, N...  5.15 us
    ppermute x1, starting transfers between devices, body(): got_a = lax.ppermute(msg_a, gx, pair)  5.11 us
  transfers between devices with their start and end apart: 6, of which 2 were waited for; matrix products, arithmetic and copies ran while one was open for 1% of the time, Pallas kernels for 1%

profile of v3, /device:TPU:2, one launch (start us, length us, event | category | flops | bytes accessed | tf_op | source)
XLA Modules:
  0.0 109.5 jit_solution(3642055033292851125)
XLA Ops:
  0.6 1.1 %fusion.1 = (f32[19,2,2,256]{3,2,1,0:T(2,128)S(1)}, f32[19,2,2,256]{3,2,1,0:T(2,128)S(1)}) fusion(f32[19,2,16,256]{3,2,1,0:T(8,128)} %pop_ref.1), kind=kLoop, calls=%fused_computation.5 | loop fusion | bytes 311296 | tf_op jit(solution)/shard_map/slice | solution.py:546
  1.8 0.1 reshape.28
  1.8 1.9 %collective-permute-start = (f32[19,4,256]{2,1,0:T(4,128)S(1)}, f32[19,4,256]{2,1,0:T(4,128)S(1)}, u32[]{:S(2)}, u32[]{:S(2)}) collective-permute-start(f32[19,4,256]{2,1,0:T(4,128)S(1)} %reshape.28), channel_id=1, source_target_pairs={{0,1},{1,2},{2,3},{3,0},{4,5},{5,6},{6,7},{7,4},{8,9},{9,10},{10,1... | collective-permute-start | bytes 233480 | tf_op jit(solution)/shard_map/ppermute | solution.py:547
  3.8 0.1 reshape.29
  3.8 3.6 %collective-permute-start.1 = (f32[19,4,256]{2,1,0:T(4,128)S(1)}, f32[19,4,256]{2,1,0:T(4,128)S(1)}, u32[]{:S(2)}, u32[]{:S(2)}) collective-permute-start(f32[19,4,256]{2,1,0:T(4,128)S(1)} %reshape.29), channel_id=1, source_target_pairs={{1,0},{2,1},{3,2},{0,3},{5,4},{6,5},{7,6},{4,7},{9,8},{10,9},{11,1... | collective-permute-start | bytes 233480 | tf_op jit(solution)/shard_map/ppermute | solution.py:548
  7.5 0.8 copy.15.wout_ref
  8.3 0.0 copy-start.2
  8.3 0.7 copy-done.2
  9.0 0.0 copy-start.4
  9.0 0.7 copy-done.4
  9.6 1.2 %prep.1 = (bf16[256,480]{1,0:T(8,128)(2,1)S(1)}, bf16[160,768]{1,0:T(8,128)(2,1)S(1)}, bf16[160,768]{1,0:T(8,128)(2,1)S(1)}, bf16[256,480]{1,0:T(8,128)(2,1)S(1)}) custom-call(f32[19,32]{1,0:T(8,128)S(1)} %copy-done.2, f32[1,32]{1,0:T(1,128)S(1)} %bitcast.9, f32[32,19]{1,0:T(8,128)S(1)} %copy.15.wout_ref), custom_call_target="tpu_custom_call" | custom-call | tf_op jit(solution)/shard_map/prep/pallas_call | solution.py:460
  10.8 0.0 collective-permute-done.before_ref
  10.8 0.0 collective-permute-done.1.after_ref
  10.8 0.0 copy-start
  10.9 1.1 copy-done
  11.9 0.0 copy-start.3
  11.9 0.7 copy-done.3
  12.6 2.9 %first.1 = (f32[344,256]{1,0:T(8,128)S(1)}, f32[344,256]{1,0:T(8,128)S(1)}, f32[19,40,256]{2,1,0:T(8,128)S(1)}, bf16[5,320,256]{2,1,0:T(8,128)(2,1)S(1)}, bf16[5,512,256]{2,1,0:T(8,128)(2,1)S(1)}) custom-call(s32[1]{0:T(128)} %bitcast.parity_ref, f32[19]{0:T(128)S(1)} %copy-done.3, f32[19,2,16,256]{3,2,1,0:T(8,128)S(1)} %copy-done, ...), custom_call_target="tpu_custom_call" | custom-call | tf_op jit(solution)/shard_map/first/pallas_call | solution.py:482
  15.5 5.1 %collective-permute-start.2 = (f32[344,256]{1,0:T(8,128)S(1)}, f32[344,256]{1,0:T(8,128)S(1)}, u32[]{:S(2)}, u32[]{:S(2)}) collective-permute-start(f32[344,256]{1,0:T(8,128)S(1)} %get-tuple-element.22), channel_id=1, source_target_pairs={{0,4},{4,0},{8,12},{12,8},{16,20},{20,16},{24,28},{28,24},{32,36},... | collective-permute-start | bytes 1056776 | tf_op jit(solution)/shard_map/ppermute | solution.py:553
  20.6 7.6 %collective-permute-start.3 = (f32[344,256]{1,0:T(8,128)S(1)}, f32[344,256]{1,0:T(8,128)S(1)}, u32[]{:S(2)}, u32[]{:S(2)}) collective-permute-start(f32[344,256]{1,0:T(8,128)S(1)} %get-tuple-element.23), channel_id=1, source_target_pairs={{0,508},{4,8},{8,4},{12,16},{16,12},{20,24},{24,20},{28,32},{32,28... | collective-permute-start | bytes 1056776 | tf_op jit(solution)/shard_map/ppermute | solution.py:554
  28.2 8.8 %collective-permute-done.2.msg_a_ref = f32[344,256]{1,0:T(8,128)S(1)} collective-permute-done((f32[344,256]{1,0:T(8,128)S(1)}, f32[344,256]{1,0:T(8,128)S(1)}, u32[]{:S(2)}, u32[]{:S(2)}) %collective-permute-start.2) | collective-permute-done | bytes 352288 | tf_op jit(solution)/shard_map/ppermute | solution.py:553
  37.0 0.0 collective-permute-done.3.msg_b_ref
  37.0 0.0 copy-start.1
  37.0 0.8 copy-done.1
  37.7 5.1 %second.1 = (f32[4,2,16,256]{3,2,1,0:T(8,128)}, f32[32,256]{1,0:T(8,128)S(1)}, bf16[5,320,256]{2,1,0:T(8,128)(2,1)S(1)}, bf16[9,512,256]{2,1,0:T(8,128)(2,1)S(1)}, f32[9,3,8,256]{3,2,1,0:T(8,128)S(1)}) custom-call(s32[1]{0:T(128)} %bitcast.parity_ref, f32[19]{0:T(128)S(1)} %copy-done.3, f32[19,40,256]{2,1,0:T(8,128)S(1)} %get-tuple-element.21.c1_ref, ...), custom_call_target="tpu_custom_call" | custom-call | tf_op jit(solution)/shard_map/second/pallas_call | solution.py:500
  42.9 4.8 %collective-permute-start.5 = (f32[32,256]{1,0:T(8,128)S(1)}, f32[32,256]{1,0:T(8,128)S(1)}, u32[]{:S(2)}, u32[]{:S(2)}) collective-permute-start(f32[32,256]{1,0:T(8,128)S(1)} %get-tuple-element.25.r_ref), channel_id=1, source_target_pairs={{0,4},{4,0},{8,12},{12,8},{16,20},{20,16},{24,28},{28,24},{32,36},... | collective-permute-start | bytes 98312 | tf_op jit(solution)/shard_map/ppermute | solution.py:558
  47.7 8.0 %collective-permute-start.4 = (f32[32,256]{1,0:T(8,128)S(1)}, f32[32,256]{1,0:T(8,128)S(1)}, u32[]{:S(2)}, u32[]{:S(2)}) collective-permute-start(f32[32,256]{1,0:T(8,128)S(1)} %get-tuple-element.25.r_ref), channel_id=1, source_target_pairs={{0,508},{4,8},{8,4},{12,16},{16,12},{20,24},{24,20},{28,32},{32,28... | collective-permute-start | bytes 98312 | tf_op jit(solution)/shard_map/ppermute | solution.py:559
  55.7 0.0 collective-permute-done.5.r_a_ref
  55.7 1.9 %collective-permute-done.4.r_b_ref = f32[32,256]{1,0:T(8,128)S(1)} collective-permute-done((f32[32,256]{1,0:T(8,128)S(1)}, f32[32,256]{1,0:T(8,128)S(1)}, u32[]{:S(2)}, u32[]{:S(2)}) %collective-permute-start.4) | collective-permute-done | bytes 32800 | tf_op jit(solution)/shard_map/ppermute | solution.py:559
  57.6 6.2 %third.1 = f32[16,128]{1,0:T(8,128)S(1)} custom-call(s32[1]{0:T(128)} %bitcast.parity_ref, f32[32,256]{1,0:T(8,128)S(1)} %get-tuple-element.25.r_ref, f32[32,256]{1,0:T(8,128)S(1)} %collective-permute-done.4.r_b_ref, f32[32,256]{1,0:T(8,128)S(1)} %collective-permute-done.5.r_a_ref, bf16[5,320,256]{2,1,0:T(8,128)(2,1)S(1)} %get-tuple-element.26.x1_ref, ...), custom_call_target="tpu_custom_call" | custom-call | tf_op jit(solution)/shard_map/third/pallas_call | solution.py:518
  63.8 8.0 %all_to_all.10 = f32[8,16,128]{2,1,0:T(8,128)S(1)} all-to-all(f32[8,16,128]{2,1,0:T(8,128)S(1)} %broadcast_in_dim.4), channel_id=1, replica_groups=mesh['zh'=4,'zl'=4,'x'=4,'yh'=2,'yl'=2,'c'=2] {'yh','yl','c'}, dimensions={0} | all-to-all | bytes 131072 | tf_op jit(solution)/shard_map/all_to_all | solution.py:538
  71.8 17.0 %all_to_all.11 = f32[16,16,128]{2,1,0:T(8,128)S(1)} all-to-all(f32[16,16,128]{2,1,0:T(8,128)S(1)} %broadcast_in_dim.5), channel_id=1, replica_groups=mesh['zh'=4,'zl'=4,'x'=4,'yh'=2,'yl'=2,'c'=2] {'zl','x'}, dimensions={0} | all-to-all | bytes 262144 | tf_op jit(solution)/shard_map/all_to_all | solution.py:538
  88.8 18.7 %psum.7 = f32[16,128]{1,0:T(8,128)S(1)} all-reduce(f32[16,128]{1,0:T(8,128)S(1)} %reduce_sum.19), channel_id=1, replica_groups=mesh['zh'=4,'zl'=4,'x'=4,'yh'=2,'yl'=2,'c'=2] {'zh'}, use_global_device_ids=true, to_apply=%region_2.3 | all-reduce | flops 2048 | bytes 16384 | tf_op jit(solution)/shard_map/psum | solution.py:563
  107.6 0.6 slice_bitcast_fusion.1
  108.1 0.1 fusion.2
  108.2 0.1 copy.16
  108.3 0.6 reshape.31
  108.9 0.6 fusion
  (5 shorter events, 0.1 us)
Async XLA Ops:
  1.8 9.0 %collective-permute-start = (f32[19,4,256]{2,1,0:T(4,128)S(1)}, f32[19,4,256]{2,1,0:T(4,128)S(1)}, u32[]{:S(2)}, u32[]{:S(2)}) collective-permute-start(f32[19,4,256]{2,1,0:T(4,128)S(1)} %reshape.28), channel_id=1, source_target_pairs={{0,1},{1,2},{2,3},{3,0},{4,5},{5,6},{6,7},{7,4},{8,9},{9,10},{10,1... | collective-permute-start | bytes 233480 | tf_op jit(solution)/shard_map/ppermute | solution.py:547
  3.8 7.0 %collective-permute-start.1 = (f32[19,4,256]{2,1,0:T(4,128)S(1)}, f32[19,4,256]{2,1,0:T(4,128)S(1)}, u32[]{:S(2)}, u32[]{:S(2)}) collective-permute-start(f32[19,4,256]{2,1,0:T(4,128)S(1)} %reshape.29), channel_id=1, source_target_pairs={{1,0},{2,1},{3,2},{0,3},{5,4},{6,5},{7,6},{4,7},{9,8},{10,9},{11,1... | collective-permute-start | bytes 233480 | tf_op jit(solution)/shard_map/ppermute | solution.py:548
  8.3 0.7 copy-start.2
  9.0 0.7 copy-start.4
  10.8 1.1 copy-start
  11.9 0.7 copy-start.3
  15.5 21.5 %collective-permute-start.2 = (f32[344,256]{1,0:T(8,128)S(1)}, f32[344,256]{1,0:T(8,128)S(1)}, u32[]{:S(2)}, u32[]{:S(2)}) collective-permute-start(f32[344,256]{1,0:T(8,128)S(1)} %get-tuple-element.22), channel_id=1, source_target_pairs={{0,4},{4,0},{8,12},{12,8},{16,20},{20,16},{24,28},{28,24},{32,36},... | collective-permute-start | bytes 1056776 | tf_op jit(solution)/shard_map/ppermute | solution.py:553
  20.6 16.4 %collective-permute-start.3 = (f32[344,256]{1,0:T(8,128)S(1)}, f32[344,256]{1,0:T(8,128)S(1)}, u32[]{:S(2)}, u32[]{:S(2)}) collective-permute-start(f32[344,256]{1,0:T(8,128)S(1)} %get-tuple-element.23), channel_id=1, source_target_pairs={{0,508},{4,8},{8,4},{12,16},{16,12},{20,24},{24,20},{28,32},{32,28... | collective-permute-start | bytes 1056776 | tf_op jit(solution)/shard_map/ppermute | solution.py:554
  37.0 0.8 copy-start.1
  42.9 12.8 %collective-permute-start.5 = (f32[32,256]{1,0:T(8,128)S(1)}, f32[32,256]{1,0:T(8,128)S(1)}, u32[]{:S(2)}, u32[]{:S(2)}) collective-permute-start(f32[32,256]{1,0:T(8,128)S(1)} %get-tuple-element.25.r_ref), channel_id=1, source_target_pairs={{0,4},{4,0},{8,12},{12,8},{16,20},{20,16},{24,28},{28,24},{32,36},... | collective-permute-start | bytes 98312 | tf_op jit(solution)/shard_map/ppermute | solution.py:558
  47.7 9.9 %collective-permute-start.4 = (f32[32,256]{1,0:T(8,128)S(1)}, f32[32,256]{1,0:T(8,128)S(1)}, u32[]{:S(2)}, u32[]{:S(2)}) collective-permute-start(f32[32,256]{1,0:T(8,128)S(1)} %get-tuple-element.25.r_ref), channel_id=1, source_target_pairs={{0,508},{4,8},{8,4},{12,16},{16,12},{20,24},{24,20},{28,32},{32,28... | collective-permute-start | bytes 98312 | tf_op jit(solution)/shard_map/ppermute | solution.py:559

commit v4 on v3

v4 whole, which is shorter than its diff:
```python
import math

import jax
import jax.numpy as jnp
from jax import lax
from jax.experimental import pallas as pl
from jax.experimental.pallas import tpu as pltpu
from jax.sharding import Mesh, PartitionSpec as P

velocity_table = (
    (0, 0, 0),
    (1, 0, 0),
    (-1, 0, 0),
    (0, 1, 0),
    (0, -1, 0),
    (0, 0, 1),
    (0, 0, -1),
    (1, 1, 0),
    (-1, -1, 0),
    (1, -1, 0),
    (-1, 1, 0),
    (1, 0, 1),
    (-1, 0, -1),
    (1, 0, -1),
    (-1, 0, 1),
    (0, 1, 1),
    (0, -1, -1),
    (0, 1, -1),
    (0, -1, 1),
)
lattice_weights = (1.0 / 3.0,) + (1.0 / 18.0,) * 6 + (1.0 / 36.0,) * 12
input_scale = 8.0
output_scale = 0.05
relax_time = 0.8

Q = 19
H = 32
NZ = 256
W1 = 20
W2 = 18
G1 = 2 * W1 // 8
G2 = 4 * W2 // 8
PG = (2, 7)
MARGIN = 8
SP = 8
QS = 20 * SP
HS = H * SP
MSG = 344
F32 = jnp.float32
BF16 = jnp.bfloat16
MIB = 1024 * 1024
B1, B2, B4, B5 = 5, 9, 3, 3

to_right = [(q, -1) for q in range(19) if velocity_table[q][0] >= 0]
to_right += [(q, 0) for q in range(19) if velocity_table[q][0] == 1]
to_left = [(q, 2) for q in range(19) if velocity_table[q][0] <= 0]
to_left += [(q, 1) for q in range(19) if velocity_table[q][0] == -1]


def split(x):
    hi = x.astype(BF16)
    lo = (x - hi.astype(F32)).astype(BF16)
    return hi, lo


def mm(a, b):
    return lax.dot_general(a, b, (((1,), (0,)), ((), ())), preferred_element_type=F32)


def mm_nt(a, b):
    return lax.dot_general(a, b, (((1,), (1,)), ((), ())), preferred_element_type=F32)


def expanded(packed_ref):
    hp = lax.Precision.HIGHEST
    nn = (((1,), (0,)), ((), ()))
    eq = (
        lax.broadcasted_iota(jnp.int32, (QS, 20), 0) // SP
        == lax.broadcasted_iota(jnp.int32, (QS, 20), 1)
    ).astype(F32)
    eh = (
        lax.broadcasted_iota(jnp.int32, (HS, H), 0) // SP
        == lax.broadcasted_iota(jnp.int32, (HS, H), 1)
    ).astype(F32)
    row = lax.broadcasted_iota(jnp.int32, (20, H), 0)
    w_in = packed_ref[0:20, :] * jnp.where(row < Q, input_scale, 1.0)
    w_out = jnp.where(row < Q, packed_ref[20:40, :] * output_scale, 0.0)
    t_in = lax.dot_general(eq, w_in, nn, precision=hp, preferred_element_type=F32)
    t_out = lax.dot_general(eq, w_out, nn, precision=hp, preferred_element_type=F32)
    return eh, t_in, t_out


def put(ref, a, b):
    hp = lax.Precision.HIGHEST
    nt = (((1,), (1,)), ((), ()))
    full = lax.dot_general(a, b, nt, precision=hp, preferred_element_type=F32)
    m, n = full.shape
    row = lax.broadcasted_iota(jnp.int32, (m, n), 0)
    column = lax.broadcasted_iota(jnp.int32, (m, n), 1)
    hi, lo = split(jnp.where((row % SP) == (column % SP), full, 0.0))
    ref[:, 0:n] = hi
    ref[:, n : 2 * n] = hi
    ref[:, 2 * n : 3 * n] = lo


def prep_kernel(packed_ref, lin_ref, lout_ref, bout_ref):
    eh, t_in, t_out = expanded(packed_ref)
    put(lin_ref, eh, t_in)
    put(lout_ref, t_out, eh)
    pick = (
        lax.broadcasted_iota(jnp.int32, (QS, H), 0) // SP
        == lax.broadcasted_iota(jnp.int32, (QS, H), 1)
    ).astype(F32)
    bias = jnp.sum(pick * (packed_ref[39:40, :] * output_scale), axis=1, keepdims=True)
    bout_ref[...] = jnp.broadcast_to(bias, (QS, NZ))


def middle_kernel(after_first, packed_ref, target_in, lint_ref, loutt_ref, target_ref):
    target_ref[...] = target_in[...]
    eh, t_in, t_out = expanded(packed_ref)
    is_bias = lax.broadcasted_iota(jnp.int32, (QS, H), 0) >= Q * SP
    put(lint_ref, jnp.where(is_bias, 0.0, t_in), eh)
    put(loutt_ref, eh, t_out)


def equilibrium_parts(f):
    density = f[0]
    for q in range(1, Q):
        density = density + f[q]
    momentum = []
    for a in range(3):
        plus = None
        minus = None
        for q in range(Q):
            c = velocity_table[q][a]
            if c == 1:
                plus = f[q] if plus is None else plus + f[q]
            elif c == -1:
                minus = f[q] if minus is None else minus + f[q]
        momentum.append(plus - minus)
    return density, momentum


def project(q, m):
    out = None
    for a in range(3):
        c = velocity_table[q][a]
        if c == 0:
            continue
        if out is None:
            out = m[a] if c == 1 else -m[a]
        else:
            out = out + m[a] if c == 1 else out - m[a]
    return out


def excess_of(f):
    density, m = equilibrium_parts(f)
    base = density - 1.5 * (m[0] * m[0] + m[1] * m[1] + m[2] * m[2])
    excess = [f[0] - lattice_weights[0] * base]
    for q in range(1, Q, 2):
        w = lattice_weights[q]
        cm = project(q, m)
        even = w * (base + 4.5 * (cm * cm))
        odd = (3.0 * w) * cm
        excess.append(f[q] - (even + odd))
        excess.append(f[q + 1] - (even - odd))
    return excess, m


def rows8(x, q):
    return x[q * SP : (q + 1) * SP, :]


def batches(groups, size):
    return [range(g, min(g + size, groups)) for g in range(0, groups, size)]


def lanes(parts):
    return parts[0] if len(parts) == 1 else jnp.concatenate(parts, axis=1)


def block(x, i):
    return x[:, i * NZ : (i + 1) * NZ]


def stack3(hi, lo):
    return jnp.concatenate([hi, lo, hi], axis=0)


def collide(fs, lin_ref, lout_ref, bout_ref, save_x, save_h):
    excesses, ms, his, los = [], [], [], []
    for i, f in enumerate(fs):
        excess, m = excess_of(f)
        x = jnp.concatenate(excess + [jnp.ones((SP, NZ), F32)], axis=0)
        xhi, xlo = split(x)
        save_x(i, xhi, xlo)
        excesses.append(excess)
        ms.append(m)
        his.append(xhi)
        los.append(xlo)
    pre = mm(lin_ref[...], stack3(lanes(his), lanes(los)))
    hhi, hlo = split(jnp.tanh(pre))
    for i in range(len(fs)):
        save_h(i, block(hhi, i), block(hlo, i))
    corr = mm(lout_ref[...], stack3(hhi, hlo))
    outs = []
    for i, f in enumerate(fs):
        out = []
        for q in range(Q):
            bias = bout_ref[q * SP : (q + 1) * SP, :]
            add = block(rows8(corr, q), i) + bias
            out.append(f[q] - excesses[i][q] * (1.0 / relax_time) + add)
        outs.append(out)
    return outs, ms


def zroll(x, step):
    if step == 0:
        return x
    return pltpu.roll(x, step % NZ, 1)


def edges_kernel(pop_hbm, last_ref, start_ref, pop_ref, sem):
    copy = pltpu.make_async_copy(pop_hbm, pop_ref, sem)
    copy.start()
    copy.wait()
    for x in range(2):
        last_ref[:, 2 * x : 2 * x + 2, :] = pop_ref[:, x, 14:16, :]
        start_ref[:, 2 * x : 2 * x + 2, :] = pop_ref[:, x, 0:2, :]


def first_kernel(
    parity_ref,
    bout_ref,
    pop_ref,
    before_ref,
    after_ref,
    lin_ref,
    lout_ref,
    msg_a_ref,
    msg_b_ref,
    c1_ref,
    x1_ref,
    h1_ref,
    fs,
):
    for x in range(2):
        fs[:, W1 * x : W1 * x + 2, :] = before_ref[:, 2 * x : 2 * x + 2, :]
        fs[:, W1 * x + 2 : W1 * x + 18, :] = pop_ref[:, x]
        fs[:, W1 * x + 18 : W1 * x + 20, :] = after_ref[:, 2 * x : 2 * x + 2, :]
    for batch in batches(G1, B1):
        f = [[fs[q, 8 * g : 8 * g + 8, :] for q in range(Q)] for g in batch]

        def save_x(i, hi, lo):
            x1_ref[batch[i], 0:QS, :] = hi
            x1_ref[batch[i], QS : 2 * QS, :] = lo

        def save_h(i, hi, lo):
            h1_ref[batch[i], 0:HS, :] = hi
            h1_ref[batch[i], HS : 2 * HS, :] = lo

        outs, _m = collide(f, lin_ref, lout_ref, bout_ref, save_x, save_h)
        for g, out in zip(batch, outs):
            for q in range(Q):
                c1_ref[q, 8 * g : 8 * g + 8, :] = zroll(out[q], velocity_table[q][2])
    odd = parity_ref[0] == 1

    def piece(q, plane):
        start = W1 * (plane - velocity_table[q][0]) + 1 - velocity_table[q][1]
        return c1_ref[q, start : start + W2, :]

    for k in range(Q):
        q, plane = to_right[k]
        right = piece(q, plane + 2)
        q, plane = to_left[k]
        left = piece(q, plane - 2)
        msg_a_ref[W2 * k : W2 * k + W2, :] = jnp.where(odd, left, right)
        msg_b_ref[W2 * k : W2 * k + W2, :] = jnp.where(odd, right, left)
    msg_a_ref[W2 * Q :, :] = jnp.zeros((MSG - W2 * Q, NZ), F32)
    msg_b_ref[W2 * Q :, :] = jnp.zeros((MSG - W2 * Q, NZ), F32)


def second_kernel(
    parity_ref,
    bout_ref,
    c1_ref,
    msg_a_ref,
    msg_b_ref,
    target_ref,
    lin_ref,
    lout_ref,
    moments_ref,
    r_ref,
    x2_ref,
    h2_ref,
    m2_ref,
    a1,
    c2,
):
    odd = parity_ref[0] == 1
    for k in range(Q):
        rows = slice(W2 * k, W2 * k + W2)
        msg_a = msg_a_ref[rows, :]
        msg_b = msg_b_ref[rows, :]
        q, plane = to_right[k]
        a1[q, W2 * (plane + 1) : W2 * (plane + 2), :] = jnp.where(odd, msg_a, msg_b)
        q, plane = to_left[k]
        a1[q, W2 * (plane + 1) : W2 * (plane + 2), :] = jnp.where(odd, msg_b, msg_a)
    for q in range(Q):
        for plane in range(-1, 3):
            source = plane - velocity_table[q][0]
            if source in (0, 1):
                start = W1 * source + 1 - velocity_table[q][1]
                a1[q, W2 * (plane + 1) : W2 * (plane + 2), :] = c1_ref[q, start : start + W2, :]
    for batch in batches(G2, B2):
        f = [[a1[q, 8 * g : 8 * g + 8, :] for q in range(Q)] for g in batch]

        def save_x(i, hi, lo):
            if PG[0] <= batch[i] < PG[1]:
                x2_ref[batch[i] - PG[0], 0:QS, :] = hi
                x2_ref[batch[i] - PG[0], QS : 2 * QS, :] = lo

        def save_h(i, hi, lo):
            h2_ref[batch[i], 0:HS, :] = hi
            h2_ref[batch[i], HS : 2 * HS, :] = lo

        outs, ms = collide(f, lin_ref, lout_ref, bout_ref, save_x, save_h)
        for g, out, m in zip(batch, outs, ms):
            for a in range(3):
                m2_ref[g, a] = m[a]
            for q in range(Q):
                c2[q, 8 * g : 8 * g + 8, :] = zroll(out[q], velocity_table[q][2])
    residual_scale = 1.0 / math.sqrt(256 * 64 * 256)
    for x in range(2):
        for half in range(2):
            first = W2 * (x + 1) + 1 + 8 * half
            f = []
            for q in range(Q):
                start = first - W2 * velocity_table[q][0] - velocity_table[q][1]
                f.append(c2[q, start : start + 8, :])
            density, m = equilibrium_parts(f)
            moments_ref[0, x, 8 * half : 8 * half + 8, :] = density
            for a in range(3):
                moments_ref[a + 1, x, 8 * half : 8 * half + 8, :] = m[a]
            r = (density - target_ref[x, 8 * half : 8 * half + 8, :]) * residual_scale
            r_ref[16 * x + 8 * half : 16 * x + 8 * half + 8, :] = r


def third_kernel(
    parity_ref,
    r_ref,
    r_b_ref,
    r_a_ref,
    x1_ref,
    h1_ref,
    x2_ref,
    h2_ref,
    m2_ref,
    lint_ref,
    loutt_ref,
    grads_ref,
    rs,
    g1s,
    acc_in,
    acc_out,
    acc_b,
):
    odd = parity_ref[0] == 1
    rs[...] = jnp.zeros_like(rs)
    g1s[...] = jnp.zeros_like(g1s)
    acc_in[...] = jnp.zeros_like(acc_in)
    acc_out[...] = jnp.zeros_like(acc_out)
    acc_b[...] = jnp.zeros_like(acc_b)
    r_a, r_b = r_a_ref[...], r_b_ref[...]
    parts = (jnp.where(odd, r_a, r_b), r_ref[...], jnp.where(odd, r_b, r_a))
    for i in range(6):
        first = MARGIN + W2 * i + 1
        for half in range(2):
            at = 16 * (i % 2) + 8 * half
            r = parts[i // 2][at : at + 8, :]
            rows = slice(first + 8 * half, first + 8 * half + 8)
            rs[0, rows, :] = r
            rs[1, rows, :] = zroll(r, -1)
            rs[2, rows, :] = zroll(r, 1)

    def hidden_pull(gqs, h_ref, batch):
        gs, ghi, glo = [], [], []
        for gq in gqs:
            g = jnp.concatenate(gq + [jnp.zeros((SP, NZ), F32)], axis=0)
            hi, lo = split(g)
            gs.append(g)
            ghi.append(hi)
            glo.append(lo)
        dh = mm(loutt_ref[...], stack3(lanes(ghi), lanes(glo)))
        dpre = []
        for i, g in enumerate(batch):
            hid = h_ref[g, 0:HS, :].astype(F32) + h_ref[g, HS : 2 * HS, :].astype(F32)
            dpre.append(block(dh, i) * (1.0 - hid * hid))
        return gs, dpre

    def add_params(gs, dpre, x_ref, h_ref, x_at, h_at):
        ghi, glo = zip(*[split(g) for g in gs])
        dhi, dlo = zip(*[split(d) for d in dpre])
        xhi = [x_ref[g, 0:QS, :] for g in x_at]
        xlo = [x_ref[g, QS : 2 * QS, :] for g in x_at]
        hhi = [h_ref[g, 0:HS, :] for g in h_at]
        hlo = [h_ref[g, HS : 2 * HS, :] for g in h_at]
        xh, xl, dh, dl = lanes(xhi), lanes(xlo), lanes(dhi), lanes(dlo)
        both = mm_nt(jnp.concatenate([xh, xl], axis=0), dh)
        acc_in[...] += both[0:QS] + both[QS:] + mm_nt(xh, dl)
        gh, gl, hh, hl = lanes(ghi), lanes(glo), lanes(hhi), lanes(hlo)
        both = mm_nt(jnp.concatenate([gh, gl], axis=0), hh)
        acc_out[...] += both[0:QS] + both[QS:] + mm_nt(gh, hl)
        acc_b[...] += sum(gs[1:], gs[0])

    def keep(x, lo, hi):
        if lo == 0 and hi == SP:
            return x
        row = lax.broadcasted_iota(jnp.int32, x.shape, 0) % SP
        return jnp.where((row >= lo) & (row < hi), x, 0.0)

    for batch in batches(G2, B4):
        gqs = []
        for g in batch:
            gq = []
            for q in range(Q):
                cx, cy, cz = velocity_table[q]
                start = MARGIN + W2 + 8 * g + W2 * cx + cy
                gq.append(rs[{0: 0, 1: 1, -1: 2}[cz], start : start + 8, :])
            gqs.append(gq)
        gs, dpre = hidden_pull(gqs, h2_ref, batch)
        kept_g, kept_d, kept_at = [], [], []
        for i, g in enumerate(batch):
            if PG[0] <= g < PG[1]:
                lo = max(W2 - 8 * g, 0)
                hi = min(3 * W2 - 8 * g, SP)
                kept_g.append(keep(gs[i], lo, hi))
                kept_d.append(keep(dpre[i], lo, hi))
                kept_at.append(g)
        if kept_at:
            add_params(kept_g, kept_d, x2_ref, h2_ref, [g - PG[0] for g in kept_at], kept_at)
        dhi, dlo = split(lanes(dpre))
        back = mm(lint_ref[...], stack3(dhi, dlo))
        for i, g in enumerate(batch):
            m = [m2_ref[g, a] for a in range(3)]
            de = [block(rows8(back, q), i) - gqs[i][q] * (1.0 / relax_time) for q in range(Q)]
            t = [lattice_weights[q] * de[q] for q in range(Q)]
            drho = t[0]
            for q in range(1, Q):
                drho = drho + t[q]
            u = [None] * Q
            for q in range(1, Q, 2):
                cm = 9.0 * project(q, m)
                u[q] = t[q] * (3.0 + cm)
                u[q + 1] = t[q + 1] * (3.0 - cm)
            dm = []
            for a in range(3):
                plus = None
                minus = None
                for q in range(Q):
                    c = velocity_table[q][a]
                    if c == 1:
                        plus = u[q] if plus is None else plus + u[q]
                    elif c == -1:
                        minus = u[q] if minus is None else minus + u[q]
                dm.append(plus - minus - 3.0 * m[a] * drho)
            for q in range(Q):
                df = gqs[i][q] + de[q] - drho
                if q:
                    df = df - project(q, dm)
                df = zroll(df, -velocity_table[q][2])
                for plane in range(4):
                    lo = max(W2 * plane, 8 * g)
                    hi = min(W2 * plane + W2, 8 * g + 8)
                    if lo < hi:
                        at = MARGIN + 1 + 2 * plane
                        g1s[q, at + lo : at + hi, :] = df[lo - 8 * g : hi - 8 * g, :]

    for batch in batches(G1, B5):
        gqs = []
        for g in batch:
            gq = []
            for q in range(Q):
                cx, cy, _cz = velocity_table[q]
                start = MARGIN + W1 + 8 * g + W1 * cx + cy
                gq.append(g1s[q, start : start + 8, :])
            gqs.append(gq)
        gs, dpre = hidden_pull(gqs, h1_ref, batch)
        add_params(gs, dpre, x1_ref, h1_ref, batch, batch)

    hp = lax.Precision.HIGHEST
    rq = lax.broadcasted_iota(jnp.int32, (QS, HS), 0)
    rh = lax.broadcasted_iota(jnp.int32, (QS, HS), 1)
    mask = (rq % SP) == (rh % SP)
    fold = (
        lax.broadcasted_iota(jnp.int32, (HS, H), 0) // SP
        == lax.broadcasted_iota(jnp.int32, (HS, H), 1)
    ).astype(F32)

    def trace(acc):
        kept = jnp.where(mask, acc[...], 0.0).reshape(20, SP, HS).sum(axis=1)
        return lax.dot_general(
            kept, fold, (((1,), (0,)), ((), ())), precision=hp, preferred_element_type=F32
        )

    q_index = lax.broadcasted_iota(jnp.int32, (20, H), 0)
    d_in = trace(acc_in) * jnp.where(q_index < Q, input_scale, 1.0)
    d_out = trace(acc_out) * output_scale
    nt = (((1,), (1,)), ((), ()))
    b_row = lax.dot_general(
        jnp.full((1, NZ), output_scale, F32), acc_b[...], nt, precision=hp, preferred_element_type=F32
    )
    d_b = lax.dot_general(
        b_row,
        (
            lax.broadcasted_iota(jnp.int32, (QS, 20), 0) // SP
            == lax.broadcasted_iota(jnp.int32, (QS, 20), 1)
        ).astype(F32),
        (((1,), (0,)), ((), ())),
        precision=hp,
        preferred_element_type=F32,
    )
    grads_ref[...] = jnp.zeros_like(grads_ref)
    grads_ref[0:10, 0:H] = d_in[0:10]
    grads_ref[0:10, H : 2 * H] = d_in[10:20]
    grads_ref[0:10, 2 * H : 3 * H] = d_out[0:10]
    grads_ref[0:10, 3 * H : 4 * H] = d_out[10:20]
    grads_ref[10:11, 0:20] = d_b


def unpack_kernel(grads_ref, win_ref, bin_ref, woutt_ref, bout_ref):
    g = grads_ref[...]
    win_ref[0:10, :] = g[0:10, 0:H]
    win_ref[10:Q, :] = g[0:9, H : 2 * H]
    bin_ref[...] = g[9:10, H : 2 * H]
    woutt_ref[0:10, :] = g[0:10, 2 * H : 3 * H]
    woutt_ref[10:Q, :] = g[0:9, 3 * H : 4 * H]
    bout_ref[...] = g[10:11, 0:Q]


VMEM = pl.BlockSpec(memory_space=pltpu.VMEM)
SMEM = pl.BlockSpec(memory_space=pltpu.SMEM)


def shape(*dims, kind=F32):
    return jax.ShapeDtypeStruct(dims, kind)


HBM = pl.BlockSpec(memory_space=pltpu.HBM)


def prep(packed):
    return pl.pallas_call(
        prep_kernel,
        out_shape=(
            shape(HS, 3 * QS, kind=BF16),
            shape(QS, 3 * HS, kind=BF16),
            shape(QS, NZ),
        ),
        in_specs=[VMEM],
        out_specs=(VMEM,) * 3,
        compiler_params=pltpu.CompilerParams(vmem_limit_bytes=24 * MIB),
        name="prep",
    )(packed)


def middle(c1, packed, target):
    return pl.pallas_call(
        middle_kernel,
        out_shape=(
            shape(QS, 3 * HS, kind=BF16),
            shape(HS, 3 * QS, kind=BF16),
            shape(2, 16, NZ),
        ),
        in_specs=[pl.BlockSpec(memory_space=pl.ANY)] + [VMEM] * 2,
        out_specs=(VMEM,) * 3,
        compiler_params=pltpu.CompilerParams(vmem_limit_bytes=24 * MIB),
        name="middle",
    )(c1, packed, target)


def edges(populations):
    return pl.pallas_call(
        edges_kernel,
        out_shape=(shape(Q, 4, NZ), shape(Q, 4, NZ), shape(Q, 2, 16, NZ)),
        in_specs=[HBM],
        out_specs=(VMEM,) * 3,
        scratch_shapes=[pltpu.SemaphoreType.DMA],
        compiler_params=pltpu.CompilerParams(vmem_limit_bytes=24 * MIB),
        name="edges",
    )(populations)


def unpack(grads):
    win, bin_, woutt, bout = pl.pallas_call(
        unpack_kernel,
        out_shape=(shape(Q, H), shape(1, H), shape(Q, H), shape(1, Q)),
        in_specs=[VMEM],
        out_specs=(VMEM,) * 4,
        name="unpack",
    )(grads)
    return win, bin_.reshape(H), woutt.T, bout.reshape(Q)


def first(parity, bias_out, populations, before, after, lin, lout):
    return pl.pallas_call(
        first_kernel,
        out_shape=(
            shape(MSG, NZ),
            shape(MSG, NZ),
            shape(Q, 2 * W1, NZ),
            shape(G1, 2 * QS, NZ, kind=BF16),
            shape(G1, 2 * HS, NZ, kind=BF16),
        ),
        in_specs=[SMEM] + [VMEM] * 6,
        out_specs=(VMEM,) * 5,
        scratch_shapes=[pltpu.VMEM((Q, 2 * W1, NZ), F32)],
        compiler_params=pltpu.CompilerParams(vmem_limit_bytes=24 * MIB),
        name="first",
    )(parity, bias_out, populations, before, after, lin, lout)


def second(parity, bias_out, c1, msg_a, msg_b, target, lin, lout):
    return pl.pallas_call(
        second_kernel,
        out_shape=(
            shape(4, 2, 16, NZ),
            shape(32, NZ),
            shape(PG[1] - PG[0], 2 * QS, NZ, kind=BF16),
            shape(G2, 2 * HS, NZ, kind=BF16),
            shape(G2, 3, SP, NZ),
        ),
        in_specs=[SMEM] + [VMEM] * 7,
        out_specs=(VMEM,) * 5,
        scratch_shapes=[
            pltpu.VMEM((Q, 4 * W2, NZ), F32),
            pltpu.VMEM((Q, 4 * W2, NZ), F32),
        ],
        compiler_params=pltpu.CompilerParams(vmem_limit_bytes=24 * MIB),
        name="second",
    )(parity, bias_out, c1, msg_a, msg_b, target, lin, lout)


def third(parity, r, r_b, r_a, x1, h1, x2, h2, m2, lint, loutt):
    return pl.pallas_call(
        third_kernel,
        out_shape=shape(16, 128),
        in_specs=[SMEM] + [VMEM] * 10,
        out_specs=VMEM,
        scratch_shapes=[
            pltpu.VMEM((3, 2 * MARGIN + 6 * W2 + 4, NZ), F32),
            pltpu.VMEM((Q, 2 * MARGIN + 4 * W1, NZ), F32),
            pltpu.VMEM((QS, HS), F32),
            pltpu.VMEM((QS, HS), F32),
            pltpu.VMEM((QS, NZ), F32),
        ],
        compiler_params=pltpu.CompilerParams(vmem_limit_bytes=24 * MIB),
        name="third",
    )(parity, r, r_b, r_a, x1, h1, x2, h2, m2, lint, loutt)


def gather_sum(x, axes):
    peers = lax.axis_size(axes)
    copies = jnp.broadcast_to(x[None], (peers,) + x.shape)
    return jnp.sum(lax.all_to_all(copies, axes, 0, 0, tiled=True), axis=0)


def body(populations, target_density, weight_in, bias_in, weight_out, bias_out):
    gx, gy = ("zh", "zl", "x", "yh"), ("yl", "c")
    nx, ny = lax.axis_size(gx), lax.axis_size(gy)
    last, start, pops = edges(populations)
    packed = jnp.concatenate(
        [
            weight_in,
            bias_in.reshape(1, H),
            weight_out.T,
            jnp.pad(bias_out, (0, H - Q)).reshape(1, H),
        ],
        axis=0,
    )
    lin, lout, bout = prep(packed)
    before = lax.ppermute(last, gy, [(j, (j + 1) % ny) for j in range(ny)])
    after = lax.ppermute(start, gy, [((j + 1) % ny, j) for j in range(ny)])
    pair = [(i, i ^ 1) for i in range(nx)]
    cross = [(i, (i + 1) % nx if i % 2 else (i - 1) % nx) for i in range(nx)]
    parity = (lax.axis_index("yh") % 2).astype(jnp.int32).reshape(1)
    msg_a, msg_b, c1, x1, h1 = first(parity, bout, pops, before, after, lin, lout)
    lint, loutt, target = middle(c1, packed, target_density)
    got_a = lax.ppermute(msg_a, gx, pair)
    got_b = lax.ppermute(msg_b, gx, cross)
    moments, r, x2, h2, m2 = second(
        parity, bout, c1, got_a, got_b, target, lin, lout
    )
    r_a = lax.ppermute(r, gx, pair)
    r_b = lax.ppermute(r, gx, cross)
    grads = third(parity, r, r_b, r_a, x1, h1, x2, h2, m2, lint, loutt)
    grads = gather_sum(grads, ("yh", "yl", "c"))
    grads = gather_sum(grads, ("zl", "x"))
    grads = lax.psum(grads, "zh")
    return (moments, *unpack(grads))


def solution(mesh):
    fine = Mesh(mesh.devices.reshape(4, 4, 4, 2, 2, 2), ("zh", "zl", "x", "yh", "yl", "c"))
    gx, gy = ("zh", "zl", "x", "yh"), ("yl", "c")
    placed = (P(None, gx, gy, None), P(gx, gy, None), P(), P(), P(), P())
    return jax.shard_map(
        body,
        mesh=fine,
        in_specs=placed,
        out_specs=(P(None, gx, gy, None), P(), P(), P(), P()),
        check_vma=False,
    )
```

time: 110 us -> 102 us (0.927)
  local copies, waits for them, and re-layouts: 7.26 us -> 2.5 us
  Pallas kernels: 15.4 us -> 12.2 us
  waiting for transfers between devices: 10.7 us -> 9.21 us
    unnamed x11 -> x4, local copies, waits for them, and re-layouts: 4.63 us -> 1.82 us
    pallas_call x1, Pallas kernels: 5.15 us -> 2.68 us  [second(): pl.pallas_call(second_kernel, out_shape=(shape(4, 2, 16, NZ), shape(32, N...]
    pallas_call x1 -> x4, Pallas kernels: 1.16 us -> 3.26 us  [the longest x1 1.37 us: unpack(): pl.pallas_call(unpack_kernel, out_shape=(shape(Q, H), shape(1, H), shape(...]
    pallas_call x1, Pallas kernels: 2.9 us -> 1.24 us  [first(): pl.pallas_call(first_kernel, out_shape=(shape(MSG, NZ), shape(MSG, NZ), s...]
    ppermute x1, waiting for transfers between devices: 8.77 us -> 7.33 us  [body(): got_a = lax.ppermute(msg_a, gx, pair)]
    pallas_call x1, Pallas kernels: 6.22 us -> 4.97 us  [third(): pl.pallas_call(third_kernel, out_shape=shape(16, 128), in_specs=[SMEM] +...]
    slice x2 -> x0, local copies, waits for them, and re-layouts: 1.2 us -> none  [the longest x1 1.13 us: body(): start = populations[:, :, 0:2, :].reshape(Q, 4, NZ)]
  transfers between devices with their start and end apart: 6 -> 6, of which waited for: 2 -> 2; matrix products, arithmetic and copies ran while one was open for 1% -> 1% of each run, Pallas kernels for 1% -> 2%
where the time goes in v4:
time: 102 us; the launch traced here: 101 us
  blocking collectives  44.7 us (44%)
  starting transfers between devices  31.1 us (30%)
  Pallas kernels  12.2 us (12%)
  waiting for transfers between devices  9.21 us (9%)
  local copies, waits for them, and re-layouts  2.5 us (2%)
    all_to_all x2, blocking collectives, gather_sum(): return jnp.sum(lax.all_to_all(copies, axes, 0, 0, tiled=True), axis=0)  25.4 us
    psum x1, blocking collectives, body(): grads = lax.psum(grads, 'zh')  19.3 us
    ppermute x1, starting transfers between devices, body(): got_b = lax.ppermute(msg_b, gx, cross)  7.59 us
    ppermute x1, starting transfers between devices, body(): r_b = lax.ppermute(r, gx, cross)  7.5 us
    ppermute x1, waiting for transfers between devices, body(): got_a = lax.ppermute(msg_a, gx, pair)  7.33 us
    ppermute x1, starting transfers between devices, body(): r_a = lax.ppermute(r, gx, pair)  5.32 us
    ppermute x1, starting transfers between devices, body(): got_a = lax.ppermute(msg_a, gx, pair)  5.11 us
    pallas_call x1, Pallas kernels, third(): pl.pallas_call(third_kernel, out_shape=shape(16, 128), in_specs=[SMEM] +...  4.97 us
  transfers between devices with their start and end apart: 6, of which 2 were waited for; matrix products, arithmetic and copies ran while one was open for 1% of the time, Pallas kernels for 2%

profile of v4, /device:TPU:2, one launch (start us, length us, event | category | flops | bytes accessed | tf_op | source)
XLA Modules:
  0.0 101.2 jit_solution(9596437449345344961)
XLA Ops:
  0.6 0.0 copy-start
  0.6 1.1 %copy-done = f32[19,2,16,256]{3,2,1,0:T(8,128)S(1)} copy-done((f32[19,2,16,256]{3,2,1,0:T(8,128)S(1)}, f32[19,2,16,256]{3,2,1,0:T(8,128)}, u32[]{:S(2)}) %copy-start) | copy-done | bytes 622616
  1.7 0.2 edges.1
  1.9 1.9 %collective-permute-start = (f32[19,4,256]{2,1,0:T(4,128)S(1)}, f32[19,4,256]{2,1,0:T(4,128)S(1)}, u32[]{:S(2)}, u32[]{:S(2)}) collective-permute-start(f32[19,4,256]{2,1,0:T(4,128)S(1)} %get-tuple-element.30), channel_id=1, source_target_pairs={{0,1},{1,2},{2,3},{3,0},{4,5},{5,6},{6,7},{7,4},{8,9},{9,10},{10,1... | collective-permute-start | bytes 233480 | tf_op jit(solution)/shard_map/ppermute | solution.py:683
  3.9 3.6 %collective-permute-start.1 = (f32[19,4,256]{2,1,0:T(4,128)S(1)}, f32[19,4,256]{2,1,0:T(4,128)S(1)}, u32[]{:S(2)}, u32[]{:S(2)}) collective-permute-start(f32[19,4,256]{2,1,0:T(4,128)S(1)} %get-tuple-element.31), channel_id=1, source_target_pairs={{1,0},{2,1},{3,2},{0,3},{5,4},{6,5},{7,6},{4,7},{9,8},{10,9},{11,1... | collective-permute-start | bytes 233480 | tf_op jit(solution)/shard_map/ppermute | solution.py:684
  7.5 0.7 pad_bitcast_fusion
  8.2 0.7 pad_maximum_fusion.packed_ref
  8.9 0.8 prep.1
  9.8 0.0 collective-permute-done.before_ref
  9.8 0.0 collective-permute-done.1.after_ref
  9.8 1.2 %first.1 = (f32[344,256]{1,0:T(8,128)S(1)}, f32[344,256]{1,0:T(8,128)S(1)}, f32[19,40,256]{2,1,0:T(8,128)S(1)}, bf16[5,320,256]{2,1,0:T(8,128)(2,1)S(1)}, bf16[5,512,256]{2,1,0:T(8,128)(2,1)S(1)}) custom-call(s32[1]{0:T(128)} %bitcast.parity_ref, f32[160,256]{1,0:T(8,128)S(1)} %get-tuple-element.28.bout_ref, ...), custom_call_target="tpu_custom_call" | custom-call | tf_op jit(solution)/shard_map/first/pallas_call | solution.py:607
  11.0 5.1 %collective-permute-start.2 = (f32[344,256]{1,0:T(8,128)S(1)}, f32[344,256]{1,0:T(8,128)S(1)}, u32[]{:S(2)}, u32[]{:S(2)}) collective-permute-start(f32[344,256]{1,0:T(8,128)S(1)} %get-tuple-element.35), channel_id=1, source_target_pairs={{0,4},{4,0},{8,12},{12,8},{16,20},{20,16},{24,28},{28,24},{32,36},... | collective-permute-start | bytes 1056776 | tf_op jit(solution)/shard_map/ppermute | solution.py:690
  16.2 7.6 %collective-permute-start.3 = (f32[344,256]{1,0:T(8,128)S(1)}, f32[344,256]{1,0:T(8,128)S(1)}, u32[]{:S(2)}, u32[]{:S(2)}) collective-permute-start(f32[344,256]{1,0:T(8,128)S(1)} %get-tuple-element.36), channel_id=1, source_target_pairs={{0,508},{4,8},{8,4},{12,16},{16,12},{20,24},{24,20},{28,32},{32,28... | collective-permute-start | bytes 1056776 | tf_op jit(solution)/shard_map/ppermute | solution.py:691
  23.8 0.0 copy-start.1
  23.8 0.7 copy-done.1
  24.5 0.8 middle.1
  25.4 7.3 %collective-permute-done.2.msg_a_ref = f32[344,256]{1,0:T(8,128)S(1)} collective-permute-done((f32[344,256]{1,0:T(8,128)S(1)}, f32[344,256]{1,0:T(8,128)S(1)}, u32[]{:S(2)}, u32[]{:S(2)}) %collective-permute-start.2) | collective-permute-done | bytes 352288 | tf_op jit(solution)/shard_map/ppermute | solution.py:690
  32.7 0.0 collective-permute-done.3.msg_b_ref
  32.7 2.7 %second.1 = (f32[4,2,16,256]{3,2,1,0:T(8,128)}, f32[32,256]{1,0:T(8,128)S(1)}, bf16[5,320,256]{2,1,0:T(8,128)(2,1)S(1)}, bf16[9,512,256]{2,1,0:T(8,128)(2,1)S(1)}, f32[9,3,8,256]{3,2,1,0:T(8,128)S(1)}) custom-call(s32[1]{0:T(128)} %bitcast.parity_ref, f32[160,256]{1,0:T(8,128)S(1)} %get-tuple-element.28.bout_ref, ...), custom_call_target="tpu_custom_call" | custom-call | tf_op jit(solution)/shard_map/second/pallas_call | solution.py:625
  35.4 5.3 %collective-permute-start.5 = (f32[32,256]{1,0:T(8,128)S(1)}, f32[32,256]{1,0:T(8,128)S(1)}, u32[]{:S(2)}, u32[]{:S(2)}) collective-permute-start(f32[32,256]{1,0:T(8,128)S(1)} %get-tuple-element.39.r_ref), channel_id=1, source_target_pairs={{0,4},{4,0},{8,12},{12,8},{16,20},{20,16},{24,28},{28,24},{32,36},... | collective-permute-start | bytes 98312 | tf_op jit(solution)/shard_map/ppermute | solution.py:695
  40.7 7.5 %collective-permute-start.4 = (f32[32,256]{1,0:T(8,128)S(1)}, f32[32,256]{1,0:T(8,128)S(1)}, u32[]{:S(2)}, u32[]{:S(2)}) collective-permute-start(f32[32,256]{1,0:T(8,128)S(1)} %get-tuple-element.39.r_ref), channel_id=1, source_target_pairs={{0,508},{4,8},{8,4},{12,16},{16,12},{20,24},{24,20},{28,32},{32,28... | collective-permute-start | bytes 98312 | tf_op jit(solution)/shard_map/ppermute | solution.py:696
  48.2 0.0 collective-permute-done.5.r_a_ref
  48.2 1.9 %collective-permute-done.4.r_b_ref = f32[32,256]{1,0:T(8,128)S(1)} collective-permute-done((f32[32,256]{1,0:T(8,128)S(1)}, f32[32,256]{1,0:T(8,128)S(1)}, u32[]{:S(2)}, u32[]{:S(2)}) %collective-permute-start.4) | collective-permute-done | bytes 32800 | tf_op jit(solution)/shard_map/ppermute | solution.py:696
  50.1 5.0 %third.1 = f32[16,128]{1,0:T(8,128)S(1)} custom-call(s32[1]{0:T(128)} %bitcast.parity_ref, f32[32,256]{1,0:T(8,128)S(1)} %get-tuple-element.39.r_ref, f32[32,256]{1,0:T(8,128)S(1)} %collective-permute-done.4.r_b_ref, f32[32,256]{1,0:T(8,128)S(1)} %collective-permute-done.5.r_a_ref, bf16[5,320,256]{2,1,0:T(8,128)(2,1)S(1)} %get-tuple-element.40.x1_ref, ...), custom_call_target="tpu_custom_call" | custom-call | tf_op jit(solution)/shard_map/third/pallas_call | solution.py:646
  55.1 8.0 %all_to_all.10 = f32[8,16,128]{2,1,0:T(8,128)S(1)} all-to-all(f32[8,16,128]{2,1,0:T(8,128)S(1)} %broadcast_in_dim.4), channel_id=1, replica_groups=mesh['zh'=4,'zl'=4,'x'=4,'yh'=2,'yl'=2,'c'=2] {'yh','yl','c'}, dimensions={0} | all-to-all | bytes 131072 | tf_op jit(solution)/shard_map/all_to_all | solution.py:666
  63.1 17.4 %all_to_all.11 = f32[16,16,128]{2,1,0:T(8,128)S(1)} all-to-all(f32[16,16,128]{2,1,0:T(8,128)S(1)} %broadcast_in_dim.5), channel_id=1, replica_groups=mesh['zh'=4,'zl'=4,'x'=4,'yh'=2,'yl'=2,'c'=2] {'zl','x'}, dimensions={0} | all-to-all | bytes 262144 | tf_op jit(solution)/shard_map/all_to_all | solution.py:666
  80.6 19.3 %psum.7.grads_ref = f32[16,128]{1,0:T(8,128)} all-reduce(f32[16,128]{1,0:T(8,128)S(1)} %reduce_sum.19), channel_id=1, replica_groups=mesh['zh'=4,'zl'=4,'x'=4,'yh'=2,'yl'=2,'c'=2] {'zh'}, use_global_device_ids=true, to_apply=%region_2.3 | all-reduce | flops 2048 | bytes 16384 | tf_op jit(solution)/shard_map/psum | solution.py:700
  99.8 1.4 %unpack.1 = (f32[19,32]{1,0:T(8,128)}, f32[1,32]{1,0:T(1,128)}, f32[19,32]{1,0:T(8,128)}, f32[1,19]{1,0:T(1,128)}) custom-call(f32[16,128]{1,0:T(8,128)} %psum.7.grads_ref), custom_call_target="tpu_custom_call" | custom-call | tf_op jit(solution)/shard_map/unpack/pallas_call | solution.py:596
  (4 shorter events, 0.0 us)
Async XLA Ops:
  0.6 1.1 %copy-start = (f32[19,2,16,256]{3,2,1,0:T(8,128)S(1)}, f32[19,2,16,256]{3,2,1,0:T(8,128)}, u32[]{:S(2)}) copy-start(f32[19,2,16,256]{3,2,1,0:T(8,128)} %pop_hbm.1) | copy-start | bytes 1867780
  1.9 7.9 %collective-permute-start = (f32[19,4,256]{2,1,0:T(4,128)S(1)}, f32[19,4,256]{2,1,0:T(4,128)S(1)}, u32[]{:S(2)}, u32[]{:S(2)}) collective-permute-start(f32[19,4,256]{2,1,0:T(4,128)S(1)} %get-tuple-element.30), channel_id=1, source_target_pairs={{0,1},{1,2},{2,3},{3,0},{4,5},{5,6},{6,7},{7,4},{8,9},{9,10},{10,1... | collective-permute-start | bytes 233480 | tf_op jit(solution)/shard_map/ppermute | solution.py:683
  3.9 5.9 %collective-permute-start.1 = (f32[19,4,256]{2,1,0:T(4,128)S(1)}, f32[19,4,256]{2,1,0:T(4,128)S(1)}, u32[]{:S(2)}, u32[]{:S(2)}) collective-permute-start(f32[19,4,256]{2,1,0:T(4,128)S(1)} %get-tuple-element.31), channel_id=1, source_target_pairs={{1,0},{2,1},{3,2},{0,3},{5,4},{6,5},{7,6},{4,7},{9,8},{10,9},{11,1... | collective-permute-start | bytes 233480 | tf_op jit(solution)/shard_map/ppermute | solution.py:684
  11.0 21.7 %collective-permute-start.2 = (f32[344,256]{1,0:T(8,128)S(1)}, f32[344,256]{1,0:T(8,128)S(1)}, u32[]{:S(2)}, u32[]{:S(2)}) collective-permute-start(f32[344,256]{1,0:T(8,128)S(1)} %get-tuple-element.35), channel_id=1, source_target_pairs={{0,4},{4,0},{8,12},{12,8},{16,20},{20,16},{24,28},{28,24},{32,36},... | collective-permute-start | bytes 1056776 | tf_op jit(solution)/shard_map/ppermute | solution.py:690
  16.2 16.5 %collective-permute-start.3 = (f32[344,256]{1,0:T(8,128)S(1)}, f32[344,256]{1,0:T(8,128)S(1)}, u32[]{:S(2)}, u32[]{:S(2)}) collective-permute-start(f32[344,256]{1,0:T(8,128)S(1)} %get-tuple-element.36), channel_id=1, source_target_pairs={{0,508},{4,8},{8,4},{12,16},{16,12},{20,24},{24,20},{28,32},{32,28... | collective-permute-start | bytes 1056776 | tf_op jit(solution)/shard_map/ppermute | solution.py:691
  23.8 0.8 copy-start.1
  35.4 12.8 %collective-permute-start.5 = (f32[32,256]{1,0:T(8,128)S(1)}, f32[32,256]{1,0:T(8,128)S(1)}, u32[]{:S(2)}, u32[]{:S(2)}) collective-permute-start(f32[32,256]{1,0:T(8,128)S(1)} %get-tuple-element.39.r_ref), channel_id=1, source_target_pairs={{0,4},{4,0},{8,12},{12,8},{16,20},{20,16},{24,28},{28,24},{32,36},... | collective-permute-start | bytes 98312 | tf_op jit(solution)/shard_map/ppermute | solution.py:695
  40.7 9.4 %collective-permute-start.4 = (f32[32,256]{1,0:T(8,128)S(1)}, f32[32,256]{1,0:T(8,128)S(1)}, u32[]{:S(2)}, u32[]{:S(2)}) collective-permute-start(f32[32,256]{1,0:T(8,128)S(1)} %get-tuple-element.39.r_ref), channel_id=1, source_target_pairs={{0,508},{4,8},{8,4},{12,16},{16,12},{20,24},{24,20},{28,32},{32,28... | collective-permute-start | bytes 98312 | tf_op jit(solution)/shard_map/ppermute | solution.py:696

commit v5 on v4

--- a/solution.py
+++ b/solution.py
@@ -221,21 +221,23 @@
     return pltpu.roll(x, step % NZ, 1)
 
 
-def edges_kernel(pop_hbm, last_ref, start_ref, pop_ref, sem):
+def edges_kernel(pop_hbm, near_ref, far_ref, pop_ref, sem):
     copy = pltpu.make_async_copy(pop_hbm, pop_ref, sem)
     copy.start()
     copy.wait()
+    odd = lax.axis_index("c") == 1
     for x in range(2):
-        last_ref[:, 2 * x : 2 * x + 2, :] = pop_ref[:, x, 14:16, :]
-        start_ref[:, 2 * x : 2 * x + 2, :] = pop_ref[:, x, 0:2, :]
+        last = pop_ref[:, x, 14:16, :]
+        start = pop_ref[:, x, 0:2, :]
+        near_ref[:, 2 * x : 2 * x + 2, :] = jnp.where(odd, start, last)
+        far_ref[:, 2 * x : 2 * x + 2, :] = jnp.where(odd, last, start)
 
 
 def first_kernel(
-    parity_ref,
     bout_ref,
     pop_ref,
-    before_ref,
-    after_ref,
+    far_ref,
+    near_ref,
     lin_ref,
     lout_ref,
     msg_a_ref,
@@ -245,10 +247,13 @@
     h1_ref,
     fs,
 ):
+    odd = lax.axis_index("c") == 1
     for x in range(2):
-        fs[:, W1 * x : W1 * x + 2, :] = before_ref[:, 2 * x : 2 * x + 2, :]
+        near = near_ref[:, 2 * x : 2 * x + 2, :]
+        far = far_ref[:, 2 * x : 2 * x + 2, :]
+        fs[:, W1 * x : W1 * x + 2, :] = jnp.where(odd, near, far)
         fs[:, W1 * x + 2 : W1 * x + 18, :] = pop_ref[:, x]
-        fs[:, W1 * x + 18 : W1 * x + 20, :] = after_ref[:, 2 * x : 2 * x + 2, :]
+        fs[:, W1 * x + 18 : W1 * x + 20, :] = jnp.where(odd, far, near)
     for batch in batches(G1, B1):
         f = [[fs[q, 8 * g : 8 * g + 8, :] for q in range(Q)] for g in batch]
 
@@ -264,7 +269,7 @@
         for g, out in zip(batch, outs):
             for q in range(Q):
                 c1_ref[q, 8 * g : 8 * g + 8, :] = zroll(out[q], velocity_table[q][2])
-    odd = parity_ref[0] == 1
+    odd = lax.axis_index("yh") == 1
 
     def piece(q, plane):
         start = W1 * (plane - velocity_table[q][0]) + 1 - velocity_table[q][1]
@@ -281,8 +286,26 @@
     msg_b_ref[W2 * Q :, :] = jnp.zeros((MSG - W2 * Q, NZ), F32)
 
 
+def streamed(c2, x, half):
+    f = []
+    for q in range(Q):
+        start = W2 * (x + 1) + 1 + 8 * half - W2 * velocity_table[q][0] - velocity_table[q][1]
+        f.append(c2[q, start : start + 8, :])
+    return f
+
+
+def moments_kernel(c2_ref, moments_ref, done_ref):
+    done_ref[...] = jnp.zeros_like(done_ref)
+    for x in range(2):
+        for half in range(2):
+            rows = slice(8 * half, 8 * half + 8)
+            density, m = equilibrium_parts(streamed(c2_ref, x, half))
+            moments_ref[0, x, rows, :] = density
+            for a in range(3):
+                moments_ref[a + 1, x, rows, :] = m[a]
+
+
 def second_kernel(
-    parity_ref,
     bout_ref,
     c1_ref,
     msg_a_ref,
@@ -290,15 +313,14 @@
     target_ref,
     lin_ref,
     lout_ref,
-    moments_ref,
     r_ref,
+    c2,
     x2_ref,
     h2_ref,
     m2_ref,
     a1,
-    c2,
 ):
-    odd = parity_ref[0] == 1
+    odd = lax.axis_index("yh") == 1
     for k in range(Q):
         rows = slice(W2 * k, W2 * k + W2)
         msg_a = msg_a_ref[rows, :]
@@ -334,21 +356,16 @@
     residual_scale = 1.0 / math.sqrt(256 * 64 * 256)
     for x in range(2):
         for half in range(2):
-            first = W2 * (x + 1) + 1 + 8 * half
-            f = []
-            for q in range(Q):
-                start = first - W2 * velocity_table[q][0] - velocity_table[q][1]
-                f.append(c2[q, start : start + 8, :])
-            density, m = equilibrium_parts(f)
-            moments_ref[0, x, 8 * half : 8 * half + 8, :] = density
-            for a in range(3):
-                moments_ref[a + 1, x, 8 * half : 8 * half + 8, :] = m[a]
+            f = streamed(c2, x, half)
+            density = f[0]
+            for q in range(1, Q):
+                density = density + f[q]
             r = (density - target_ref[x, 8 * half : 8 * half + 8, :]) * residual_scale
             r_ref[16 * x + 8 * half : 16 * x + 8 * half + 8, :] = r
 
 
 def third_kernel(
-    parity_ref,
+    _after_moments,
     r_ref,
     r_b_ref,
     r_a_ref,
@@ -366,7 +383,7 @@
     acc_out,
     acc_b,
 ):
-    odd = parity_ref[0] == 1
+    odd = lax.axis_index("yh") == 1
     rs[...] = jnp.zeros_like(rs)
     g1s[...] = jnp.zeros_like(g1s)
     acc_in[...] = jnp.zeros_like(acc_in)
@@ -529,14 +546,28 @@
     grads_ref[10:11, 0:20] = d_b
 
 
-def unpack_kernel(grads_ref, win_ref, bin_ref, woutt_ref, bout_ref):
+def unpack_kernel(
+    grads_ref, win_hbm, bin_hbm, woutt_hbm, bout_hbm, win_ref, bin_ref, woutt_ref, bout_ref, sems
+):
     g = grads_ref[...]
+    copies = []
+
+    def send(ref, hbm):
+        copies.append(pltpu.make_async_copy(ref, hbm, sems.at[len(copies)]))
+        copies[-1].start()
+
     win_ref[0:10, :] = g[0:10, 0:H]
     win_ref[10:Q, :] = g[0:9, H : 2 * H]
-    bin_ref[...] = g[9:10, H : 2 * H]
+    send(win_ref, win_hbm)
     woutt_ref[0:10, :] = g[0:10, 2 * H : 3 * H]
     woutt_ref[10:Q, :] = g[0:9, 3 * H : 4 * H]
+    send(woutt_ref, woutt_hbm)
+    bin_ref[...] = g[9:10, H : 2 * H]
+    send(bin_ref, bin_hbm)
     bout_ref[...] = g[10:11, 0:Q]
+    send(bout_ref, bout_hbm)
+    for c in copies:
+        c.wait()
 
 
 VMEM = pl.BlockSpec(memory_space=pltpu.VMEM)
@@ -597,13 +628,20 @@
         unpack_kernel,
         out_shape=(shape(Q, H), shape(1, H), shape(Q, H), shape(1, Q)),
         in_specs=[VMEM],
-        out_specs=(VMEM,) * 4,
+        out_specs=(HBM,) * 4,
+        scratch_shapes=[
+            pltpu.VMEM((Q, H), F32),
+            pltpu.VMEM((1, H), F32),
+            pltpu.VMEM((Q, H), F32),
+            pltpu.VMEM((1, Q), F32),
+            pltpu.SemaphoreType.DMA((4,)),
+        ],
         name="unpack",
     )(grads)
     return win, bin_.reshape(H), woutt.T, bout.reshape(Q)
 
 
-def first(parity, bias_out, populations, before, after, lin, lout):
+def first(bias_out, populations, far, near, lin, lout):
     return pl.pallas_call(
         first_kernel,
         out_shape=(
@@ -613,40 +651,48 @@
             shape(G1, 2 * QS, NZ, kind=BF16),
             shape(G1, 2 * HS, NZ, kind=BF16),
         ),
-        in_specs=[SMEM] + [VMEM] * 6,
+        in_specs=[VMEM] * 6,
         out_specs=(VMEM,) * 5,
         scratch_shapes=[pltpu.VMEM((Q, 2 * W1, NZ), F32)],
         compiler_params=pltpu.CompilerParams(vmem_limit_bytes=24 * MIB),
         name="first",
-    )(parity, bias_out, populations, before, after, lin, lout)
-
-
-def second(parity, bias_out, c1, msg_a, msg_b, target, lin, lout):
+    )(bias_out, populations, far, near, lin, lout)
+
+
+def second(bias_out, c1, msg_a, msg_b, target, lin, lout):
     return pl.pallas_call(
         second_kernel,
         out_shape=(
-            shape(4, 2, 16, NZ),
             shape(32, NZ),
+            shape(Q, 4 * W2, NZ),
             shape(PG[1] - PG[0], 2 * QS, NZ, kind=BF16),
             shape(G2, 2 * HS, NZ, kind=BF16),
             shape(G2, 3, SP, NZ),
         ),
-        in_specs=[SMEM] + [VMEM] * 7,
+        in_specs=[VMEM] * 7,
         out_specs=(VMEM,) * 5,
-        scratch_shapes=[
-            pltpu.VMEM((Q, 4 * W2, NZ), F32),
-            pltpu.VMEM((Q, 4 * W2, NZ), F32),
-        ],
+        scratch_shapes=[pltpu.VMEM((Q, 4 * W2, NZ), F32)],
         compiler_params=pltpu.CompilerParams(vmem_limit_bytes=24 * MIB),
         name="second",
-    )(parity, bias_out, c1, msg_a, msg_b, target, lin, lout)
-
-
-def third(parity, r, r_b, r_a, x1, h1, x2, h2, m2, lint, loutt):
+    )(bias_out, c1, msg_a, msg_b, target, lin, lout)
+
+
+def moments_of(c2):
+    return pl.pallas_call(
+        moments_kernel,
+        out_shape=(shape(4, 2, 16, NZ), shape(8, 128)),
+        in_specs=[VMEM],
+        out_specs=(VMEM,) * 2,
+        compiler_params=pltpu.CompilerParams(vmem_limit_bytes=8 * MIB),
+        name="moments",
+    )(c2)
+
+
+def third(done, r, r_b, r_a, x1, h1, x2, h2, m2, lint, loutt):
     return pl.pallas_call(
         third_kernel,
         out_shape=shape(16, 128),
-        in_specs=[SMEM] + [VMEM] * 10,
+        in_specs=[VMEM] * 11,
         out_specs=VMEM,
         scratch_shapes=[
             pltpu.VMEM((3, 2 * MARGIN + 6 * W2 + 4, NZ), F32),
@@ -657,7 +703,7 @@
         ],
         compiler_params=pltpu.CompilerParams(vmem_limit_bytes=24 * MIB),
         name="third",
-    )(parity, r, r_b, r_a, x1, h1, x2, h2, m2, lint, loutt)
+    )(done, r, r_b, r_a, x1, h1, x2, h2, m2, lint, loutt)
 
 
 def gather_sum(x, axes):
@@ -669,7 +715,7 @@
 def body(populations, target_density, weight_in, bias_in, weight_out, bias_out):
     gx, gy = ("zh", "zl", "x", "yh"), ("yl", "c")
     nx, ny = lax.axis_size(gx), lax.axis_size(gy)
-    last, start, pops = edges(populations)
+    near, far, pops = edges(populations)
     packed = jnp.concatenate(
         [
             weight_in,
@@ -680,24 +726,23 @@
         axis=0,
     )
     lin, lout, bout = prep(packed)
-    before = lax.ppermute(last, gy, [(j, (j + 1) % ny) for j in range(ny)])
-    after = lax.ppermute(start, gy, [((j + 1) % ny, j) for j in range(ny)])
+    got_near = lax.ppermute(near, gy, [(j, j ^ 1) for j in range(ny)])
+    got_far = lax.ppermute(far, gy, [(j, (j + 1) % ny if j % 2 else (j - 1) % ny) for j in range(ny)])
     pair = [(i, i ^ 1) for i in range(nx)]
     cross = [(i, (i + 1) % nx if i % 2 else (i - 1) % nx) for i in range(nx)]
-    parity = (lax.axis_index("yh") % 2).astype(jnp.int32).reshape(1)
-    msg_a, msg_b, c1, x1, h1 = first(parity, bout, pops, before, after, lin, lout)
+    msg_a, msg_b, c1, x1, h1 = first(bout, pops, got_far, got_near, lin, lout)
     lint, loutt, target = middle(c1, packed, target_density)
     got_a = lax.ppermute(msg_a, gx, pair)
     got_b = lax.ppermute(msg_b, gx, cross)
-    moments, r, x2, h2, m2 = second(
-        parity, bout, c1, got_a, got_b, target, lin, lout
+    r, c2, x2, h2, m2 = second(
+        bout, c1, got_a, got_b, target, lin, lout
     )
+    moments, done = moments_of(c2)
     r_a = lax.ppermute(r, gx, pair)
     r_b = lax.ppermute(r, gx, cross)
-    grads = third(parity, r, r_b, r_a, x1, h1, x2, h2, m2, lint, loutt)
-    grads = gather_sum(grads, ("yh", "yl", "c"))
-    grads = gather_sum(grads, ("zl", "x"))
-    grads = lax.psum(grads, "zh")
+    grads = third(done, r, r_b, r_a, x1, h1, x2, h2, m2, lint, loutt)
+    grads = gather_sum(grads, ("x", "yh", "yl", "c"))
+    grads = gather_sum(grads, ("zh", "zl"))
     return (moments, *unpack(grads))
 
 

time: 102 us -> 98.9 us (0.970)
  the two profiles are of different devices: /device:TPU:2 before, /device:TPU:1 now
where the time goes in v5:
time: 98.9 us; the launch traced here: 97.7 us
  blocking collectives  37.2 us (38%)
  starting transfers between devices  36.8 us (37%)
  Pallas kernels  12.3 us (12%)
  waiting for transfers between devices  7.4 us (7%)
  local copies, waits for them, and re-layouts  1.77 us (2%)
  other arithmetic  1.4 us (1%)
    all_to_all x2, blocking collectives, gather_sum(): return jnp.sum(lax.all_to_all(copies, axes, 0, 0, tiled=True), axis=0)  37.2 us
    ppermute x1, starting transfers between devices, body(): got_b = lax.ppermute(msg_b, gx, cross)  11.8 us
    ppermute x1, starting transfers between devices, body(): r_b = lax.ppermute(r, gx, cross)  10.5 us
    ppermute x1, starting transfers between devices, body(): got_near = lax.ppermute(near, gy, [(j, j ^ 1) for j in range(ny)])  6.11 us
    pallas_call x1, Pallas kernels, third(): pl.pallas_call(third_kernel, out_shape=shape(16, 128), in_specs=[VMEM] *...  4.82 us
    ppermute x1, starting transfers between devices, body(): lax.ppermute(far, gy, [(j, (j + 1) % ny if j % 2 else (j - 1) % ny) for j...  4.59 us
    ppermute x1, waiting for transfers between devices, body(): got_b = lax.ppermute(msg_b, gx, cross)  4.25 us
    ppermute x1, waiting for transfers between devices, body(): got_a = lax.ppermute(msg_a, gx, pair)  2.72 us
  transfers between devices with their start and end apart: 6, of which 3 were waited for; matrix products, arithmetic and copies ran while one was open for 1% of the time, Pallas kernels for 3%

profile of v5, /device:TPU:1, one launch (start us, length us, event | category | flops | bytes accessed | tf_op | source)
XLA Modules:
  0.0 97.7 jit_solution(12687584118241462927)
XLA Ops:
  0.6 0.0 copy-start
  0.6 1.1 %copy-done = f32[19,2,16,256]{3,2,1,0:T(8,128)S(1)} copy-done((f32[19,2,16,256]{3,2,1,0:T(8,128)S(1)}, f32[19,2,16,256]{3,2,1,0:T(8,128)}, u32[]{:S(2)}) %copy-start) | copy-done | bytes 622616
  1.7 0.0 copy-start.1
  1.7 0.2 edges.1
  2.0 4.6 %collective-permute-start = (f32[19,4,256]{2,1,0:T(4,128)S(1)}, f32[19,4,256]{2,1,0:T(4,128)S(1)}, u32[]{:S(2)}, u32[]{:S(2)}) collective-permute-start(f32[19,4,256]{2,1,0:T(4,128)S(1)} %get-tuple-element.32), channel_id=1, source_target_pairs={{0,3},{1,2},{2,1},{3,0},{4,7},{5,6},{6,5},{7,4},{8,11},{9,10},{10,... | collective-permute-start | bytes 233480 | tf_op jit(solution)/shard_map/ppermute | solution.py:730
  6.6 6.1 %collective-permute-start.1 = (f32[19,4,256]{2,1,0:T(4,128)S(1)}, f32[19,4,256]{2,1,0:T(4,128)S(1)}, u32[]{:S(2)}, u32[]{:S(2)}) collective-permute-start(f32[19,4,256]{2,1,0:T(4,128)S(1)} %get-tuple-element.33), channel_id=1, source_target_pairs={{0,1},{1,0},{2,3},{3,2},{4,5},{5,4},{6,7},{7,6},{8,9},{9,8},{10,11... | collective-permute-start | bytes 233480 | tf_op jit(solution)/shard_map/ppermute | solution.py:729
  12.7 0.7 pad_bitcast_fusion
  13.3 0.7 pad_maximum_fusion.packed_ref
  14.1 0.8 prep.1
  14.9 0.0 collective-permute-done.far_ref
  15.0 0.0 collective-permute-done.1.near_ref
  15.0 1.3 %first.1 = (f32[344,256]{1,0:T(8,128)S(1)}, f32[344,256]{1,0:T(8,128)S(1)}, f32[19,40,256]{2,1,0:T(8,128)S(1)}, bf16[5,320,256]{2,1,0:T(8,128)(2,1)S(1)}, bf16[5,512,256]{2,1,0:T(8,128)(2,1)S(1)}) custom-call(f32[160,256]{1,0:T(8,128)S(1)} %get-tuple-element.30.bout_ref, f32[19,2,16,256]{3,2,1,0:T(8,128)S(1)} %get-tuple-element.31.pop_ref, ...), custom_call_target="tpu_custom_call" | custom-call | tf_op jit(solution)/shard_map/first/pallas_call | solution.py:645
  16.2 1.9 %collective-permute-start.2 = (f32[344,256]{1,0:T(8,128)S(1)}, f32[344,256]{1,0:T(8,128)S(1)}, u32[]{:S(2)}, u32[]{:S(2)}) collective-permute-start(f32[344,256]{1,0:T(8,128)S(1)} %get-tuple-element.37), channel_id=1, source_target_pairs={{0,4},{4,0},{8,12},{12,8},{16,20},{20,16},{24,28},{28,24},{32,36},... | collective-permute-start | bytes 1056776 | tf_op jit(solution)/shard_map/ppermute | solution.py:735
  18.2 11.8 %collective-permute-start.3 = (f32[344,256]{1,0:T(8,128)S(1)}, f32[344,256]{1,0:T(8,128)S(1)}, u32[]{:S(2)}, u32[]{:S(2)}) collective-permute-start(f32[344,256]{1,0:T(8,128)S(1)} %get-tuple-element.38), channel_id=1, source_target_pairs={{0,508},{4,8},{8,4},{12,16},{16,12},{20,24},{24,20},{28,32},{32,28... | collective-permute-start | bytes 1056776 | tf_op jit(solution)/shard_map/ppermute | solution.py:736
  30.0 0.0 copy-done.1
  30.0 0.8 middle.1
  30.8 2.7 %collective-permute-done.2.msg_a_ref = f32[344,256]{1,0:T(8,128)S(1)} collective-permute-done((f32[344,256]{1,0:T(8,128)S(1)}, f32[344,256]{1,0:T(8,128)S(1)}, u32[]{:S(2)}, u32[]{:S(2)}) %collective-permute-start.2) | collective-permute-done | bytes 352288 | tf_op jit(solution)/shard_map/ppermute | solution.py:735
  33.5 4.3 %collective-permute-done.3.msg_b_ref = f32[344,256]{1,0:T(8,128)S(1)} collective-permute-done((f32[344,256]{1,0:T(8,128)S(1)}, f32[344,256]{1,0:T(8,128)S(1)}, u32[]{:S(2)}, u32[]{:S(2)}) %collective-permute-start.3) | collective-permute-done | bytes 352288 | tf_op jit(solution)/shard_map/ppermute | solution.py:736
  37.8 2.0 %second.1 = (f32[32,256]{1,0:T(8,128)S(1)}, f32[19,72,256]{2,1,0:T(8,128)S(1)}, bf16[5,320,256]{2,1,0:T(8,128)(2,1)S(1)}, bf16[9,512,256]{2,1,0:T(8,128)(2,1)S(1)}, f32[9,3,8,256]{3,2,1,0:T(8,128)S(1)}) custom-call(f32[160,256]{1,0:T(8,128)S(1)} %get-tuple-element.30.bout_ref, f32[19,40,256]{2,1,0:T(8,128)S(1)} %get-tuple-element.36.after_first.c1_ref, ...), custom_call_target="tpu_custom_call" | custom-call | tf_op jit(solution)/shard_map/second/pallas_call | solution.py:663
  39.8 1.9 %collective-permute-start.5 = (f32[32,256]{1,0:T(8,128)S(1)}, f32[32,256]{1,0:T(8,128)S(1)}, u32[]{:S(2)}, u32[]{:S(2)}) collective-permute-start(f32[32,256]{1,0:T(8,128)S(1)} %get-tuple-element.43.r_ref), channel_id=1, source_target_pairs={{0,4},{4,0},{8,12},{12,8},{16,20},{20,16},{24,28},{28,24},{32,36},... | collective-permute-start | bytes 98312 | tf_op jit(solution)/shard_map/ppermute | solution.py:741
  41.8 10.5 %collective-permute-start.4 = (f32[32,256]{1,0:T(8,128)S(1)}, f32[32,256]{1,0:T(8,128)S(1)}, u32[]{:S(2)}, u32[]{:S(2)}) collective-permute-start(f32[32,256]{1,0:T(8,128)S(1)} %get-tuple-element.43.r_ref), channel_id=1, source_target_pairs={{0,508},{4,8},{8,4},{12,16},{16,12},{20,24},{24,20},{28,32},{32,28... | collective-permute-start | bytes 98312 | tf_op jit(solution)/shard_map/ppermute | solution.py:742
  52.3 0.9 moments.1
  53.1 0.0 collective-permute-done.5.r_a_ref
  53.1 0.4 collective-permute-done.4.r_b_ref
  53.6 4.8 %third.1 = f32[16,128]{1,0:T(8,128)S(1)} custom-call(f32[8,128]{1,0:T(8,128)S(1)} %get-tuple-element.42._after_moments, f32[32,256]{1,0:T(8,128)S(1)} %get-tuple-element.43.r_ref, f32[32,256]{1,0:T(8,128)S(1)} %collective-permute-done.4.r_b_ref, f32[32,256]{1,0:T(8,128)S(1)} %collective-permute-done.5.r_a_ref, ...), custom_call_target="tpu_custom_call" | custom-call | tf_op jit(solution)/shard_map/third/pallas_call | solution.py:692
  58.4 14.2 %all_to_all.10 = f32[32,16,128]{2,1,0:T(8,128)S(1)} all-to-all(f32[32,16,128]{2,1,0:T(8,128)S(1)} %broadcast_in_dim.4), channel_id=1, replica_groups=mesh['zh'=4,'zl'=4,'x'=4,'yh'=2,'yl'=2,'c'=2] {'x','yh','yl','c'}, dimensions={0} | all-to-all | bytes 524288 | tf_op jit(solution)/shard_map/all_to_all | solution.py:712
  72.7 22.9 %all_to_all.11 = f32[16,16,128]{2,1,0:T(8,128)S(1)} all-to-all(f32[16,16,128]{2,1,0:T(8,128)S(1)} %broadcast_in_dim.5), channel_id=1, replica_groups=mesh['zh'=4,'zl'=4,'x'=4,'yh'=2,'yl'=2,'c'=2] {'zh','zl'}, dimensions={0} | all-to-all | bytes 262144 | tf_op jit(solution)/shard_map/all_to_all | solution.py:712
  95.6 0.6 reduce_sum.19.grads_ref
  96.3 1.4 %unpack.1 = (f32[19,32]{1,0:T(8,128)}, f32[1,32]{1,0:T(1,128)}, f32[19,32]{1,0:T(8,128)}, f32[1,19]{1,0:T(1,128)}) custom-call(f32[16,128]{1,0:T(8,128)} %reduce_sum.19.grads_ref), custom_call_target="tpu_custom_call" | custom-call | tf_op jit(solution)/shard_map/unpack/pallas_call | solution.py:627
  (3 shorter events, 0.1 us)
Async XLA Ops:
  0.6 1.1 %copy-start = (f32[19,2,16,256]{3,2,1,0:T(8,128)S(1)}, f32[19,2,16,256]{3,2,1,0:T(8,128)}, u32[]{:S(2)}) copy-start(f32[19,2,16,256]{3,2,1,0:T(8,128)} %pop_hbm.1) | copy-start | bytes 1867780
  1.7 28.3 %copy-start.1 = (f32[2,16,256]{2,1,0:T(8,128)S(1)}, f32[2,16,256]{2,1,0:T(8,128)}, u32[]{:S(2)}) copy-start(f32[2,16,256]{2,1,0:T(8,128)} %target_in.1) | copy-start | bytes 98308
  2.0 13.0 %collective-permute-start = (f32[19,4,256]{2,1,0:T(4,128)S(1)}, f32[19,4,256]{2,1,0:T(4,128)S(1)}, u32[]{:S(2)}, u32[]{:S(2)}) collective-permute-start(f32[19,4,256]{2,1,0:T(4,128)S(1)} %get-tuple-element.32), channel_id=1, source_target_pairs={{0,3},{1,2},{2,1},{3,0},{4,7},{5,6},{6,5},{7,4},{8,11},{9,10},{10,... | collective-permute-start | bytes 233480 | tf_op jit(solution)/shard_map/ppermute | solution.py:730
  6.6 8.4 %collective-permute-start.1 = (f32[19,4,256]{2,1,0:T(4,128)S(1)}, f32[19,4,256]{2,1,0:T(4,128)S(1)}, u32[]{:S(2)}, u32[]{:S(2)}) collective-permute-start(f32[19,4,256]{2,1,0:T(4,128)S(1)} %get-tuple-element.33), channel_id=1, source_target_pairs={{0,1},{1,0},{2,3},{3,2},{4,5},{5,4},{6,7},{7,6},{8,9},{9,8},{10,11... | collective-permute-start | bytes 233480 | tf_op jit(solution)/shard_map/ppermute | solution.py:729
  16.2 17.3 %collective-permute-start.2 = (f32[344,256]{1,0:T(8,128)S(1)}, f32[344,256]{1,0:T(8,128)S(1)}, u32[]{:S(2)}, u32[]{:S(2)}) collective-permute-start(f32[344,256]{1,0:T(8,128)S(1)} %get-tuple-element.37), channel_id=1, source_target_pairs={{0,4},{4,0},{8,12},{12,8},{16,20},{20,16},{24,28},{28,24},{32,36},... | collective-permute-start | bytes 1056776 | tf_op jit(solution)/shard_map/ppermute | solution.py:735
  18.2 19.6 %collective-permute-start.3 = (f32[344,256]{1,0:T(8,128)S(1)}, f32[344,256]{1,0:T(8,128)S(1)}, u32[]{:S(2)}, u32[]{:S(2)}) collective-permute-start(f32[344,256]{1,0:T(8,128)S(1)} %get-tuple-element.38), channel_id=1, source_target_pairs={{0,508},{4,8},{8,4},{12,16},{16,12},{20,24},{24,20},{28,32},{32,28... | collective-permute-start | bytes 1056776 | tf_op jit(solution)/shard_map/ppermute | solution.py:736
  39.8 13.3 %collective-permute-start.5 = (f32[32,256]{1,0:T(8,128)S(1)}, f32[32,256]{1,0:T(8,128)S(1)}, u32[]{:S(2)}, u32[]{:S(2)}) collective-permute-start(f32[32,256]{1,0:T(8,128)S(1)} %get-tuple-element.43.r_ref), channel_id=1, source_target_pairs={{0,4},{4,0},{8,12},{12,8},{16,20},{20,16},{24,28},{28,24},{32,36},... | collective-permute-start | bytes 98312 | tf_op jit(solution)/shard_map/ppermute | solution.py:741
  41.8 11.8 %collective-permute-start.4 = (f32[32,256]{1,0:T(8,128)S(1)}, f32[32,256]{1,0:T(8,128)S(1)}, u32[]{:S(2)}, u32[]{:S(2)}) collective-permute-start(f32[32,256]{1,0:T(8,128)S(1)} %get-tuple-element.43.r_ref), channel_id=1, source_target_pairs={{0,508},{4,8},{8,4},{12,16},{16,12},{20,24},{24,20},{28,32},{32,28... | collective-permute-start | bytes 98312 | tf_op jit(solution)/shard_map/ppermute | solution.py:742

commit v6 on v5

--- a/solution.py
+++ b/solution.py
@@ -367,8 +367,8 @@
 def third_kernel(
     _after_moments,
     r_ref,
+    r_a_ref,
     r_b_ref,
-    r_a_ref,
     x1_ref,
     h1_ref,
     x2_ref,
@@ -688,7 +688,7 @@
     )(c2)
 
 
-def third(done, r, r_b, r_a, x1, h1, x2, h2, m2, lint, loutt):
+def third(done, r, r_a, r_b, x1, h1, x2, h2, m2, lint, loutt):
     return pl.pallas_call(
         third_kernel,
         out_shape=shape(16, 128),
@@ -703,7 +703,7 @@
         ],
         compiler_params=pltpu.CompilerParams(vmem_limit_bytes=24 * MIB),
         name="third",
-    )(done, r, r_b, r_a, x1, h1, x2, h2, m2, lint, loutt)
+    )(done, r, r_a, r_b, x1, h1, x2, h2, m2, lint, loutt)
 
 
 def gather_sum(x, axes):
@@ -721,7 +721,7 @@
             weight_in,
             bias_in.reshape(1, H),
             weight_out.T,
-            jnp.pad(bias_out, (0, H - Q)).reshape(1, H),
+            jnp.pad(bias_out.reshape(1, Q), ((0, 0), (0, H - Q))),
         ],
         axis=0,
     )
@@ -740,7 +740,7 @@
     moments, done = moments_of(c2)
     r_a = lax.ppermute(r, gx, pair)
     r_b = lax.ppermute(r, gx, cross)
-    grads = third(done, r, r_b, r_a, x1, h1, x2, h2, m2, lint, loutt)
+    grads = third(done, r, r_a, r_b, x1, h1, x2, h2, m2, lint, loutt)
     grads = gather_sum(grads, ("x", "yh", "yl", "c"))
     grads = gather_sum(grads, ("zh", "zl"))
     return (moments, *unpack(grads))

time: 98.9 us -> 96.4 us (0.975)
  blocking collectives: 37.2 us -> 32.7 us
  waiting for transfers between devices: 7.4 us -> 10.3 us
    all_to_all x2, blocking collectives: 37.2 us -> 32.7 us  [gather_sum(): return jnp.sum(lax.all_to_all(copies, axes, 0, 0, tiled=True), axis=0)]
    ppermute x1, waiting for transfers between devices: 0.01 us -> 3.37 us  [body(): r_a = lax.ppermute(r, gx, pair)]
where the time goes in v6:
time: 96.4 us; the launch traced here: 95.1 us
  starting transfers between devices  36.5 us (38%)
  blocking collectives  32.7 us (34%)
  Pallas kernels  12.3 us (13%)
  waiting for transfers between devices  10.3 us (11%)
  other arithmetic  1.42 us (1%)
  local copies, waits for them, and re-layouts  1.11 us (1%)
    all_to_all x2, blocking collectives, gather_sum(): return jnp.sum(lax.all_to_all(copies, axes, 0, 0, tiled=True), axis=0)  32.7 us
    ppermute x1, starting transfers between devices, body(): got_b = lax.ppermute(msg_b, gx, cross)  11.8 us
    ppermute x1, starting transfers between devices, body(): r_b = lax.ppermute(r, gx, cross)  10.2 us
    ppermute x1, starting transfers between devices, body(): got_near = lax.ppermute(near, gy, [(j, j ^ 1) for j in range(ny)])  6.11 us
    pallas_call x1, Pallas kernels, third(): pl.pallas_call(third_kernel, out_shape=shape(16, 128), in_specs=[VMEM] *...  4.82 us
    ppermute x1, starting transfers between devices, body(): lax.ppermute(far, gy, [(j, (j + 1) % ny if j % 2 else (j - 1) % ny) for j...  4.59 us
    ppermute x1, waiting for transfers between devices, body(): got_b = lax.ppermute(msg_b, gx, cross)  4.37 us
    ppermute x1, waiting for transfers between devices, body(): r_a = lax.ppermute(r, gx, pair)  3.37 us
  transfers between devices with their start and end apart: 6, of which 3 were waited for; matrix products, arithmetic and copies ran while one was open for 1% of the time, Pallas kernels for 3%

profile of v6, /device:TPU:1, one launch (start us, length us, event | category | flops | bytes accessed | tf_op | source)
XLA Modules:
  0.0 95.1 jit_solution(15281667820010568621)
XLA Ops:
  0.6 0.0 copy-start
  0.6 1.1 %copy-done = f32[19,2,16,256]{3,2,1,0:T(8,128)S(1)} copy-done((f32[19,2,16,256]{3,2,1,0:T(8,128)S(1)}, f32[19,2,16,256]{3,2,1,0:T(8,128)}, u32[]{:S(2)}) %copy-start) | copy-done | bytes 622616
  1.7 0.0 copy-start.1
  1.7 0.2 edges.1
  2.0 4.6 %collective-permute-start = (f32[19,4,256]{2,1,0:T(4,128)S(1)}, f32[19,4,256]{2,1,0:T(4,128)S(1)}, u32[]{:S(2)}, u32[]{:S(2)}) collective-permute-start(f32[19,4,256]{2,1,0:T(4,128)S(1)} %get-tuple-element.32), channel_id=1, source_target_pairs={{0,3},{1,2},{2,1},{3,0},{4,7},{5,6},{6,5},{7,4},{8,11},{9,10},{10,... | collective-permute-start | bytes 233480 | tf_op jit(solution)/shard_map/ppermute | solution.py:730
  6.6 6.1 %collective-permute-start.1 = (f32[19,4,256]{2,1,0:T(4,128)S(1)}, f32[19,4,256]{2,1,0:T(4,128)S(1)}, u32[]{:S(2)}, u32[]{:S(2)}) collective-permute-start(f32[19,4,256]{2,1,0:T(4,128)S(1)} %get-tuple-element.33), channel_id=1, source_target_pairs={{0,1},{1,0},{2,3},{3,2},{4,5},{5,4},{6,7},{7,6},{8,9},{9,8},{10,11... | collective-permute-start | bytes 233480 | tf_op jit(solution)/shard_map/ppermute | solution.py:729
  12.7 0.8 select_maximum_fusion.packed_ref
  13.5 0.8 prep.1
  14.3 0.0 collective-permute-done.far_ref
  14.3 0.0 collective-permute-done.1.near_ref
  14.3 1.3 %first.1 = (f32[344,256]{1,0:T(8,128)S(1)}, f32[344,256]{1,0:T(8,128)S(1)}, f32[19,40,256]{2,1,0:T(8,128)S(1)}, bf16[5,320,256]{2,1,0:T(8,128)(2,1)S(1)}, bf16[5,512,256]{2,1,0:T(8,128)(2,1)S(1)}) custom-call(f32[160,256]{1,0:T(8,128)S(1)} %get-tuple-element.30.bout_ref, f32[19,2,16,256]{3,2,1,0:T(8,128)S(1)} %get-tuple-element.31.pop_ref, ...), custom_call_target="tpu_custom_call" | custom-call | tf_op jit(solution)/shard_map/first/pallas_call | solution.py:645
  15.6 1.9 %collective-permute-start.2 = (f32[344,256]{1,0:T(8,128)S(1)}, f32[344,256]{1,0:T(8,128)S(1)}, u32[]{:S(2)}, u32[]{:S(2)}) collective-permute-start(f32[344,256]{1,0:T(8,128)S(1)} %get-tuple-element.37), channel_id=1, source_target_pairs={{0,4},{4,0},{8,12},{12,8},{16,20},{20,16},{24,28},{28,24},{32,36},... | collective-permute-start | bytes 1056776 | tf_op jit(solution)/shard_map/ppermute | solution.py:735
  17.5 11.8 %collective-permute-start.3 = (f32[344,256]{1,0:T(8,128)S(1)}, f32[344,256]{1,0:T(8,128)S(1)}, u32[]{:S(2)}, u32[]{:S(2)}) collective-permute-start(f32[344,256]{1,0:T(8,128)S(1)} %get-tuple-element.38), channel_id=1, source_target_pairs={{0,508},{4,8},{8,4},{12,16},{16,12},{20,24},{24,20},{28,32},{32,28... | collective-permute-start | bytes 1056776 | tf_op jit(solution)/shard_map/ppermute | solution.py:736
  29.3 0.0 copy-done.1
  29.3 0.9 middle.1
  30.2 2.6 %collective-permute-done.2.msg_a_ref = f32[344,256]{1,0:T(8,128)S(1)} collective-permute-done((f32[344,256]{1,0:T(8,128)S(1)}, f32[344,256]{1,0:T(8,128)S(1)}, u32[]{:S(2)}, u32[]{:S(2)}) %collective-permute-start.2) | collective-permute-done | bytes 352288 | tf_op jit(solution)/shard_map/ppermute | solution.py:735
  32.8 4.4 %collective-permute-done.3.msg_b_ref = f32[344,256]{1,0:T(8,128)S(1)} collective-permute-done((f32[344,256]{1,0:T(8,128)S(1)}, f32[344,256]{1,0:T(8,128)S(1)}, u32[]{:S(2)}, u32[]{:S(2)}) %collective-permute-start.3) | collective-permute-done | bytes 352288 | tf_op jit(solution)/shard_map/ppermute | solution.py:736
  37.1 2.0 %second.1 = (f32[32,256]{1,0:T(8,128)S(1)}, f32[19,72,256]{2,1,0:T(8,128)S(1)}, bf16[5,320,256]{2,1,0:T(8,128)(2,1)S(1)}, bf16[9,512,256]{2,1,0:T(8,128)(2,1)S(1)}, f32[9,3,8,256]{3,2,1,0:T(8,128)S(1)}) custom-call(f32[160,256]{1,0:T(8,128)S(1)} %get-tuple-element.30.bout_ref, f32[19,40,256]{2,1,0:T(8,128)S(1)} %get-tuple-element.36.after_first.c1_ref, ...), custom_call_target="tpu_custom_call" | custom-call | tf_op jit(solution)/shard_map/second/pallas_call | solution.py:663
  39.2 10.2 %collective-permute-start.5 = (f32[32,256]{1,0:T(8,128)S(1)}, f32[32,256]{1,0:T(8,128)S(1)}, u32[]{:S(2)}, u32[]{:S(2)}) collective-permute-start(f32[32,256]{1,0:T(8,128)S(1)} %get-tuple-element.43.r_ref), channel_id=1, source_target_pairs={{0,508},{4,8},{8,4},{12,16},{16,12},{20,24},{24,20},{28,32},{32,28... | collective-permute-start | bytes 98312 | tf_op jit(solution)/shard_map/ppermute | solution.py:742
  49.4 1.9 %collective-permute-start.4 = (f32[32,256]{1,0:T(8,128)S(1)}, f32[32,256]{1,0:T(8,128)S(1)}, u32[]{:S(2)}, u32[]{:S(2)}) collective-permute-start(f32[32,256]{1,0:T(8,128)S(1)} %get-tuple-element.43.r_ref), channel_id=1, source_target_pairs={{0,4},{4,0},{8,12},{12,8},{16,20},{20,16},{24,28},{28,24},{32,36},... | collective-permute-start | bytes 98312 | tf_op jit(solution)/shard_map/ppermute | solution.py:741
  51.3 0.9 moments.1
  52.2 0.0 collective-permute-done.5.r_b_ref
  52.2 3.4 %collective-permute-done.4.r_a_ref = f32[32,256]{1,0:T(8,128)S(1)} collective-permute-done((f32[32,256]{1,0:T(8,128)S(1)}, f32[32,256]{1,0:T(8,128)S(1)}, u32[]{:S(2)}, u32[]{:S(2)}) %collective-permute-start.4) | collective-permute-done | bytes 32800 | tf_op jit(solution)/shard_map/ppermute | solution.py:741
  55.5 4.8 %third.1 = f32[16,128]{1,0:T(8,128)S(1)} custom-call(f32[8,128]{1,0:T(8,128)S(1)} %get-tuple-element.42._after_moments, f32[32,256]{1,0:T(8,128)S(1)} %get-tuple-element.43.r_ref, f32[32,256]{1,0:T(8,128)S(1)} %collective-permute-done.4.r_a_ref, f32[32,256]{1,0:T(8,128)S(1)} %collective-permute-done.5.r_b_ref, ...), custom_call_target="tpu_custom_call" | custom-call | tf_op jit(solution)/shard_map/third/pallas_call | solution.py:692
  60.4 14.5 %all_to_all.10 = f32[32,16,128]{2,1,0:T(8,128)S(1)} all-to-all(f32[32,16,128]{2,1,0:T(8,128)S(1)} %broadcast_in_dim.4), channel_id=1, replica_groups=mesh['zh'=4,'zl'=4,'x'=4,'yh'=2,'yl'=2,'c'=2] {'x','yh','yl','c'}, dimensions={0} | all-to-all | bytes 524288 | tf_op jit(solution)/shard_map/all_to_all | solution.py:712
  74.9 18.2 %all_to_all.11 = f32[16,16,128]{2,1,0:T(8,128)S(1)} all-to-all(f32[16,16,128]{2,1,0:T(8,128)S(1)} %broadcast_in_dim.5), channel_id=1, replica_groups=mesh['zh'=4,'zl'=4,'x'=4,'yh'=2,'yl'=2,'c'=2] {'zh','zl'}, dimensions={0} | all-to-all | bytes 262144 | tf_op jit(solution)/shard_map/all_to_all | solution.py:712
  93.1 0.6 reduce_sum.19.grads_ref
  93.7 1.4 %unpack.1 = (f32[19,32]{1,0:T(8,128)}, f32[1,32]{1,0:T(1,128)}, f32[19,32]{1,0:T(8,128)}, f32[1,19]{1,0:T(1,128)}) custom-call(f32[16,128]{1,0:T(8,128)} %reduce_sum.19.grads_ref), custom_call_target="tpu_custom_call" | custom-call | tf_op jit(solution)/shard_map/unpack/pallas_call | solution.py:627
  (3 shorter events, 0.1 us)
Async XLA Ops:
  0.6 1.1 %copy-start = (f32[19,2,16,256]{3,2,1,0:T(8,128)S(1)}, f32[19,2,16,256]{3,2,1,0:T(8,128)}, u32[]{:S(2)}) copy-start(f32[19,2,16,256]{3,2,1,0:T(8,128)} %pop_hbm.1) | copy-start | bytes 1867780
  1.7 27.6 %copy-start.1 = (f32[2,16,256]{2,1,0:T(8,128)S(1)}, f32[2,16,256]{2,1,0:T(8,128)}, u32[]{:S(2)}) copy-start(f32[2,16,256]{2,1,0:T(8,128)} %target_in.1) | copy-start | bytes 98308
  2.0 12.3 %collective-permute-start = (f32[19,4,256]{2,1,0:T(4,128)S(1)}, f32[19,4,256]{2,1,0:T(4,128)S(1)}, u32[]{:S(2)}, u32[]{:S(2)}) collective-permute-start(f32[19,4,256]{2,1,0:T(4,128)S(1)} %get-tuple-element.32), channel_id=1, source_target_pairs={{0,3},{1,2},{2,1},{3,0},{4,7},{5,6},{6,5},{7,4},{8,11},{9,10},{10,... | collective-permute-start | bytes 233480 | tf_op jit(solution)/shard_map/ppermute | solution.py:730
  6.6 7.8 %collective-permute-start.1 = (f32[19,4,256]{2,1,0:T(4,128)S(1)}, f32[19,4,256]{2,1,0:T(4,128)S(1)}, u32[]{:S(2)}, u32[]{:S(2)}) collective-permute-start(f32[19,4,256]{2,1,0:T(4,128)S(1)} %get-tuple-element.33), channel_id=1, source_target_pairs={{0,1},{1,0},{2,3},{3,2},{4,5},{5,4},{6,7},{7,6},{8,9},{9,8},{10,11... | collective-permute-start | bytes 233480 | tf_op jit(solution)/shard_map/ppermute | solution.py:729
  15.6 17.2 %collective-permute-start.2 = (f32[344,256]{1,0:T(8,128)S(1)}, f32[344,256]{1,0:T(8,128)S(1)}, u32[]{:S(2)}, u32[]{:S(2)}) collective-permute-start(f32[344,256]{1,0:T(8,128)S(1)} %get-tuple-element.37), channel_id=1, source_target_pairs={{0,4},{4,0},{8,12},{12,8},{16,20},{20,16},{24,28},{28,24},{32,36},... | collective-permute-start | bytes 1056776 | tf_op jit(solution)/shard_map/ppermute | solution.py:735
  17.5 19.6 %collective-permute-start.3 = (f32[344,256]{1,0:T(8,128)S(1)}, f32[344,256]{1,0:T(8,128)S(1)}, u32[]{:S(2)}, u32[]{:S(2)}) collective-permute-start(f32[344,256]{1,0:T(8,128)S(1)} %get-tuple-element.38), channel_id=1, source_target_pairs={{0,508},{4,8},{8,4},{12,16},{16,12},{20,24},{24,20},{28,32},{32,28... | collective-permute-start | bytes 1056776 | tf_op jit(solution)/shard_map/ppermute | solution.py:736
  39.2 13.0 %collective-permute-start.5 = (f32[32,256]{1,0:T(8,128)S(1)}, f32[32,256]{1,0:T(8,128)S(1)}, u32[]{:S(2)}, u32[]{:S(2)}) collective-permute-start(f32[32,256]{1,0:T(8,128)S(1)} %get-tuple-element.43.r_ref), channel_id=1, source_target_pairs={{0,508},{4,8},{8,4},{12,16},{16,12},{20,24},{24,20},{28,32},{32,28... | collective-permute-start | bytes 98312 | tf_op jit(solution)/shard_map/ppermute | solution.py:742
  49.4 6.2 %collective-permute-start.4 = (f32[32,256]{1,0:T(8,128)S(1)}, f32[32,256]{1,0:T(8,128)S(1)}, u32[]{:S(2)}, u32[]{:S(2)}) collective-permute-start(f32[32,256]{1,0:T(8,128)S(1)} %get-tuple-element.43.r_ref), channel_id=1, source_target_pairs={{0,4},{4,0},{8,12},{12,8},{16,20},{20,16},{24,28},{28,24},{32,36},... | collective-permute-start | bytes 98312 | tf_op jit(solution)/shard_map/ppermute | solution.py:741

commit v7 on v6

--- a/solution.py
+++ b/solution.py
@@ -549,7 +549,7 @@
 def unpack_kernel(
     grads_ref, win_hbm, bin_hbm, woutt_hbm, bout_hbm, win_ref, bin_ref, woutt_ref, bout_ref, sems
 ):
-    g = grads_ref[...]
+    g = jnp.sum(grads_ref[...], axis=0)
     copies = []
 
     def send(ref, hbm):
@@ -706,10 +706,14 @@
     )(done, r, r_a, r_b, x1, h1, x2, h2, m2, lint, loutt)
 
 
-def gather_sum(x, axes):
+def gather_copies(x, axes):
     peers = lax.axis_size(axes)
     copies = jnp.broadcast_to(x[None], (peers,) + x.shape)
-    return jnp.sum(lax.all_to_all(copies, axes, 0, 0, tiled=True), axis=0)
+    return lax.all_to_all(copies, axes, 0, 0, tiled=True)
+
+
+def gather_sum(x, axes):
+    return jnp.sum(gather_copies(x, axes), axis=0)
 
 
 def body(populations, target_density, weight_in, bias_in, weight_out, bias_out):
@@ -742,7 +746,7 @@
     r_b = lax.ppermute(r, gx, cross)
     grads = third(done, r, r_a, r_b, x1, h1, x2, h2, m2, lint, loutt)
     grads = gather_sum(grads, ("x", "yh", "yl", "c"))
-    grads = gather_sum(grads, ("zh", "zl"))
+    grads = gather_copies(grads, ("zh", "zl"))
     return (moments, *unpack(grads))
 
 

time: 96.4 us -> 96.1 us (level)
  no operation moved by 1% of the time
where the time goes in v7:
time: 96.1 us; the launch traced here: 94.9 us
  starting transfers between devices  36.5 us (38%)
  blocking collectives  32.8 us (34%)
  Pallas kernels  12.5 us (13%)
  waiting for transfers between devices  10.3 us (11%)
  local copies, waits for them, and re-layouts  1.11 us (1%)
    all_to_all x2, blocking collectives, gather_copies(): return lax.all_to_all(copies, axes, 0, 0, tiled=True)  32.8 us
    ppermute x1, starting transfers between devices, body(): got_b = lax.ppermute(msg_b, gx, cross)  11.8 us
    ppermute x1, starting transfers between devices, body(): r_b = lax.ppermute(r, gx, cross)  10.2 us
    ppermute x1, starting transfers between devices, body(): got_near = lax.ppermute(near, gy, [(j, j ^ 1) for j in range(ny)])  6.11 us
    pallas_call x1, Pallas kernels, third(): pl.pallas_call(third_kernel, out_shape=shape(16, 128), in_specs=[VMEM] *...  4.82 us
    ppermute x1, starting transfers between devices, body(): lax.ppermute(far, gy, [(j, (j + 1) % ny if j % 2 else (j - 1) % ny) for j...  4.59 us
    ppermute x1, waiting for transfers between devices, body(): got_b = lax.ppermute(msg_b, gx, cross)  4.37 us
    ppermute x1, waiting for transfers between devices, body(): r_a = lax.ppermute(r, gx, pair)  3.37 us
  transfers between devices with their start and end apart: 6, of which 3 were waited for; matrix products, arithmetic and copies ran while one was open for 1% of the time, Pallas kernels for 3%

profile of v7, /device:TPU:1, one launch (start us, length us, event | category | flops | bytes accessed | tf_op | source)
XLA Modules:
  0.0 94.9 jit_solution(5490020741695601252)
XLA Ops:
  0.6 0.0 copy-start
  0.6 1.1 %copy-done = f32[19,2,16,256]{3,2,1,0:T(8,128)S(1)} copy-done((f32[19,2,16,256]{3,2,1,0:T(8,128)S(1)}, f32[19,2,16,256]{3,2,1,0:T(8,128)}, u32[]{:S(2)}) %copy-start) | copy-done | bytes 622616
  1.7 0.0 copy-start.1
  1.7 0.2 edges.1
  2.0 4.6 %collective-permute-start = (f32[19,4,256]{2,1,0:T(4,128)S(1)}, f32[19,4,256]{2,1,0:T(4,128)S(1)}, u32[]{:S(2)}, u32[]{:S(2)}) collective-permute-start(f32[19,4,256]{2,1,0:T(4,128)S(1)} %get-tuple-element.32), channel_id=1, source_target_pairs={{0,3},{1,2},{2,1},{3,0},{4,7},{5,6},{6,5},{7,4},{8,11},{9,10},{10,... | collective-permute-start | bytes 233480 | tf_op jit(solution)/shard_map/ppermute | solution.py:734
  6.6 6.1 %collective-permute-start.1 = (f32[19,4,256]{2,1,0:T(4,128)S(1)}, f32[19,4,256]{2,1,0:T(4,128)S(1)}, u32[]{:S(2)}, u32[]{:S(2)}) collective-permute-start(f32[19,4,256]{2,1,0:T(4,128)S(1)} %get-tuple-element.33), channel_id=1, source_target_pairs={{0,1},{1,0},{2,3},{3,2},{4,5},{5,4},{6,7},{7,6},{8,9},{9,8},{10,11... | collective-permute-start | bytes 233480 | tf_op jit(solution)/shard_map/ppermute | solution.py:733
  12.7 0.8 select_maximum_fusion.packed_ref
  13.5 0.8 prep.1
  14.3 0.0 collective-permute-done.far_ref
  14.3 0.0 collective-permute-done.1.near_ref
  14.3 1.3 %first.1 = (f32[344,256]{1,0:T(8,128)S(1)}, f32[344,256]{1,0:T(8,128)S(1)}, f32[19,40,256]{2,1,0:T(8,128)S(1)}, bf16[5,320,256]{2,1,0:T(8,128)(2,1)S(1)}, bf16[5,512,256]{2,1,0:T(8,128)(2,1)S(1)}) custom-call(f32[160,256]{1,0:T(8,128)S(1)} %get-tuple-element.30.bout_ref, f32[19,2,16,256]{3,2,1,0:T(8,128)S(1)} %get-tuple-element.31.pop_ref, ...), custom_call_target="tpu_custom_call" | custom-call | tf_op jit(solution)/shard_map/first/pallas_call | solution.py:645
  15.6 1.9 %collective-permute-start.2 = (f32[344,256]{1,0:T(8,128)S(1)}, f32[344,256]{1,0:T(8,128)S(1)}, u32[]{:S(2)}, u32[]{:S(2)}) collective-permute-start(f32[344,256]{1,0:T(8,128)S(1)} %get-tuple-element.37), channel_id=1, source_target_pairs={{0,4},{4,0},{8,12},{12,8},{16,20},{20,16},{24,28},{28,24},{32,36},... | collective-permute-start | bytes 1056776 | tf_op jit(solution)/shard_map/ppermute | solution.py:739
  17.5 11.8 %collective-permute-start.3 = (f32[344,256]{1,0:T(8,128)S(1)}, f32[344,256]{1,0:T(8,128)S(1)}, u32[]{:S(2)}, u32[]{:S(2)}) collective-permute-start(f32[344,256]{1,0:T(8,128)S(1)} %get-tuple-element.38), channel_id=1, source_target_pairs={{0,508},{4,8},{8,4},{12,16},{16,12},{20,24},{24,20},{28,32},{32,28... | collective-permute-start | bytes 1056776 | tf_op jit(solution)/shard_map/ppermute | solution.py:740
  29.3 0.0 copy-done.1
  29.3 0.9 middle.1
  30.2 2.6 %collective-permute-done.2.msg_a_ref = f32[344,256]{1,0:T(8,128)S(1)} collective-permute-done((f32[344,256]{1,0:T(8,128)S(1)}, f32[344,256]{1,0:T(8,128)S(1)}, u32[]{:S(2)}, u32[]{:S(2)}) %collective-permute-start.2) | collective-permute-done | bytes 352288 | tf_op jit(solution)/shard_map/ppermute | solution.py:739
  32.8 4.4 %collective-permute-done.3.msg_b_ref = f32[344,256]{1,0:T(8,128)S(1)} collective-permute-done((f32[344,256]{1,0:T(8,128)S(1)}, f32[344,256]{1,0:T(8,128)S(1)}, u32[]{:S(2)}, u32[]{:S(2)}) %collective-permute-start.3) | collective-permute-done | bytes 352288 | tf_op jit(solution)/shard_map/ppermute | solution.py:740
  37.1 2.0 %second.1 = (f32[32,256]{1,0:T(8,128)S(1)}, f32[19,72,256]{2,1,0:T(8,128)S(1)}, bf16[5,320,256]{2,1,0:T(8,128)(2,1)S(1)}, bf16[9,512,256]{2,1,0:T(8,128)(2,1)S(1)}, f32[9,3,8,256]{3,2,1,0:T(8,128)S(1)}) custom-call(f32[160,256]{1,0:T(8,128)S(1)} %get-tuple-element.30.bout_ref, f32[19,40,256]{2,1,0:T(8,128)S(1)} %get-tuple-element.36.after_first.c1_ref, ...), custom_call_target="tpu_custom_call" | custom-call | tf_op jit(solution)/shard_map/second/pallas_call | solution.py:663
  39.2 10.2 %collective-permute-start.5 = (f32[32,256]{1,0:T(8,128)S(1)}, f32[32,256]{1,0:T(8,128)S(1)}, u32[]{:S(2)}, u32[]{:S(2)}) collective-permute-start(f32[32,256]{1,0:T(8,128)S(1)} %get-tuple-element.43.r_ref), channel_id=1, source_target_pairs={{0,508},{4,8},{8,4},{12,16},{16,12},{20,24},{24,20},{28,32},{32,28... | collective-permute-start | bytes 98312 | tf_op jit(solution)/shard_map/ppermute | solution.py:746
  49.4 1.9 %collective-permute-start.4 = (f32[32,256]{1,0:T(8,128)S(1)}, f32[32,256]{1,0:T(8,128)S(1)}, u32[]{:S(2)}, u32[]{:S(2)}) collective-permute-start(f32[32,256]{1,0:T(8,128)S(1)} %get-tuple-element.43.r_ref), channel_id=1, source_target_pairs={{0,4},{4,0},{8,12},{12,8},{16,20},{20,16},{24,28},{28,24},{32,36},... | collective-permute-start | bytes 98312 | tf_op jit(solution)/shard_map/ppermute | solution.py:745
  51.3 0.9 moments.1
  52.2 0.0 collective-permute-done.5.r_b_ref
  52.2 3.4 %collective-permute-done.4.r_a_ref = f32[32,256]{1,0:T(8,128)S(1)} collective-permute-done((f32[32,256]{1,0:T(8,128)S(1)}, f32[32,256]{1,0:T(8,128)S(1)}, u32[]{:S(2)}, u32[]{:S(2)}) %collective-permute-start.4) | collective-permute-done | bytes 32800 | tf_op jit(solution)/shard_map/ppermute | solution.py:745
  55.5 4.8 %third.1 = f32[16,128]{1,0:T(8,128)S(1)} custom-call(f32[8,128]{1,0:T(8,128)S(1)} %get-tuple-element.42._after_moments, f32[32,256]{1,0:T(8,128)S(1)} %get-tuple-element.43.r_ref, f32[32,256]{1,0:T(8,128)S(1)} %collective-permute-done.4.r_a_ref, f32[32,256]{1,0:T(8,128)S(1)} %collective-permute-done.5.r_b_ref, ...), custom_call_target="tpu_custom_call" | custom-call | tf_op jit(solution)/shard_map/third/pallas_call | solution.py:692
  60.4 14.5 %all_to_all.10 = f32[32,16,128]{2,1,0:T(8,128)S(1)} all-to-all(f32[32,16,128]{2,1,0:T(8,128)S(1)} %broadcast_in_dim.4), channel_id=1, replica_groups=mesh['zh'=4,'zl'=4,'x'=4,'yh'=2,'yl'=2,'c'=2] {'x','yh','yl','c'}, dimensions={0} | all-to-all | bytes 524288 | tf_op jit(solution)/shard_map/all_to_all | solution.py:712
  74.9 18.3 %all_to_all.11.grads_ref = f32[16,16,128]{2,1,0:T(8,128)} all-to-all(f32[16,16,128]{2,1,0:T(8,128)S(1)} %broadcast_in_dim.5), channel_id=1, replica_groups=mesh['zh'=4,'zl'=4,'x'=4,'yh'=2,'yl'=2,'c'=2] {'zh','zl'}, dimensions={0} | all-to-all | bytes 262144 | tf_op jit(solution)/shard_map/all_to_all | solution.py:712
  93.2 1.6 %unpack.1 = (f32[19,32]{1,0:T(8,128)}, f32[1,32]{1,0:T(1,128)}, f32[19,32]{1,0:T(8,128)}, f32[1,19]{1,0:T(1,128)}) custom-call(f32[16,16,128]{2,1,0:T(8,128)} %all_to_all.11.grads_ref), custom_call_target="tpu_custom_call" | custom-call | tf_op jit(solution)/shard_map/unpack/pallas_call | solution.py:627
  (3 shorter events, 0.1 us)
Async XLA Ops:
  0.6 1.1 %copy-start = (f32[19,2,16,256]{3,2,1,0:T(8,128)S(1)}, f32[19,2,16,256]{3,2,1,0:T(8,128)}, u32[]{:S(2)}) copy-start(f32[19,2,16,256]{3,2,1,0:T(8,128)} %pop_hbm.1) | copy-start | bytes 1867780
  1.7 27.6 %copy-start.1 = (f32[2,16,256]{2,1,0:T(8,128)S(1)}, f32[2,16,256]{2,1,0:T(8,128)}, u32[]{:S(2)}) copy-start(f32[2,16,256]{2,1,0:T(8,128)} %target_in.1) | copy-start | bytes 98308
  2.0 12.3 %collective-permute-start = (f32[19,4,256]{2,1,0:T(4,128)S(1)}, f32[19,4,256]{2,1,0:T(4,128)S(1)}, u32[]{:S(2)}, u32[]{:S(2)}) collective-permute-start(f32[19,4,256]{2,1,0:T(4,128)S(1)} %get-tuple-element.32), channel_id=1, source_target_pairs={{0,3},{1,2},{2,1},{3,0},{4,7},{5,6},{6,5},{7,4},{8,11},{9,10},{10,... | collective-permute-start | bytes 233480 | tf_op jit(solution)/shard_map/ppermute | solution.py:734
  6.6 7.8 %collective-permute-start.1 = (f32[19,4,256]{2,1,0:T(4,128)S(1)}, f32[19,4,256]{2,1,0:T(4,128)S(1)}, u32[]{:S(2)}, u32[]{:S(2)}) collective-permute-start(f32[19,4,256]{2,1,0:T(4,128)S(1)} %get-tuple-element.33), channel_id=1, source_target_pairs={{0,1},{1,0},{2,3},{3,2},{4,5},{5,4},{6,7},{7,6},{8,9},{9,8},{10,11... | collective-permute-start | bytes 233480 | tf_op jit(solution)/shard_map/ppermute | solution.py:733
  15.6 17.2 %collective-permute-start.2 = (f32[344,256]{1,0:T(8,128)S(1)}, f32[344,256]{1,0:T(8,128)S(1)}, u32[]{:S(2)}, u32[]{:S(2)}) collective-permute-start(f32[344,256]{1,0:T(8,128)S(1)} %get-tuple-element.37), channel_id=1, source_target_pairs={{0,4},{4,0},{8,12},{12,8},{16,20},{20,16},{24,28},{28,24},{32,36},... | collective-permute-start | bytes 1056776 | tf_op jit(solution)/shard_map/ppermute | solution.py:739
  17.5 19.6 %collective-permute-start.3 = (f32[344,256]{1,0:T(8,128)S(1)}, f32[344,256]{1,0:T(8,128)S(1)}, u32[]{:S(2)}, u32[]{:S(2)}) collective-permute-start(f32[344,256]{1,0:T(8,128)S(1)} %get-tuple-element.38), channel_id=1, source_target_pairs={{0,508},{4,8},{8,4},{12,16},{16,12},{20,24},{24,20},{28,32},{32,28... | collective-permute-start | bytes 1056776 | tf_op jit(solution)/shard_map/ppermute | solution.py:740
  39.2 13.0 %collective-permute-start.5 = (f32[32,256]{1,0:T(8,128)S(1)}, f32[32,256]{1,0:T(8,128)S(1)}, u32[]{:S(2)}, u32[]{:S(2)}) collective-permute-start(f32[32,256]{1,0:T(8,128)S(1)} %get-tuple-element.43.r_ref), channel_id=1, source_target_pairs={{0,508},{4,8},{8,4},{12,16},{16,12},{20,24},{24,20},{28,32},{32,28... | collective-permute-start | bytes 98312 | tf_op jit(solution)/shard_map/ppermute | solution.py:746
  49.4 6.2 %collective-permute-start.4 = (f32[32,256]{1,0:T(8,128)S(1)}, f32[32,256]{1,0:T(8,128)S(1)}, u32[]{:S(2)}, u32[]{:S(2)}) collective-permute-start(f32[32,256]{1,0:T(8,128)S(1)} %get-tuple-element.43.r_ref), channel_id=1, source_target_pairs={{0,4},{4,0},{8,12},{12,8},{16,20},{20,16},{24,28},{28,24},{32,36},... | collective-permute-start | bytes 98312 | tf_op jit(solution)/shard_map/ppermute | solution.py:745
